TPU v7x, 32 devices: a whole 2x2x4 slice. The times are simulated.
32 devices in a mesh: frame: 4 (over y, x), row: 2 (over core), chan: 4 (over z).
Axes of the slice: x: 2, y: 2, z: 4, core: 2. Of those that a mesh axis runs over, the one named last changes fastest.
Arguments:
- activations: bfloat16 [320, 12, 2, 128], P('chan', 'frame', 'row'), may hold values from -12 to 12, as said below
- conv_first: bfloat16 [27, 320, 320], P(None, 'chan'), may hold values from -0.0625 to 0.0625
- conv_second: bfloat16 [27, 320, 320], P(None, 'chan'), may hold values from -0.0625 to 0.0625
- cotangent: bfloat16 [320, 12, 2, 128], P('chan', 'frame', 'row'), may hold values from -6 to 6
Outputs:
- result: bfloat16 [320, 12, 2, 128], P('chan', 'frame', 'row')
- input_grad: bfloat16 [320, 12, 2, 128], P('chan', 'frame', 'row')
- first_grad: float32 [27, 320, 320], P(None, 'chan')
- second_grad: float32 [27, 320, 320], P(None, 'chan')
Inputs may be any that keep to these rules, and one draw needn't show every extreme that they name: activations of the window.
All inputs are finite; a program needn't handle non-finite values.
Results may differ from a plain program's by a relative error of at most 0.0054.
Values may be sent and summed in bfloat16 or wider, within the bound.
No kernel may reach another device: no remote copies, remote signals or barrier semaphores. Data moves between devices by JAX's collectives and lax.ppermute only.
A program may use at most 128 MiB of HBM per device.

v0:
```python
import jax
import jax.numpy as jnp
from jax import lax
from jax.sharding import PartitionSpec as P

C = 320
GROUPS = 32


EPSILON = 1e-05


def with_halo(cells, sides, width):
    for axis, dim in sides:
        count = lax.axis_size(axis)
        ends = count - 1
        head = lax.slice_in_dim(cells, 0, width, axis=dim)
        tail = lax.slice_in_dim(cells, cells.shape[dim] - width, cells.shape[dim], axis=dim)
        cells = jnp.concatenate(
            [
                lax.ppermute(tail, axis, [(i, (i + 1) % count) for i in range(ends)]),
                cells,
                lax.ppermute(head, axis, [((i + 1) % count, i) for i in range(ends)]),
            ],
            axis=dim,
        )
    return cells


def pad_columns(values):
    return jnp.pad(values, ((0, 0), (0, 0), (0, 0), (1, 1)))


def with_rims(values):
    return with_halo(values, (("frame", 1), ("row", 2)), 1)


def collect(padded, frames, height, breadth, mirrored):
    windows = []
    for tap_frame in range(3):
        for tap_row in range(3):
            for tap_col in range(3):
                if mirrored:
                    anchor = (2 - tap_frame, 2 - tap_row, 2 - tap_col)
                else:
                    anchor = (tap_frame, tap_row, tap_col)
                window = padded[
                    :,
                    anchor[0] : anchor[0] + frames,
                    anchor[1] : anchor[1] + height,
                    anchor[2] : anchor[2] + breadth,
                ]
                windows.append(window.reshape(padded.shape[0], -1))
    return jnp.stack(windows)


def forward_conv(values, weight):
    channels_local, frames, height, breadth = values.shape
    positions = frames * height * breadth
    rimmed = with_rims(values)
    own_patches = collect(pad_columns(rimmed), frames, height, breadth, False)
    flat_own = own_patches.reshape(-1, positions)
    flat_weight = weight.reshape(-1, weight.shape[2])
    summed = lax.psum_scatter(
        lax.dot_general(
            flat_weight, flat_own, (((0,), (0,)), ((), ())), preferred_element_type=jnp.float32
        ),
        "chan",
        scatter_dimension=0,
        tiled=True,
    )
    return (summed, own_patches)


def normalize(summed):
    grouped = summed.reshape(summed.shape[0] // (C // GROUPS), -1)
    members = grouped.shape[1] * lax.axis_size("frame") * lax.axis_size("row")
    totals = lax.psum(jnp.sum(grouped, axis=1), ("frame", "row"))
    average = totals / members
    centered = grouped - average[:, None]
    variance = lax.psum(jnp.sum(centered * centered, axis=1), ("frame", "row")) / members
    inv_scale = lax.rsqrt(variance + EPSILON)
    return ((centered * inv_scale[:, None]).reshape(summed.shape), inv_scale)


def norm_back(grad_norm, normed, inv_scale):
    grouped_grad = grad_norm.reshape(inv_scale.shape[0], -1)
    grouped_norm = normed.reshape(inv_scale.shape[0], -1)
    members = grouped_grad.shape[1] * lax.axis_size("frame") * lax.axis_size("row")
    first_sum, second_sum = lax.psum(
        (jnp.sum(grouped_grad, axis=1), jnp.sum(grouped_grad * grouped_norm, axis=1)),
        ("frame", "row"),
    )
    adjusted = (
        grouped_grad
        - (first_sum / members)[:, None]
        - grouped_norm * (second_sum / members)[:, None]
    )
    return (adjusted * inv_scale[:, None]).reshape(grad_norm.shape)


def back_conv(grads, own_patches, weight):
    channels_local, frames, height, breadth = grads.shape
    positions = frames * height * breadth
    flat_own = own_patches.reshape(-1, positions)
    rimmed = with_rims(grads)
    portion = lax.all_gather(rimmed, "chan", axis=0, tiled=True)
    members = portion.shape[0]
    interior = portion[:, 1:-1, 1:-1, :].reshape(members, -1)
    shifted = collect(pad_columns(portion), frames, height, breadth, True)
    merged_w = jnp.transpose(weight, (1, 0, 2)).reshape(channels_local, -1)
    back_sum = jnp.dot(merged_w, shifted.reshape(-1, positions), preferred_element_type=jnp.float32)
    increment = lax.dot_general(
        flat_own, interior, (((1,), (1,)), ((), ())), preferred_element_type=jnp.float32
    )
    increment = increment.reshape(27, channels_local, members)
    return (back_sum, increment)


def reduce_weights(weight_grad):
    return lax.psum(weight_grad, ("frame", "row"))


def shards(activations, conv_first, conv_second, cotangent):
    layout = activations.shape
    channels_local = layout[0]
    first_sum, first_patches = forward_conv(activations, conv_first)
    first_norm, first_scale = normalize(first_sum)
    first_gate = jax.nn.sigmoid(first_norm)
    hidden = (first_norm * first_gate).astype(jnp.bfloat16).reshape(layout)
    second_sum, second_patches = forward_conv(hidden, conv_second)
    second_norm, second_scale = normalize(second_sum)
    second_gate = jax.nn.sigmoid(second_norm)
    result = (
        (activations.astype(jnp.float32).reshape(channels_local, -1) + second_norm * second_gate)
        .astype(jnp.bfloat16)
        .reshape(layout)
    )
    flat_cot = cotangent.astype(jnp.float32).reshape(channels_local, -1)
    second_dnorm = flat_cot * second_gate * (1.0 + second_norm * (1.0 - second_gate))
    grad_second = (
        norm_back(second_dnorm, second_norm, second_scale).astype(jnp.bfloat16).reshape(layout)
    )
    hidden_grad, second_weight = back_conv(grad_second, second_patches, conv_second)
    second_total = reduce_weights(second_weight)
    first_dnorm = hidden_grad * first_gate * (1.0 + first_norm * (1.0 - first_gate))
    grad_first = (
        norm_back(first_dnorm, first_norm, first_scale).astype(jnp.bfloat16).reshape(layout)
    )
    conv_back, first_weight = back_conv(grad_first, first_patches, conv_first)
    first_total = reduce_weights(first_weight)
    input_grad = (flat_cot + conv_back).astype(jnp.bfloat16).reshape(layout)
    return (result, input_grad, first_total, second_total)


def solution(mesh):
    return jax.shard_map(
        shards,
        mesh=mesh,
        in_specs=(
            P("chan", "frame", "row", None),
            P(None, "chan", None),
            P(None, "chan", None),
            P("chan", "frame", "row", None),
        ),
        out_specs=(
            P("chan", "frame", "row", None),
            P("chan", "frame", "row", None),
            P(None, "chan", None),
            P(None, "chan", None),
        ),
        check_vma=False,
    )
```

profile of v0, /device:TPU:0, one launch (start us, length us, event | category | flops | bytes accessed | tf_op | source)
XLA Modules:
  0.0 780.9 jit_solution(3901120717366569403)
XLA Ops:
  8.1 4.8 collective-permute-start
  14.4 4.2 collective-permute-done.1
  20.9 3.0 collective-permute-start.2
  75.2 3.2 convolution_bitcast_fusion.1
  78.4 22.6 %reduce-scatter.3.cloned.1.call-done = f32[80,384]{1,0:T(8,128)} async-done(((f32[320,384]{1,0:T(8,128)}), f32[80,384]{1,0:T(8,128)}) %reduce-scatter.3.cloned.1.call-update) | async-done | bytes 122896 | tf_op jit(solution)/shard_map/reduce_scatter | solution.py:64
  102.3 12.2 %psum.70 = f32[8]{0:T(128)S(1)} all-reduce(f32[8]{0:T(128)S(1)} %reduce_sum.97), channel_id=1, replica_groups=mesh['frame'=4,'row'=2,'chan'=4] {'frame','row'}, use_global_device_ids=true, to_apply=%region_3.4 | all-reduce | flops 8 | bytes 64 | tf_op jit(solution)/shard_map/psum | solution.py:78
  115.9 11.8 %psum.71 = f32[8]{0:T(128)S(1)} all-reduce(f32[8]{0:T(128)S(1)} %reduce_sum.100), channel_id=1, replica_groups=mesh['frame'=4,'row'=2,'chan'=4] {'frame','row'}, use_global_device_ids=true, to_apply=%region_6.7 | all-reduce | flops 8 | bytes 64 | tf_op jit(solution)/shard_map/psum | solution.py:81
  130.3 4.5 collective-permute-start.4
  138.6 4.4 collective-permute-start.6
  219.8 3.2 convolution_bitcast_fusion
  223.3 20.1 %reduce-scatter.5.cloned.1.call-done = f32[80,384]{1,0:T(8,128)} async-done(((f32[320,384]{1,0:T(8,128)}), f32[80,384]{1,0:T(8,128)}) %reduce-scatter.5.cloned.1.call-update) | async-done | bytes 122896 | tf_op jit(solution)/shard_map/reduce_scatter | solution.py:64
  244.6 12.1 %psum.72 = f32[8]{0:T(128)S(1)} all-reduce(f32[8]{0:T(128)S(1)} %reduce_sum.106), channel_id=1, replica_groups=mesh['frame'=4,'row'=2,'chan'=4] {'frame','row'}, use_global_device_ids=true, to_apply=%region_10.11 | all-reduce | flops 8 | bytes 64 | tf_op jit(solution)/shard_map/psum | solution.py:78
  259.7 11.8 %psum.73 = f32[8]{0:T(128)S(1)} all-reduce(f32[8]{0:T(128)S(1)} %reduce_sum.112), channel_id=1, replica_groups=mesh['frame'=4,'row'=2,'chan'=4] {'frame','row'}, use_global_device_ids=true, to_apply=%region_13.14 | all-reduce | flops 8 | bytes 64 | tf_op jit(solution)/shard_map/psum | solution.py:81
  274.6 11.8 %all-reduce.5 = (f32[8]{0:T(128)S(1)}, f32[8]{0:T(128)S(1)}) all-reduce(f32[8]{0:T(128)S(1)} %reduce_sum.145, f32[8]{0:T(128)S(1)} %reduce_sum.115), channel_id=1, replica_groups=mesh['frame'=4,'row'=2,'chan'=4] {'frame','row'}, use_global_device_ids=true, to_apply=%region_19.20 | all-reduce | flops 16 | bytes 128 | tf_op jit(solution)/shard_map/psum | solution.py:90
  290.7 4.5 collective-permute-start.8
  298.4 3.0 collective-permute-start.10
  303.5 42.6 %all-gather.3.cloned.1.call-done = bf16[320,5,3,128]{3,1,0,2:T(8,128)(2,1)} async-done(((bf16[80,5,3,128]{3,1,0,2:T(8,128)(2,1)}), bf16[320,5,3,128]{3,1,0,2:T(8,128)(2,1)}) %all-gather.3.cloned.1.call-update) | async-done | bytes 1228816 | tf_op jit(solution)/shard_map/all_gather | solution.py:107
  346.1 5.4 fusion.40
  360.5 12.4 %pad_slice_fusion.18 = (bf16[320,3,1,128]{3,1,0,2:T(4,128)(2,1)}, bf16[320,3,1,128]{3,1,0,2:T(4,128)(2,1)}, bf16[320,3,1,128]{3,1,0,2:T(4,128)(2,1)}, bf16[320,3...) fusion(bf16[320,5,3,128]{3,1,0,2:T(8,128)(2,1)} %all-gather.3.c, ...), kind=kLoop, calls=%fused_computation.18 | loop fusion | bytes 7290880 | tf_op jit(solution)/shard_map/slice | solution.py:47
  384.1 1.9 copy.73
  387.7 1.9 copy.74
  395.2 1.9 copy.76
  398.8 1.9 copy.77
  402.5 1.9 copy.78
  406.2 1.9 copy.79
  410.0 1.9 copy.80
  413.7 1.9 copy.81
  428.5 1.9 copy.85
  432.3 1.9 copy.86
  436.0 1.9 copy.87
  488.8 4.8 fusion.36
  494.0 13.6 %all-reduce.4 = (f32[8]{0:T(128)S(1)}, f32[8]{0:T(128)S(1)}) all-reduce(f32[8]{0:T(128)S(1)} %reduce_sum.151, f32[8]{0:T(128)S(1)} %reduce_sum.148), channel_id=1, replica_groups=mesh['frame'=4,'row'=2,'chan'=4] {'frame','row'}, use_global_device_ids=true, to_apply=%region_25.26 | all-reduce | flops 16 | bytes 128 | tf_op jit(solution)/shard_map/psum | solution.py:90
  510.3 4.5 collective-permute-start.12
  518.0 3.0 collective-permute-start.14
  523.1 12.1 %all-reduce.9.cloned.1.call-start = ((), (), s32[]{:S(2)}) async-start(), calls=%async_computation.6 | async-start | bytes 13271040 | tf_op jit(solution)/shard_map/psum | solution.py:121
  535.8 4.5 fusion.52
  540.3 25.4 %all-gather.5.cloned.1.call-done = bf16[320,5,3,128]{3,1,0,2:T(8,128)(2,1)} async-done(((bf16[80,5,3,128]{3,1,0,2:T(8,128)(2,1)}), bf16[320,5,3,128]{3,1,0,2:T(8,128)(2,1)}) %all-gather.5.cloned.1.call-update) | async-done | bytes 1228816 | tf_op jit(solution)/shard_map/all_gather | solution.py:107
  565.7 5.4 fusion.39
  573.4 12.2 %pad_slice_fusion = (bf16[320,3,1,128]{3,1,0,2:T(4,128)(2,1)S(1)}, bf16[320,3,1,128]{3,1,0,2:T(4,128)(2,1)}, bf16[320,3,1,128]{3,1,0,2:T(4,128)(2,1)}, bf16[320,...) fusion(bf16[320,5,3,128]{3,1,0,2:T(8,128)(2,1)} %all-gather.5.c, ...), kind=kLoop, calls=%fused_computation | loop fusion | bytes 7290880 | tf_op jit(solution)/shard_map/slice | solution.py:47
  610.8 1.9 copy.136
  614.5 1.9 copy.137
  621.9 1.9 copy.139
  625.6 1.9 copy.140
  629.3 1.9 copy.141
  650.3 4.5 fusion.51
  675.8 4.2 fusion.21
  680.7 87.7 %all-reduce.9.cloned.1.call-done = (f32[27,80,320]{2,1,0:T(8,128)}, f32[27,80,320]{2,1,0:T(8,128)}) async-done(((f32[27,80,320]{2,1,0:T(8,128)}, f32[27,80,320]{2,1,0:T(8,128)}), (f32[27,80,320]{2,1,0:T(8,128)}, f32[27,80,320]{2,1,0:T(8,128)})) %all-reduce.9.cloned.1.call-update) | async-done | bytes 5529616 | tf_op jit(solution)/shard_map/psum | solution.py:121
  768.4 4.0 copy.300
  (540 shorter events, 351.9 us)
Async XLA Ops:
  7.2 212.6 %copy-start = (bf16[27,80,320]{2,1,0:T(8,128)(2,1)S(1)}, bf16[27,80,320]{2,1,0:T(8,128)(2,1)}, u32[]{:S(2)}) copy-start(bf16[27,80,320]{2,1,0:T(8,128)(2,1)} %param.6) | copy-start | bytes 4147204
  7.2 93.9 %reduce-scatter.3.cloned.1.call-start = ((), (), s32[]{:S(2)}) async-start(), calls=%async_computation.2 | async-start | bytes 614400 | tf_op jit(solution)/shard_map/reduce_scatter | solution.py:64
  8.1 6.3 collective-permute-start
  12.9 5.7 collective-permute-start.1
  19.6 6.1 collective-permute-start.3
  20.9 4.8 collective-permute-start.2
  42.5 32.7 %copy-start.2 = (bf16[27,80,320]{2,1,0:T(8,128)(2,1)S(1)}, bf16[27,80,320]{2,1,0:T(8,128)(2,1)}, u32[]{:S(2)}) copy-start(bf16[27,80,320]{2,1,0:T(8,128)(2,1)} %param.5) | copy-start | bytes 4147204
  46.3 22.6 %copy-start.57 = (bf16[1,80,384]{2,1,0:T(8,128)(2,1)S(1)}, bf16[1,80,384]{2,1,0:T(8,128)(2,1)}, u32[]{:S(2)}) copy-start(bf16[1,80,384]{2,1,0:T(8,128)(2,1)} %stack_reshape.341) | copy-start | bytes 184324
  46.3 23.2 %copy-start.58 = (bf16[1,80,384]{2,1,0:T(8,128)(2,1)S(1)}, bf16[1,80,384]{2,1,0:T(8,128)(2,1)}, u32[]{:S(2)}) copy-start(bf16[1,80,384]{2,1,0:T(8,128)(2,1)} %stack_reshape.342) | copy-start | bytes 184324
  46.3 23.9 %copy-start.59 = (bf16[1,80,384]{2,1,0:T(8,128)(2,1)S(1)}, bf16[1,80,384]{2,1,0:T(8,128)(2,1)}, u32[]{:S(2)}) copy-start(bf16[1,80,384]{2,1,0:T(8,128)(2,1)} %stack_reshape.343) | copy-start | bytes 184324
  46.3 24.5 %copy-start.61 = (bf16[1,80,384]{2,1,0:T(8,128)(2,1)S(1)}, bf16[1,80,384]{2,1,0:T(8,128)(2,1)}, u32[]{:S(2)}) copy-start(bf16[1,80,384]{2,1,0:T(8,128)(2,1)} %stack_reshape.344) | copy-start | bytes 184324
  46.3 25.1 %copy-start.63 = (bf16[1,80,384]{2,1,0:T(8,128)(2,1)S(1)}, bf16[1,80,384]{2,1,0:T(8,128)(2,1)}, u32[]{:S(2)}) copy-start(bf16[1,80,384]{2,1,0:T(8,128)(2,1)} %stack_reshape.345) | copy-start | bytes 184324
  46.3 26.3 %copy-start.60 = (bf16[1,80,384]{2,1,0:T(8,128)(2,1)S(1)}, bf16[1,80,384]{2,1,0:T(8,128)(2,1)}, u32[]{:S(2)}) copy-start(bf16[1,80,384]{2,1,0:T(8,128)(2,1)} %stack_reshape.347) | copy-start | bytes 184324
  46.3 27.0 %copy-start.62 = (bf16[1,80,384]{2,1,0:T(8,128)(2,1)S(1)}, bf16[1,80,384]{2,1,0:T(8,128)(2,1)}, u32[]{:S(2)}) copy-start(bf16[1,80,384]{2,1,0:T(8,128)(2,1)} %stack_reshape.348) | copy-start | bytes 184324
  46.3 27.6 %copy-start.64 = (bf16[1,80,384]{2,1,0:T(8,128)(2,1)S(1)}, bf16[1,80,384]{2,1,0:T(8,128)(2,1)}, u32[]{:S(2)}) copy-start(bf16[1,80,384]{2,1,0:T(8,128)(2,1)} %stack_reshape.349) | copy-start | bytes 184324
  46.3 28.2 %copy-start.65 = (bf16[1,80,384]{2,1,0:T(8,128)(2,1)S(1)}, bf16[1,80,384]{2,1,0:T(8,128)(2,1)}, u32[]{:S(2)}) copy-start(bf16[1,80,384]{2,1,0:T(8,128)(2,1)} %stack_reshape.350) | copy-start | bytes 184324
  78.4 165.0 %reduce-scatter.5.cloned.1.call-start = ((), (), s32[]{:S(2)}) async-start(), calls=%async_computation.3 | async-start | bytes 614400 | tf_op jit(solution)/shard_map/reduce_scatter | solution.py:64
  129.0 5.9 collective-permute-start.5
  130.3 6.2 collective-permute-start.4
  137.3 9.6 %collective-permute-start.7 = (bf16[80,5,1,128]{3,1,0,2:T(8,128)(2,1)}, bf16[80,5,1,128]{3,1,0,2:T(8,128)(2,1)}, u32[]{:S(2)}, u32[]{:S(2)}) collective-permute-start(bf16[80,5,1,128]{3,1,0,2:T(8,128)(2,1)} %pad_maximum_fusion.2), channel_id=1, source_target_pairs={{4,0},{5,1},{6,2},{7,3},{12,8},{13,9},{14,10},{15,11},{20,16},{21,... | collective-permute-start | bytes 307208 | tf_op jit(solution)/shard_map/ppermute | solution.py:23
  138.6 8.3 %collective-permute-start.6 = (bf16[80,5,1,128]{3,1,0,2:T(8,128)(2,1)}, bf16[80,5,1,128]{3,1,0,2:T(8,128)(2,1)}, u32[]{:S(2)}, u32[]{:S(2)}) collective-permute-start(bf16[80,5,1,128]{3,1,0,2:T(8,128)(2,1)} %pad_maximum_fusion.2), channel_id=1, source_target_pairs={{0,4},{1,5},{2,6},{3,7},{8,12},{9,13},{10,14},{11,15},{16,20},{17,... | collective-permute-start | bytes 307208 | tf_op jit(solution)/shard_map/ppermute | solution.py:21
  164.8 43.5 %copy-start.3 = (f32[80,384]{1,0:T(8,128)S(1)}, f32[80,384]{1,0:T(8,128)}, u32[]{:S(2)}) copy-start(f32[80,384]{1,0:T(8,128)} %reduce-scatter.3.cloned.1.call-done) | copy-start | bytes 368644
  190.6 22.8 %copy-start.74 = (bf16[1,80,384]{2,1,0:T(8,128)(2,1)S(1)}, bf16[1,80,384]{2,1,0:T(8,128)(2,1)}, u32[]{:S(2)}) copy-start(bf16[1,80,384]{2,1,0:T(8,128)(2,1)} %stack_reshape.368) | copy-start | bytes 184324
  190.6 23.5 %copy-start.72 = (bf16[1,80,384]{2,1,0:T(8,128)(2,1)S(1)}, bf16[1,80,384]{2,1,0:T(8,128)(2,1)}, u32[]{:S(2)}) copy-start(bf16[1,80,384]{2,1,0:T(8,128)(2,1)} %stack_reshape.369) | copy-start | bytes 184324
  190.6 24.1 %copy-start.73 = (bf16[1,80,384]{2,1,0:T(8,128)(2,1)S(1)}, bf16[1,80,384]{2,1,0:T(8,128)(2,1)}, u32[]{:S(2)}) copy-start(bf16[1,80,384]{2,1,0:T(8,128)(2,1)} %stack_reshape.370) | copy-start | bytes 184324
  190.6 24.7 %copy-start.71 = (bf16[1,80,384]{2,1,0:T(8,128)(2,1)S(1)}, bf16[1,80,384]{2,1,0:T(8,128)(2,1)}, u32[]{:S(2)}) copy-start(bf16[1,80,384]{2,1,0:T(8,128)(2,1)} %stack_reshape.371) | copy-start | bytes 184324
  190.6 25.3 %copy-start.70 = (bf16[1,80,384]{2,1,0:T(8,128)(2,1)S(1)}, bf16[1,80,384]{2,1,0:T(8,128)(2,1)}, u32[]{:S(2)}) copy-start(bf16[1,80,384]{2,1,0:T(8,128)(2,1)} %stack_reshape.372) | copy-start | bytes 184324
  190.6 26.0 %copy-start.56 = (bf16[1,80,384]{2,1,0:T(8,128)(2,1)S(1)}, bf16[1,80,384]{2,1,0:T(8,128)(2,1)}, u32[]{:S(2)}) copy-start(bf16[1,80,384]{2,1,0:T(8,128)(2,1)} %stack_reshape.373) | copy-start | bytes 184324
  190.6 26.6 %copy-start.69 = (bf16[1,80,384]{2,1,0:T(8,128)(2,1)S(1)}, bf16[1,80,384]{2,1,0:T(8,128)(2,1)}, u32[]{:S(2)}) copy-start(bf16[1,80,384]{2,1,0:T(8,128)(2,1)} %stack_reshape.374) | copy-start | bytes 184324
  190.6 27.2 %copy-start.66 = (bf16[1,80,384]{2,1,0:T(8,128)(2,1)S(1)}, bf16[1,80,384]{2,1,0:T(8,128)(2,1)}, u32[]{:S(2)}) copy-start(bf16[1,80,384]{2,1,0:T(8,128)(2,1)} %stack_reshape.375) | copy-start | bytes 184324
  190.7 27.8 %copy-start.67 = (bf16[1,80,384]{2,1,0:T(8,128)(2,1)S(1)}, bf16[1,80,384]{2,1,0:T(8,128)(2,1)}, u32[]{:S(2)}) copy-start(bf16[1,80,384]{2,1,0:T(8,128)(2,1)} %stack_reshape.376) | copy-start | bytes 184324
  190.7 28.5 %copy-start.68 = (bf16[1,80,384]{2,1,0:T(8,128)(2,1)S(1)}, bf16[1,80,384]{2,1,0:T(8,128)(2,1)}, u32[]{:S(2)}) copy-start(bf16[1,80,384]{2,1,0:T(8,128)(2,1)} %stack_reshape.377) | copy-start | bytes 184324
  219.8 54.2 %copy-start.54 = (bf16[80,3,1,128]{3,0,2,1:T(8,128)(2,1)S(1)}, bf16[80,3,1,128]{3,0,2,1:T(8,128)(2,1)}, u32[]{:S(2)}) copy-start(bf16[80,3,1,128]{3,0,2,1:T(8,128)(2,1)} %param.4) | copy-start | bytes 184324
  223.0 123.1 %all-gather.3.cloned.1.call-start = ((), (), s32[]{:S(2)}) async-start(), calls=%async_computation.4 | async-start | bytes 2457600 | tf_op jit(solution)/shard_map/all_gather | solution.py:107
  289.4 5.9 collective-permute-start.9
  290.7 6.2 collective-permute-start.8
  297.1 4.4 collective-permute-start.11
  298.4 4.1 collective-permute-start.10
  303.5 262.3 %all-gather.5.cloned.1.call-start = ((), (), s32[]{:S(2)}) async-start(), calls=%async_computation.5 | async-start | bytes 2457600 | tf_op jit(solution)/shard_map/all_gather | solution.py:107
  465.7 9.1 %copy-start.30 = (bf16[1,320,384]{2,1,0:T(8,128)(2,1)S(1)}, bf16[1,320,384]{2,1,0:T(8,128)(2,1)}, u32[]{:S(2)}) copy-start(bf16[1,320,384]{2,1,0:T(8,128)(2,1)} %copy.103) | copy-start | bytes 737284
  465.7 9.9 %copy-start.32 = (bf16[1,320,384]{2,1,0:T(8,128)(2,1)S(1)}, bf16[1,320,384]{2,1,0:T(8,128)(2,1)}, u32[]{:S(2)}) copy-start(bf16[1,320,384]{2,1,0:T(8,128)(2,1)} %copy.104) | copy-start | bytes 737284
  493.6 41.6 %copy-start.55 = (bf16[80,384]{1,0:T(8,128)(2,1)S(1)}, bf16[80,384]{1,0:T(8,128)(2,1)}, u32[]{:S(2)}) copy-start(bf16[80,384]{1,0:T(8,128)(2,1)} %get-tuple-element.120) | copy-start | bytes 184324
  493.6 42.2 %copy-start.5 = (bf16[320,3,1,128]{0,3,1,2:T(8,128)(2,1)S(1)}, bf16[320,3,1,128]{0,3,1,2:T(8,128)(2,1)}, u32[]{:S(2)}) copy-start(bf16[320,3,1,128]{0,3,1,2:T(8,128)(2,1)} %copy.81) | copy-start | bytes 737284
  509.0 5.9 collective-permute-start.13
  510.3 6.2 collective-permute-start.12
  516.7 4.4 collective-permute-start.15
  518.0 4.1 collective-permute-start.14
  523.1 245.3 %all-reduce.9.cloned.1.call-start = ((), (), s32[]{:S(2)}) async-start(), calls=%async_computation.6 | async-start | bytes 13271040 | tf_op jit(solution)/shard_map/psum | solution.py:121
  (48 other events, 262.6 us)
Sparse Core Ops, SparseCore 0:
  78.5 22.4 reduce-scatter.2
  223.1 20.2 reduce-scatter.4
  303.6 42.4 all-gather.2
  523.2 42.4 all-gather.4
  661.1 107.2 all-reduce.8
where the time goes:
time: 796 us; the launch traced here: 781 us
  local copies, waits for them, and re-layouts  385 us (48%)
  waiting for transfers between devices  210 us (26%)
  blocking collectives  73.3 us (9%)
  starting transfers between devices  54.8 us (7%)
  matrix products  24.4 us (3%)
  other arithmetic  18.7 us (2%)
  between operations  14.9 us (2%)
    another operation x111, local copies, waits for them, and re-layouts, collect(): return jnp.stack(windows)  139 us
    slice x90, local copies, waits for them, and re-layouts, collect(): padded[:, anchor[0]:anchor[0] + frames, anchor[1]:anchor[1] + height, anc...  130 us
    unnamed x259, local copies, waits for them, and re-layouts  111 us
    psum x1, waiting for transfers between devices, reduce_weights(): return lax.psum(weight_grad, ('frame', 'row'))  87.7 us
    all_gather x2, waiting for transfers between devices, back_conv(): portion = lax.all_gather(rimmed, 'chan', axis=0, tiled=True)  68 us
    reduce_scatter x2, waiting for transfers between devices, forward_conv(): lax.psum_scatter(lax.dot_general(flat_weight, flat_own, (((0,), (0,)), ((...  42.7 us
    ppermute x8, starting transfers between devices, with_halo(): lax.ppermute(tail, axis, [(i, (i + 1) % count) for i in range(ends)])  32 us
    psum x2, blocking collectives, norm_back(): lax.psum((jnp.sum(grouped_grad, axis=1), jnp.sum(grouped_grad * grouped_n...  25.4 us
  transfers between devices with their start and end apart: 21, of which 12 were waited for; matrix products, arithmetic and copies ran while one was open for 4% of the time, Pallas kernels for 0%

commit v1 on v0

--- a/solution.py
+++ b/solution.py
@@ -1,6 +1,10 @@
+import functools
+
 import jax
 import jax.numpy as jnp
 from jax import lax
+from jax.experimental import pallas as pl
+from jax.experimental.pallas import tpu as pltpu
 from jax.sharding import PartitionSpec as P
 
 C = 320
@@ -8,6 +12,7 @@
 
 
 EPSILON = 1e-05
+LINK = jnp.float32
 
 
 def with_halo(cells, sides, width):
@@ -121,7 +126,7 @@
     return lax.psum(weight_grad, ("frame", "row"))
 
 
-def shards(activations, conv_first, conv_second, cotangent):
+def shards_general(activations, conv_first, conv_second, cotangent):
     layout = activations.shape
     channels_local = layout[0]
     first_sum, first_patches = forward_conv(activations, conv_first)
@@ -153,9 +158,401 @@
     return (result, input_grad, first_total, second_total)
 
 
+BF16 = jnp.bfloat16
+F32 = jnp.float32
+LANES = 128
+HIGH = lax.Precision.HIGHEST
+FR = ("frame", "row")
+
+
+def call(kernel, outs, args, scratch=(), grid=None, specs=None, flops=0, reads=0):
+    vmem = pl.BlockSpec(memory_space=pltpu.VMEM)
+    in_specs = [pl.BlockSpec(memory_space=pltpu.SMEM)] + [vmem] * (len(args) - 1)
+    params = dict(vmem_limit_bytes=60 * 1024 * 1024)
+    if grid is not None:
+        params["dimension_semantics"] = ("arbitrary",) * len(grid)
+    extra = {} if grid is None else {"grid": grid}
+    return pl.pallas_call(
+        kernel,
+        out_shape=outs,
+        in_specs=in_specs,
+        out_specs=[vmem] * len(outs) if specs is None else specs,
+        scratch_shapes=list(scratch),
+        compiler_params=pltpu.CompilerParams(**params),
+        cost_estimate=pl.CostEstimate(flops=flops, bytes_accessed=reads, transcendentals=0),
+        **extra,
+    )(*args)
+
+
+def shift(block, step):
+    if step == 1:
+        return block
+    lane = lax.broadcasted_iota(jnp.int32, block.shape, 1)
+    if step == 0:
+        moved = pltpu.roll(block, 1, 1)
+        return jnp.where(lane == 0, jnp.zeros_like(moved), moved)
+    moved = pltpu.roll(block, block.shape[1] - 1, 1)
+    return jnp.where(lane == block.shape[1] - 1, jnp.zeros_like(moved), moved)
+
+
+def fill_patches(patches, block, channels, frames, mirrored, base=0, stride=None):
+    stride = channels if stride is None else stride
+    for place in range(frames + 2):
+        for row in range(2):
+            cells = block(place, row)
+            pick = 1 - row if mirrored else row
+            for tap_col in range(3):
+                moved = shift(cells, 2 - tap_col if mirrored else tap_col)
+                for tap_frame in range(3):
+                    frame = place - 2 + tap_frame if mirrored else place - tap_frame
+                    if 0 <= frame < frames:
+                        start = ((tap_frame * 2 + pick) * 3 + tap_col) * stride + base
+                        if not isinstance(start, int):
+                            start = pl.multiple_of(start, 16)
+                        patches[pl.ds(start, channels), pl.ds(frame * LANES, LANES)] = moved
+
+
+def frame_block(place, my_frame, frames, count):
+    if place == 0:
+        return jnp.maximum(my_frame - 1, 0), frames - 1, my_frame > 0
+    if place == frames + 1:
+        return jnp.minimum(my_frame + 1, count - 1), 0, my_frame < count - 1
+    return my_frame, place - 1, None
+
+
+def masked(block, keep):
+    if keep is None:
+        return block
+    return jnp.where(keep, block, jnp.zeros_like(block))
+
+
+def send_slots(total, parts, place, scratch):
+    channels = total.shape[0] // 4
+    scratch[...] = total
+    for slot in range(4):
+        owner = jnp.bitwise_xor(place, slot)
+        rows = pl.ds(pl.multiple_of(owner * channels, 16), channels)
+        parts[slot][...] = scratch[rows, :].astype(parts[slot].dtype)
+
+
+def group_total(mixer, sums):
+    wide = jnp.broadcast_to(sums, (sums.shape[0], LANES))
+    return jnp.dot(mixer, wide, precision=HIGH, preferred_element_type=F32)
+
+
+def first_kernel(frames, where, weight, gathered, p0, p1, p2, p3, patches, total):
+    my_frame, place = where[0], where[2]
+    count = gathered.shape[0] // 2
+
+    def block(spot, row):
+        owner, inner, keep = frame_block(spot, my_frame, frames, count)
+        return masked(gathered[owner * 2 + row, 0, :, pl.ds(inner * LANES, LANES)], keep)
+
+    fill_patches(patches, block, gathered.shape[2], frames, False)
+    out = jnp.dot(weight[...], patches[...], preferred_element_type=F32)
+    send_slots(out, (p0, p1, p2, p3), place, total)
+
+
+def statistics(sums, mixer, members):
+    blocks = sums.shape[0]
+    acc = sums[0]
+    for k in range(1, blocks):
+        acc = acc + sums[k]
+    mean = group_total(mixer, jnp.sum(acc, axis=1, keepdims=True))[:, :1] / members
+    acc = None
+    for k in range(blocks):
+        centered = sums[k] - mean
+        acc = centered * centered if acc is None else acc + centered * centered
+    variance = group_total(mixer, jnp.sum(acc, axis=1, keepdims=True))[:, :1] / members
+    return mean, lax.rsqrt(variance + EPSILON)
+
+
+def second_kernel(
+    frames, members, where, weight, mixer, sums, hidden, norm, scale, p0, p1, p2, p3, patches, total
+):
+    my_frame, my_row, place = where[0], where[1], where[2]
+    count = sums.shape[0] // 2
+    mean, inv = statistics(sums, mixer[...], members)
+    for k in range(sums.shape[0]):
+        normed = (sums[k] - mean) * inv
+        hidden[k] = (normed * jax.nn.sigmoid(normed)).astype(BF16)
+    norm[...] = (sums[my_frame * 2 + my_row] - mean) * inv
+    scale[...] = jnp.broadcast_to(inv, scale.shape)
+
+    def block(spot, row):
+        owner, inner, keep = frame_block(spot, my_frame, frames, count)
+        return masked(hidden[owner * 2 + row, :, pl.ds(inner * LANES, LANES)], keep)
+
+    fill_patches(patches, block, sums.shape[1], frames, False)
+    out = jnp.dot(weight[...], patches[...], preferred_element_type=F32)
+    send_slots(out, (p0, p1, p2, p3), place, total)
+
+
+def third_kernel(frames, members, where, mixer, sums, gathered, result, halo, grads, norms, ready):
+    my_frame, my_row = where[0], where[1]
+    blocks = sums.shape[0]
+    count = blocks // 2
+    mean, inv = statistics(sums, mixer[...], members)
+    first = second = None
+    for k in range(blocks):
+        normed = (sums[k] - mean) * inv
+        gate = jax.nn.sigmoid(normed)
+        grad = gathered[k, 1].astype(F32) * gate * (1.0 + normed * (1.0 - gate))
+        norms[k] = normed
+        grads[k] = grad
+        first = grad if first is None else first + grad
+        second = grad * normed if second is None else second + grad * normed
+    first = group_total(mixer[...], jnp.sum(first, axis=1, keepdims=True))[:, :1] / members
+    second = group_total(mixer[...], jnp.sum(second, axis=1, keepdims=True))[:, :1] / members
+    for k in range(blocks):
+        ready[k] = ((grads[k] - first - norms[k] * second) * inv).astype(BF16)
+    own = my_frame * 2 + my_row
+    normed = norms[own]
+    result[...] = (gathered[own, 0].astype(F32) + normed * jax.nn.sigmoid(normed)).astype(BF16)
+    for spot in range(frames + 2):
+        owner, inner, keep = frame_block(spot, my_frame, frames, count)
+        cells = ready[owner * 2 + my_row, :, pl.ds(inner * LANES, LANES)]
+        halo[:, pl.ds(spot * LANES, LANES)] = masked(cells, keep)
+
+
+def fourth_kernel(frames, where, weight, mine, theirs, norm, grad, sums, patches):
+    my_row, place = where[1], where[2]
+    channels = mine.shape[1]
+    for slot in range(4):
+        owner = jnp.bitwise_xor(place, slot)
+
+        def block(spot, row):
+            lanes = pl.ds(spot * LANES, LANES)
+            return jnp.where(my_row == row, mine[slot, :, lanes], theirs[slot, :, lanes])
+
+        fill_patches(
+            patches, block, channels, frames, True, owner * channels, 4 * channels
+        )
+    out = jnp.dot(weight[...], patches[...], preferred_element_type=F32)
+    normed = norm[...]
+    gate = jax.nn.sigmoid(normed)
+    out = out * gate * (1.0 + normed * (1.0 - gate))
+    grad[...] = out
+    lane = lax.broadcasted_iota(jnp.int32, sums.shape, 1)
+    sums[...] = jnp.where(
+        lane == 0,
+        jnp.sum(out, axis=1, keepdims=True),
+        jnp.where(lane == 1, jnp.sum(out * normed, axis=1, keepdims=True), 0.0),
+    )
+
+
+def fifth_kernel(members, where, mixer, sums, grad, norm, scale, out):
+    acc = sums[0]
+    for k in range(1, sums.shape[0]):
+        acc = acc + sums[k]
+    means = jnp.dot(mixer[...], acc, precision=HIGH, preferred_element_type=F32) / members
+    out[...] = ((grad[...] - means[:, :1] - norm[...] * means[:, 1:2]) * scale[:, :1]).astype(BF16)
+
+
+def spread(full, where, frames, pieces):
+    my_frame, my_row, place = where[0], where[1], where[2]
+    mine, theirs, near, far = pieces
+    channels = mine.shape[1]
+
+    def put(row, slot, frame_slot, value):
+        owner = jnp.bitwise_xor(place, slot)
+        rows = pl.ds(pl.multiple_of(owner * channels, 16), channels)
+        width = frames * LANES
+        lanes = pl.ds(pl.multiple_of(jnp.bitwise_xor(my_frame, frame_slot) * width, LANES), width)
+        full[row, rows, lanes] = value
+
+    for slot in range(4):
+        put(my_row, slot, 0, mine[slot])
+        put(1 - my_row, slot, 0, theirs[slot])
+    for index in range(3):
+        for half in range(2):
+            for side in range(2):
+                put(jnp.bitwise_xor(my_row, side), 2 * my_row + half, index + 1, near[index][side, half])
+                put(jnp.bitwise_xor(1 - my_row, side), 2 * (1 - my_row) + half, index + 1, far[index][side, half])
+
+
+def weight_step(inputs_at, frames, where, pieces, out, padded, full):
+    tap_frame = pl.program_id(0)
+    total = full.shape[2] // LANES
+    count = total // frames
+
+    @pl.when(tap_frame == 0)
+    def _():
+        spread(full, where, frames, pieces)
+        channels = padded.shape[0] // 6
+        zeros = jnp.zeros((padded.shape[0], LANES), padded.dtype)
+        padded[:, pl.ds(0, LANES)] = zeros
+        padded[:, pl.ds((total + 1) * LANES, LANES)] = zeros
+        for frame in range(total):
+            for row in range(2):
+                cells = inputs_at(frame // frames * 2 + row, frame % frames)
+                for tap_col in range(3):
+                    rows = pl.ds((row * 3 + tap_col) * channels, channels)
+                    padded[rows, pl.ds((frame + 1) * LANES, LANES)] = shift(cells, tap_col)
+
+    channels = padded.shape[0] // 6
+    window = padded[:, pl.ds(pl.multiple_of(tap_frame * LANES, LANES), total * LANES)]
+    top = lax.dot_general(window, full[0], (((1,), (1,)), ((), ())), preferred_element_type=F32)
+    low = lax.dot_general(window, full[1], (((1,), (1,)), ((), ())), preferred_element_type=F32)
+    for tap_col in range(3):
+        upper = slice(tap_col * channels, (tap_col + 1) * channels)
+        under = slice((3 + tap_col) * channels, (4 + tap_col) * channels)
+        out[tap_col] = low[upper]
+        out[3 + tap_col] = top[upper] + low[under]
+        out[6 + tap_col] = top[under]
+
+
+def weight_kernel(frames, where, inputs, mine, theirs, n1, n2, n3, f1, f2, f3, out, padded, full):
+    weight_step(
+        lambda k, inner: inputs[k, :, pl.ds(inner * LANES, LANES)],
+        frames, where, (mine, theirs, (n1, n2, n3), (f1, f2, f3)), out, padded, full,
+    )
+
+
+def last_kernel(
+    frames, where, weight, inputs, mine, theirs, n1, n2, n3, f1, f2, f3, out, back, padded, full, patches
+):
+    weight_step(
+        lambda k, inner: inputs[k, 0, :, pl.ds(inner * LANES, LANES)],
+        frames, where, (mine, theirs, (n1, n2, n3), (f1, f2, f3)), out, padded, full,
+    )
+
+    @pl.when(pl.program_id(0) == 0)
+    def _():
+        my_frame, my_row = where[0], where[1]
+        total = full.shape[2] // LANES
+
+        def block(spot, row):
+            frame = my_frame * frames - 1 + spot
+            keep = None
+            if spot == 0:
+                keep = frame >= 0
+                frame = jnp.maximum(frame, 0)
+            elif spot == frames + 1:
+                keep = frame < total
+                frame = jnp.minimum(frame, total - 1)
+            return masked(full[row, :, pl.ds(pl.multiple_of(frame * LANES, LANES), LANES)], keep)
+
+        fill_patches(patches, block, full.shape[1], frames, True)
+        grown = jnp.dot(weight[...], patches[...], preferred_element_type=F32)
+        back[...] = (inputs[my_frame * 2 + my_row, 1].astype(F32) + grown).astype(BF16)
+
+
+def swap(values):
+    return lax.ppermute(values, "row", [(0, 1), (1, 0)])
+
+
+def hop(values, axis, step):
+    return lax.ppermute(values, axis, [(i, i ^ step) for i in range(4)])
+
+
+def over_channels(parts):
+    return parts[0] + sum(hop(parts[k], "chan", k).astype(F32) for k in range(1, 4))
+
+
+def exchange(mine, theirs, my_row):
+    both = jnp.stack([mine, theirs])
+    half = lax.dynamic_slice_in_dim(both, 2 * my_row, 2, axis=1)
+    near = [hop(half, "frame", k) for k in range(1, 4)]
+    return near, [swap(values) for values in near]
+
+
+def shards_paired(activations, conv_first, conv_second, cotangent):
+    layout = activations.shape
+    channels, frames = layout[0], layout[1]
+    cells = frames * LANES
+    count = lax.axis_size("frame")
+    wide = 4 * channels
+    members = (C // GROUPS) * cells * count * 2
+    my_frame, my_row, place = (lax.axis_index(a) for a in ("frame", "row", "chan"))
+    where = jnp.stack([my_frame, my_row, place]).astype(jnp.int32)
+    group = jnp.arange(channels) // (C // GROUPS)
+    mixer = (group[:, None] == group[None, :]).astype(F32)
+    conv_cost = dict(flops=2 * channels * wide * 18 * cells, reads=18 * channels * wide * 2)
+
+    def ahead(weight):
+        taps = lax.dynamic_slice_in_dim(weight.reshape(3, 3, 3, channels, wide), 1 - my_row, 2, axis=1)
+        return taps.reshape(18 * channels, wide).T
+
+    def behind(weight):
+        taps = lax.dynamic_slice_in_dim(weight.reshape(3, 3, 3, channels, wide), my_row, 2, axis=1)
+        return taps.transpose(3, 0, 1, 2, 4).reshape(channels, 18 * wide)
+
+    sums_shape = jax.ShapeDtypeStruct((channels, cells), F32)
+    cells_shape = jax.ShapeDtypeStruct((channels, cells), BF16)
+    parts_shape = [sums_shape] + [jax.ShapeDtypeStruct((channels, cells), LINK)] * 3
+    patches = pltpu.VMEM((18 * channels, cells), BF16)
+    wide_patches = pltpu.VMEM((18 * wide, cells), BF16)
+    total = pltpu.VMEM((wide, cells), F32)
+
+    pair = jnp.stack([activations.reshape(channels, cells), cotangent.reshape(channels, cells)])
+    gathered = lax.all_gather(pair, FR, axis=0)
+    parts = call(
+        functools.partial(first_kernel, frames), parts_shape,
+        (where, ahead(conv_first), gathered), (patches, total), **conv_cost,
+    )
+    first_sums = lax.all_gather(over_channels(parts), FR, axis=0)
+    hidden, norm, scale, *parts = call(
+        functools.partial(second_kernel, frames, members),
+        [
+            jax.ShapeDtypeStruct((2 * count, channels, cells), BF16),
+            sums_shape,
+            jax.ShapeDtypeStruct((channels, LANES), F32),
+            *parts_shape,
+        ],
+        (where, ahead(conv_second), mixer, first_sums), (patches, total), **conv_cost,
+    )
+    second_sums = lax.all_gather(over_channels(parts), FR, axis=0)
+    blocks = (2 * count, channels, cells)
+    result, halo = call(
+        functools.partial(third_kernel, frames, members),
+        [cells_shape, jax.ShapeDtypeStruct((channels, cells + 2 * LANES), BF16)],
+        (where, mixer, second_sums, gathered),
+        (pltpu.VMEM(blocks, F32), pltpu.VMEM(blocks, F32), pltpu.VMEM(blocks, BF16)),
+    )
+    mine = jnp.stack([halo] + [hop(halo, "chan", k) for k in range(1, 4)])
+    theirs = swap(mine)
+    grad, sums = call(
+        functools.partial(fourth_kernel, frames),
+        [sums_shape, jax.ShapeDtypeStruct((channels, LANES), F32)],
+        (where, behind(conv_second), mine, theirs, norm), (wide_patches,), **conv_cost,
+    )
+    own_mine = mine[:, :, LANES:-LANES]
+    own_theirs = theirs[:, :, LANES:-LANES]
+    near, far = exchange(own_mine, own_theirs, my_row)
+
+    sums = lax.all_gather(sums, FR, axis=0)
+    (grad_first,) = call(
+        functools.partial(fifth_kernel, members), [cells_shape], (where, mixer, sums, grad, norm, scale)
+    )
+    padded = pltpu.VMEM((6 * channels, (frames * count + 2) * LANES), BF16)
+    full = pltpu.VMEM((2, wide, cells * count), BF16)
+    grad_shape = jax.ShapeDtypeStruct((27, channels, wide), F32)
+    grad_spec = pl.BlockSpec((9, channels, wide), lambda a: (a, 0, 0))
+    grad_cost = dict(flops=2 * 18 * channels * wide * cells * count * 2, reads=8000000)
+    (second_grad,) = call(
+        functools.partial(weight_kernel, frames), [grad_shape],
+        (where, hidden, own_mine, own_theirs, *near, *far), (padded, full),
+        grid=(3,), specs=[grad_spec], **grad_cost,
+    )
+    mine = jnp.stack([grad_first] + [hop(grad_first, "chan", k) for k in range(1, 4)])
+    theirs = swap(mine)
+    near, far = exchange(mine, theirs, my_row)
+    first_grad, input_grad = call(
+        functools.partial(last_kernel, frames), [grad_shape, cells_shape],
+        (where, behind(conv_first), gathered, mine, theirs, *near, *far), (padded, full, wide_patches),
+        grid=(3,), specs=[grad_spec, pl.BlockSpec((channels, cells), lambda a: (0, 0))], **grad_cost,
+    )
+    return (result.reshape(layout), input_grad.reshape(layout), first_grad, second_grad)
+
+
+def paired(mesh):
+    return mesh.shape["frame"] == 4 and mesh.shape["row"] == 2 and mesh.shape["chan"] == 4
+
+
 def solution(mesh):
     return jax.shard_map(
-        shards,
+        shards_paired if paired(mesh) else shards_general,
         mesh=mesh,
         in_specs=(
             P("chan", "frame", "row", None),

time: 796 us -> 173 us (0.22); the launches traced: 781 us -> 172 us
  local copies, waits for them, and re-layouts: 385 us -> 20.7 us
  waiting for transfers between devices: 210 us -> 38.7 us
  Pallas kernels: 0 us -> 35.1 us
  starting transfers between devices: 54.8 us -> 27.1 us
  blocking collectives: 73.3 us -> 46.4 us
  matrix products: 24.4 us -> 0 us
  other arithmetic: 18.7 us -> 3.45 us
  between operations: 14.9 us -> 0.85 us
    another operation x111 -> x4, local copies, waits for them, and re-layouts: 139 us -> 2.53 us  [the longest x2 2.41 us: exchange(): both = jnp.stack([mine, theirs])]
    slice x94 -> x0, local copies, waits for them, and re-layouts: 131 us -> none  [the longest x90 130 us: collect(): padded[:, anchor[0]:anchor[0] + frames, anchor[1]:anchor[1] + height, anc...]
    unnamed x259 -> x36, local copies, waits for them, and re-layouts: 111 us -> 6.25 us
    psum x1 -> x0, waiting for transfers between devices: 87.7 us -> none  [reduce_weights(): return lax.psum(weight_grad, ('frame', 'row'))]
    psum x6 -> x0, blocking collectives: 73.3 us -> none  [the longest x2 25.4 us: norm_back(): lax.psum((jnp.sum(grouped_grad, axis=1), jnp.sum(grouped_grad * grouped_n...]
    all_gather x2 -> x0, waiting for transfers between devices: 68 us -> none  [back_conv(): portion = lax.all_gather(rimmed, 'chan', axis=0, tiled=True)]
    all_gather x0 -> x4, blocking collectives: none -> 46.4 us  [the longest x1 13.3 us: shards_paired(): gathered = lax.all_gather(pair, FR, axis=0)]
    reduce_scatter x2 -> x0, waiting for transfers between devices: 42.7 us -> none  [forward_conv(): lax.psum_scatter(lax.dot_general(flat_weight, flat_own, (((0,), (0,)), ((...]
  transfers between devices with their start and end apart: 21 -> 26, of which waited for: 12 -> 11; matrix products, arithmetic and copies ran while one was open for 4% -> 7% of each run, Pallas kernels for 0% -> 5%
where the time goes in v1:
time: 173 us; the launch traced here: 172 us
  blocking collectives  46.4 us (27%)
  waiting for transfers between devices  38.7 us (22%)
  Pallas kernels  35.1 us (20%)
  starting transfers between devices  27.1 us (16%)
  local copies, waits for them, and re-layouts  20.7 us (12%)
  other arithmetic  3.45 us (2%)
    ppermute x18, waiting for transfers between devices, hop(): return lax.ppermute(values, axis, [(i, i ^ step) for i in range(4)])  38.7 us
    pallas_call x7, Pallas kernels, call(): pl.pallas_call(kernel, out_shape=outs, in_specs=in_specs, out_specs=[vmem...  35.1 us
    ppermute x18, starting transfers between devices, hop(): return lax.ppermute(values, axis, [(i, i ^ step) for i in range(4)])  25.4 us
    all_gather x1, blocking collectives, shards_paired(): gathered = lax.all_gather(pair, FR, axis=0)  13.3 us
    all_gather x1, blocking collectives, shards_paired(): first_sums = lax.all_gather(over_channels(parts), FR, axis=0)  11.7 us
    all_gather x1, blocking collectives, shards_paired(): second_sums = lax.all_gather(over_channels(parts), FR, axis=0)  10.9 us
    all_gather x1, blocking collectives, shards_paired(): sums = lax.all_gather(sums, FR, axis=0)  10.5 us
    unnamed x36, local copies, waits for them, and re-layouts  6.25 us
  transfers between devices with their start and end apart: 26, of which 11 were waited for; matrix products, arithmetic and copies ran while one was open for 7% of the time, Pallas kernels for 5%

profile of v1, /device:TPU:0, one launch (start us, length us, event | category | flops | bytes accessed | tf_op | source)
XLA Modules:
  0.0 172.4 jit_solution(5290208597076230175)
XLA Ops:
  0.6 3.7 %constant_dynamic-slice_fusion = (bf16[3,2,3,80,320]{4,3,2,1,0:T(8,128)(2,1)}, bf16[3,2,3,80,320]{4,3,2,1,0:T(8,128)(2,1)S(1)}, bf16[3,2,3,80,320]{4,3,2,1,0:T(8,128)(2,1)S(1)}, bf16[3,2,3,80,320]{4,3,2,1,0:T(8,128)(2,1)S(1)}) fusion(bf16[3,3,3,80,320]{4,3,2,1,0:T(8,128)(2,1)} %bitcast.49, s32[]{:T(128)S(6)} %select_n.31, s32[]{:T(128)S(6)} %select_n.30, ...), kind=kLoop, calls=%fused_computation.14 | loop fusion | bytes 7372808 | tf_op jit(solution)/shard_map/dynamic_slice | solution.py:478
  4.4 1.9 %copy.23 = bf16[1440,320]{0,1:T(8,128)(2,1)} copy(bf16[1440,320]{1,0:T(8,128)(2,1)S(1)} %bitcast.44) | data formatting | bytes 1843200 | tf_op jit(solution)/shard_map/reshape | solution.py:475
  6.5 13.3 %all-gather = bf16[16,80,384]{2,1,0:T(8,128)(2,1)} all-gather(bf16[2,80,384]{2,1,0:T(8,128)(2,1)S(1)} %pad_maximum_fusion.2), channel_id=2, replica_groups=mesh['frame'=4,'row'=2,'chan'=4] {'frame','row'}, dimensions={0}, use_global_device_ids=true | all-gather | bytes 1105920 | tf_op jit(solution)/shard_map/all_gather | solution.py:489
  20.5 3.1 %shard_map.75 = (f32[80,384]{1,0:T(8,128)}, f32[80,384]{1,0:T(8,128)}, f32[80,384]{1,0:T(8,128)}, f32[80,384]{1,0:T(8,128)}) custom-call(s32[3]{0:T(128)} %pad_add_fusion.where, bf16[320,1440]{1,0:T(8,128)(2,1)} %bitcast.46, bf16[8,2,80,384]{3,2,1,0:T(8,128)(2,1)} %bitcast.38), custom_call_target="tpu_custom_call" | custom-call | flops 353894400 | bytes 921600 | tf_op jit(solution)/shard_map/pallas_call | solution.py:175
  23.6 3.6 %collective-permute-start.2 = (f32[80,384]{1,0:T(8,128)}, f32[80,384]{1,0:T(8,128)S(1)}, u32[]{:S(2)}, u32[]{:S(2)}) collective-permute-start(f32[80,384]{1,0:T(8,128)} %get-tuple-element.24), channel_id=1, source_target_pairs={{0,3},{1,2},{2,1},{3,0},{4,7},{5,6},{6,5},{7,4},{8,11},{9,10},{10,... | collective-permute-start | bytes 368648 | tf_op jit(solution)/shard_map/ppermute | solution.py:446
  27.2 0.8 collective-permute-start.1
  28.0 1.9 %copy.22 = bf16[1440,320]{0,1:T(8,128)(2,1)} copy(bf16[1440,320]{1,0:T(8,128)(2,1)S(1)} %bitcast.43) | data formatting | bytes 1843200 | tf_op jit(solution)/shard_map/reshape | solution.py:475
  30.6 1.2 collective-permute-done.2
  31.8 3.2 %collective-permute-done = f32[80,384]{1,0:T(8,128)S(1)} collective-permute-done((f32[80,384]{1,0:T(8,128)}, f32[80,384]{1,0:T(8,128)S(1)}, u32[]{:S(2)}, u32[]{:S(2)}) %collective-permute-start) | collective-permute-done | bytes 122912 | tf_op jit(solution)/shard_map/ppermute | solution.py:446
  35.0 3.3 %collective-permute-done.1 = f32[80,384]{1,0:T(8,128)S(1)} collective-permute-done((f32[80,384]{1,0:T(8,128)}, f32[80,384]{1,0:T(8,128)S(1)}, u32[]{:S(2)}, u32[]{:S(2)}) %collective-permute-start.1) | collective-permute-done | bytes 122912 | tf_op jit(solution)/shard_map/ppermute | solution.py:446
  38.4 11.7 %all-gather.1 = f32[640,384]{1,0:T(8,128)} all-gather(f32[80,384]{1,0:T(8,128)S(1)} %add_add_fusion.1), channel_id=3, replica_groups=mesh['frame'=4,'row'=2,'chan'=4] {'frame','row'}, dimensions={0}, use_global_device_ids=true | all-gather | bytes 1105920 | tf_op jit(solution)/shard_map/all_gather | solution.py:494
  50.1 4.1 %shard_map.76 = (bf16[8,80,384]{2,1,0:T(8,128)(2,1)}, f32[80,384]{1,0:T(8,128)}, f32[80,128]{1,0:T(8,128)}, f32[80,384]{1,0:T(8,128)}, f32[80,384]{1,0:T(8,128)}, /*index=5*/f32[80,384]{1,0:T(8,128)}, f32[80,384]{1,0:T(8,128)}) custom-call(s32[3]{0:T(128)} %pad_add_fusion.where, bf16[320,1440]{1,0:T(8,128)(2,1)} %bitcast.45, ...), custom_call_target="tpu_custom_call" | custom-call | flops 353894400 | bytes 921600 | tf_op jit(solution)/shard_map/pallas_call | solution.py:175
  54.1 2.5 %collective-permute-start.5 = (f32[80,384]{1,0:T(8,128)}, f32[80,384]{1,0:T(8,128)S(1)}, u32[]{:S(2)}, u32[]{:S(2)}) collective-permute-start(f32[80,384]{1,0:T(8,128)} %get-tuple-element.28), channel_id=1, source_target_pairs={{0,3},{1,2},{2,1},{3,0},{4,7},{5,6},{6,5},{7,4},{8,11},{9,10},{10,... | collective-permute-start | bytes 368648 | tf_op jit(solution)/shard_map/ppermute | solution.py:446
  56.6 1.9 %collective-permute-start.4 = (f32[80,384]{1,0:T(8,128)}, f32[80,384]{1,0:T(8,128)S(1)}, u32[]{:S(2)}, u32[]{:S(2)}) collective-permute-start(f32[80,384]{1,0:T(8,128)} %get-tuple-element.27), channel_id=1, source_target_pairs={{0,2},{1,3},{2,0},{3,1},{4,6},{5,7},{6,4},{7,5},{8,10},{9,11},{10,... | collective-permute-start | bytes 368648 | tf_op jit(solution)/shard_map/ppermute | solution.py:446
  58.5 3.9 %collective-permute-done.5 = f32[80,384]{1,0:T(8,128)S(1)} collective-permute-done((f32[80,384]{1,0:T(8,128)}, f32[80,384]{1,0:T(8,128)S(1)}, u32[]{:S(2)}, u32[]{:S(2)}) %collective-permute-start.5) | collective-permute-done | bytes 122912 | tf_op jit(solution)/shard_map/ppermute | solution.py:446
  62.4 4.7 %collective-permute-done.3 = f32[80,384]{1,0:T(8,128)S(1)} collective-permute-done((f32[80,384]{1,0:T(8,128)}, f32[80,384]{1,0:T(8,128)S(1)}, u32[]{:S(2)}, u32[]{:S(2)}) %collective-permute-start.3) | collective-permute-done | bytes 122912 | tf_op jit(solution)/shard_map/ppermute | solution.py:446
  67.1 0.9 add_add_fusion
  68.0 10.9 %all-gather.2 = f32[640,384]{1,0:T(8,128)} all-gather(f32[80,384]{1,0:T(8,128)S(1)} %add_add_fusion), channel_id=4, replica_groups=mesh['frame'=4,'row'=2,'chan'=4] {'frame','row'}, dimensions={0}, use_global_device_ids=true | all-gather | bytes 1105920 | tf_op jit(solution)/shard_map/all_gather | solution.py:505
  79.0 3.9 %shard_map.77 = (bf16[80,384]{1,0:T(8,128)(2,1)}, bf16[80,640]{1,0:T(8,128)(2,1)}) custom-call(s32[3]{0:T(128)} %pad_add_fusion.where, f32[80,80]{1,0:T(8,128)} %compare_convert_fusion.mixer, f32[8,80,384]{2,1,0:T(8,128)} %bitcast.48, bf16[8,2,80,384]{3,2,1,0:T(8,128)(2,1)} %bitcast.39), custom_call_target="tpu_custom_call" | custom-call | tf_op jit(solution)/shard_map/pallas_call | solution.py:175
  82.8 2.7 %collective-permute-start.8 = (bf16[80,640]{1,0:T(8,128)(2,1)}, bf16[80,640]{1,0:T(8,128)(2,1)S(1)}, u32[]{:S(2)}, u32[]{:S(2)}) collective-permute-start(bf16[80,640]{1,0:T(8,128)(2,1)} %get-tuple-element.30), channel_id=1, source_target_pairs={{0,3},{1,2},{2,1},{3,0},{4,7},{5,6},{6,5},{7,4},{8,11},{9,10},{10,... | collective-permute-start | bytes 307208 | tf_op jit(solution)/shard_map/ppermute | solution.py:446
  85.5 1.7 %collective-permute-start.6 = (bf16[80,640]{1,0:T(8,128)(2,1)}, bf16[80,640]{1,0:T(8,128)(2,1)S(1)}, u32[]{:S(2)}, u32[]{:S(2)}) collective-permute-start(bf16[80,640]{1,0:T(8,128)(2,1)} %get-tuple-element.30), channel_id=1, source_target_pairs={{0,1},{1,0},{2,3},{3,2},{4,5},{5,4},{6,7},{7,6},{8,9},{9,8},{10,11... | collective-permute-start | bytes 307208 | tf_op jit(solution)/shard_map/ppermute | solution.py:446
  87.2 3.4 %collective-permute-done.8 = bf16[80,640]{1,0:T(8,128)(2,1)S(1)} collective-permute-done((bf16[80,640]{1,0:T(8,128)(2,1)}, bf16[80,640]{1,0:T(8,128)(2,1)S(1)}, u32[]{:S(2)}, u32[]{:S(2)}) %collective-permute-start.8) | collective-permute-done | bytes 102432 | tf_op jit(solution)/shard_map/ppermute | solution.py:446
  90.7 4.2 %collective-permute-done.7 = bf16[80,640]{1,0:T(8,128)(2,1)S(1)} collective-permute-done((bf16[80,640]{1,0:T(8,128)(2,1)}, bf16[80,640]{1,0:T(8,128)(2,1)S(1)}, u32[]{:S(2)}, u32[]{:S(2)}) %collective-permute-start.7) | collective-permute-done | bytes 102432 | tf_op jit(solution)/shard_map/ppermute | solution.py:446
  94.8 1.0 pad_maximum_fusion.mine
  95.9 1.9 %copy.34 = bf16[3,2,3,80,320]{4,2,1,0,3:T(4,128)(2,1)S(1)} copy(bf16[3,2,3,80,320]{4,3,2,1,0:T(8,128)(2,1)} %get-tuple-element.50) | data formatting | bytes 1843200
  97.8 1.8 %reshape.66.weight = bf16[80,5760]{1,0:T(8,128)(2,1)} reshape(bf16[80,3,2,3,320]{4,3,2,1,0:T(4,128)(2,1)S(1)} %bitcast.41) | data formatting | bytes 1843200 | tf_op jit(solution)/shard_map/reshape | solution.py:479
  99.5 0.7 slice_bitcast_fusion.1
  100.3 0.7 copy-done.1
  101.0 3.7 %shard_map.78 = (f32[80,384]{1,0:T(8,128)}, f32[80,128]{1,0:T(8,128)}) custom-call(s32[3]{0:T(128)} %pad_add_fusion.where, bf16[80,5760]{1,0:T(8,128)(2,1)} %reshape.66.weight, bf16[4,80,640]{2,1,0:T(8,128)(2,1)} %copy-done, bf16[4,80,640]{2,1,0:T(8,128)(2,1)} %copy-done.1, f32[80,384]{1,0:T(8,128)} %get-tuple-element.31.norm), custom_call_target="tpu_custom_call" | custom-call | flops 353894400 | bytes 921600 | tf_op jit(solution)/shard_map/pallas_call | solution.py:175
  104.7 10.5 %all-gather.3 = f32[640,128]{1,0:T(8,128)} all-gather(f32[80,128]{1,0:T(8,128)} %get-tuple-element.32), channel_id=5, replica_groups=mesh['frame'=4,'row'=2,'chan'=4] {'frame','row'}, dimensions={0}, use_global_device_ids=true | all-gather | bytes 368640 | tf_op jit(solution)/shard_map/all_gather | solution.py:524
  115.2 2.0 %shard_map.79 = bf16[80,384]{1,0:T(8,128)(2,1)} custom-call(s32[3]{0:T(128)} %pad_add_fusion.where, f32[80,80]{1,0:T(8,128)} %compare_convert_fusion.mixer, f32[8,80,128]{2,1,0:T(8,128)} %bitcast.51, f32[80,384]{1,0:T(8,128)} %get-tuple-element.33.grad, f32[80,384]{1,0:T(8,128)} %get-tuple-element.31.norm, f32[80,128]{1,0:T(8,128)} %get-tuple-element.34.scale), custom_call_target="tpu_custom_call" | custom-call | tf_op jit(solution)/shard_map/pallas_call | solution.py:175
  117.2 2.5 %collective-permute-start.12 = (bf16[80,384]{1,0:T(8,128)(2,1)}, bf16[80,384]{1,0:T(8,128)(2,1)S(1)}, u32[]{:S(2)}, u32[]{:S(2)}) collective-permute-start(bf16[80,384]{1,0:T(8,128)(2,1)} %shard_map.79), channel_id=1, source_target_pairs={{0,3},{1,2},{2,1},{3,0},{4,7},{5,6},{6,5},{7,4},{8,11},{9,10},{10,... | collective-permute-start | bytes 184328 | tf_op jit(solution)/shard_map/ppermute | solution.py:446
  119.7 1.9 %collective-permute-start.10 = (bf16[80,384]{1,0:T(8,128)(2,1)}, bf16[80,384]{1,0:T(8,128)(2,1)S(1)}, u32[]{:S(2)}, u32[]{:S(2)}) collective-permute-start(bf16[80,384]{1,0:T(8,128)(2,1)} %shard_map.79), channel_id=1, source_target_pairs={{0,1},{1,0},{2,3},{3,2},{4,5},{5,4},{6,7},{7,6},{8,9},{9,8},{10,11... | collective-permute-start | bytes 184328 | tf_op jit(solution)/shard_map/ppermute | solution.py:446
  121.5 1.7 slice_bitcast_fusion
  123.3 1.4 collective-permute-start.20
  124.7 1.4 collective-permute-done.11
  126.2 1.4 collective-permute-start.21
  127.7 1.5 collective-permute-start.22
  129.1 1.7 collective-permute-done.20.n1
  130.9 1.4 collective-permute-start.14
  133.0 7.3 %collective-permute-done.21.n2 = bf16[2,2,80,384]{3,2,1,0:T(8,128)(2,1)S(1)} collective-permute-done((bf16[2,2,80,384]{3,2,1,0:T(8,128)(2,1)S(1)}, bf16[2,2,80,384]{3,2,1,0:T(8,128)(2,1)S(1)}, u32[]{:S(2)}, u32[]{:S(2)}) %collective-permute-start.21) | collective-permute-done | bytes 245792 | tf_op jit(solution)/shard_map/ppermute | solution.py:446
  140.3 1.5 collective-permute-start.16
  143.1 1.8 %reshape.65.weight = bf16[80,5760]{1,0:T(8,128)(2,1)} reshape(bf16[80,3,2,3,320]{4,3,2,1,0:T(4,128)(2,1)S(1)} %bitcast.42) | data formatting | bytes 1843200 | tf_op jit(solution)/shard_map/reshape | solution.py:479
  146.0 4.5 %collective-permute-done.15.n2 = bf16[2,2,80,384]{3,2,1,0:T(8,128)(2,1)} collective-permute-done((bf16[2,2,80,384]{3,2,1,0:T(8,128)(2,1)S(1)}, bf16[2,2,80,384]{3,2,1,0:T(8,128)(2,1)}, u32[]{:S(2)}, u32[]{:S(2)}) %collective-permute-start.15) | collective-permute-done | bytes 245792 | tf_op jit(solution)/shard_map/ppermute | solution.py:446
  151.0 8.4 %shard_map.81 = f32[27,80,320]{2,1,0:T(8,128)} custom-call(s32[3]{0:T(128)} %pad_add_fusion.where, bf16[8,80,384]{2,1,0:T(8,128)(2,1)} %get-tuple-element.37.inputs, bf16[4,80,384]{2,1,0:T(8,128)(2,1)} %get-tuple-element.57.mine, bf16[4,80,384]{2,1,0:T(8,128)(2,1)} %get-tuple-element.55.theirs, bf16[2,2,80,384]{3,2,1,0:T(8,128)(2,1)} %copy-done.9, ...), custom_call_target="tpu_custom_call" | custom-call | flops 2831155200 | bytes 8000000 | tf_op jit(solution)/shard_map/pallas_call | solution.py:175
  160.2 0.7 copy-done.14
  160.9 10.0 %shard_map.80 = (f32[27,80,320]{2,1,0:T(8,128)}, bf16[80,384]{1,0:T(8,128)(2,1)}) custom-call(s32[3]{0:T(128)} %pad_add_fusion.where, bf16[80,5760]{1,0:T(8,128)(2,1)} %reshape.65.weight, bf16[8,2,80,384]{3,2,1,0:T(8,128)(2,1)} %bitcast.40, bf16[4,80,384]{2,1,0:T(8,128)(2,1)} %copy-done.2, bf16[4,80,384]{2,1,0:T(8,128)(2,1)} %copy-done.3, ...), custom_call_target="tpu_custom_call" | custom-call | flops 2831155200 | bytes 8000000 | tf_op jit(solution)/shard_map/pallas_call | solution.py:175
  170.9 0.9 reshape.67
  (72 shorter events, 7.0 us)
Async XLA Ops:
  4.4 1.9 %copy-start.6 = (bf16[80,3,1,128]{3,0,2,1:T(8,128)(2,1)S(1)}, bf16[80,3,1,128]{3,0,2,1:T(8,128)(2,1)}, u32[]{:S(2)}) copy-start(bf16[80,3,1,128]{3,0,2,1:T(8,128)(2,1)} %param.7) | copy-start | bytes 184324
  4.4 2.0 %copy-start.7 = (bf16[80,3,1,128]{3,0,2,1:T(8,128)(2,1)S(1)}, bf16[80,3,1,128]{3,0,2,1:T(8,128)(2,1)}, u32[]{:S(2)}) copy-start(bf16[80,3,1,128]{3,0,2,1:T(8,128)(2,1)} %param.4) | copy-start | bytes 184324
  23.6 14.7 %copy-start.5 = (f32[80,384]{1,0:T(8,128)S(1)}, f32[80,384]{1,0:T(8,128)}, u32[]{:S(2)}) copy-start(f32[80,384]{1,0:T(8,128)} %get-tuple-element.21) | copy-start | bytes 368644
  23.6 8.2 %collective-permute-start.2 = (f32[80,384]{1,0:T(8,128)}, f32[80,384]{1,0:T(8,128)S(1)}, u32[]{:S(2)}, u32[]{:S(2)}) collective-permute-start(f32[80,384]{1,0:T(8,128)} %get-tuple-element.24), channel_id=1, source_target_pairs={{0,3},{1,2},{2,1},{3,0},{4,7},{5,6},{6,5},{7,4},{8,11},{9,10},{10,... | collective-permute-start | bytes 368648 | tf_op jit(solution)/shard_map/ppermute | solution.py:446
  27.2 7.8 %collective-permute-start = (f32[80,384]{1,0:T(8,128)}, f32[80,384]{1,0:T(8,128)S(1)}, u32[]{:S(2)}, u32[]{:S(2)}) collective-permute-start(f32[80,384]{1,0:T(8,128)} %get-tuple-element.22), channel_id=1, source_target_pairs={{0,1},{1,0},{2,3},{3,2},{4,5},{5,4},{6,7},{7,6},{8,9},{9,8},{10,11... | collective-permute-start | bytes 368648 | tf_op jit(solution)/shard_map/ppermute | solution.py:446
  27.2 11.1 %collective-permute-start.1 = (f32[80,384]{1,0:T(8,128)}, f32[80,384]{1,0:T(8,128)S(1)}, u32[]{:S(2)}, u32[]{:S(2)}) collective-permute-start(f32[80,384]{1,0:T(8,128)} %get-tuple-element.23), channel_id=1, source_target_pairs={{0,2},{1,3},{2,0},{3,1},{4,6},{5,7},{6,4},{7,5},{8,10},{9,11},{10,... | collective-permute-start | bytes 368648 | tf_op jit(solution)/shard_map/ppermute | solution.py:446
  54.1 8.2 %collective-permute-start.5 = (f32[80,384]{1,0:T(8,128)}, f32[80,384]{1,0:T(8,128)S(1)}, u32[]{:S(2)}, u32[]{:S(2)}) collective-permute-start(f32[80,384]{1,0:T(8,128)} %get-tuple-element.28), channel_id=1, source_target_pairs={{0,3},{1,2},{2,1},{3,0},{4,7},{5,6},{6,5},{7,4},{8,11},{9,10},{10,... | collective-permute-start | bytes 368648 | tf_op jit(solution)/shard_map/ppermute | solution.py:446
  56.6 10.5 %collective-permute-start.3 = (f32[80,384]{1,0:T(8,128)}, f32[80,384]{1,0:T(8,128)S(1)}, u32[]{:S(2)}, u32[]{:S(2)}) collective-permute-start(f32[80,384]{1,0:T(8,128)} %get-tuple-element.26), channel_id=1, source_target_pairs={{0,1},{1,0},{2,3},{3,2},{4,5},{5,4},{6,7},{7,6},{8,9},{9,8},{10,11... | collective-permute-start | bytes 368648 | tf_op jit(solution)/shard_map/ppermute | solution.py:446
  56.6 10.5 %collective-permute-start.4 = (f32[80,384]{1,0:T(8,128)}, f32[80,384]{1,0:T(8,128)S(1)}, u32[]{:S(2)}, u32[]{:S(2)}) collective-permute-start(f32[80,384]{1,0:T(8,128)} %get-tuple-element.27), channel_id=1, source_target_pairs={{0,2},{1,3},{2,0},{3,1},{4,6},{5,7},{6,4},{7,5},{8,10},{9,11},{10,... | collective-permute-start | bytes 368648 | tf_op jit(solution)/shard_map/ppermute | solution.py:446
  82.8 7.8 %collective-permute-start.8 = (bf16[80,640]{1,0:T(8,128)(2,1)}, bf16[80,640]{1,0:T(8,128)(2,1)S(1)}, u32[]{:S(2)}, u32[]{:S(2)}) collective-permute-start(bf16[80,640]{1,0:T(8,128)(2,1)} %get-tuple-element.30), channel_id=1, source_target_pairs={{0,3},{1,2},{2,1},{3,0},{4,7},{5,6},{6,5},{7,4},{8,11},{9,10},{10,... | collective-permute-start | bytes 307208 | tf_op jit(solution)/shard_map/ppermute | solution.py:446
  85.5 9.3 %collective-permute-start.7 = (bf16[80,640]{1,0:T(8,128)(2,1)}, bf16[80,640]{1,0:T(8,128)(2,1)S(1)}, u32[]{:S(2)}, u32[]{:S(2)}) collective-permute-start(bf16[80,640]{1,0:T(8,128)(2,1)} %get-tuple-element.30), channel_id=1, source_target_pairs={{0,2},{1,3},{2,0},{3,1},{4,6},{5,7},{6,4},{7,5},{8,10},{9,11},{10,... | collective-permute-start | bytes 307208 | tf_op jit(solution)/shard_map/ppermute | solution.py:446
  85.5 9.3 %collective-permute-start.6 = (bf16[80,640]{1,0:T(8,128)(2,1)}, bf16[80,640]{1,0:T(8,128)(2,1)S(1)}, u32[]{:S(2)}, u32[]{:S(2)}) collective-permute-start(bf16[80,640]{1,0:T(8,128)(2,1)} %get-tuple-element.30), channel_id=1, source_target_pairs={{0,1},{1,0},{2,3},{3,2},{4,5},{5,4},{6,7},{7,6},{8,9},{9,8},{10,11... | collective-permute-start | bytes 307208 | tf_op jit(solution)/shard_map/ppermute | solution.py:446
  95.8 3.7 %copy-start = (bf16[4,80,640]{2,1,0:T(8,128)(2,1)}, bf16[4,80,640]{2,1,0:T(8,128)(2,1)S(1)}, u32[]{:S(2)}) copy-start(bf16[4,80,640]{2,1,0:T(8,128)(2,1)S(1)} %pad_maximum_fusion.mine) | copy-start | bytes 1228804
  95.8 4.5 %collective-permute-start.9 = (bf16[4,80,640]{2,1,0:T(8,128)(2,1)S(1)}, bf16[4,80,640]{2,1,0:T(8,128)(2,1)S(1)}, u32[]{:S(2)}, u32[]{:S(2)}) collective-permute-start(bf16[4,80,640]{2,1,0:T(8,128)(2,1)S(1)} %pad_maximum_fusion.mine), channel_id=1, source_target_pairs={{0,4},{4,0},{1,5},{5,1},{2,6},{6,2},{3,7},{7,3},{8,12},{12,8},{9,1... | collective-permute-start | bytes 1228808 | tf_op jit(solution)/shard_map/ppermute | solution.py:442
  100.2 0.7 copy-start.1
  117.2 8.9 %copy-start.4 = (bf16[80,384]{1,0:T(8,128)(2,1)S(1)}, bf16[80,384]{1,0:T(8,128)(2,1)}, u32[]{:S(2)}) copy-start(bf16[80,384]{1,0:T(8,128)(2,1)} %shard_map.79) | copy-start | bytes 184324
  117.2 7.5 %collective-permute-start.12 = (bf16[80,384]{1,0:T(8,128)(2,1)}, bf16[80,384]{1,0:T(8,128)(2,1)S(1)}, u32[]{:S(2)}, u32[]{:S(2)}) collective-permute-start(bf16[80,384]{1,0:T(8,128)(2,1)} %shard_map.79), channel_id=1, source_target_pairs={{0,3},{1,2},{2,1},{3,0},{4,7},{5,6},{6,5},{7,4},{8,11},{9,10},{10,... | collective-permute-start | bytes 184328 | tf_op jit(solution)/shard_map/ppermute | solution.py:446
  119.7 6.4 %collective-permute-start.11 = (bf16[80,384]{1,0:T(8,128)(2,1)}, bf16[80,384]{1,0:T(8,128)(2,1)S(1)}, u32[]{:S(2)}, u32[]{:S(2)}) collective-permute-start(bf16[80,384]{1,0:T(8,128)(2,1)} %shard_map.79), channel_id=1, source_target_pairs={{0,2},{1,3},{2,0},{3,1},{4,6},{5,7},{6,4},{7,5},{8,10},{9,11},{10,... | collective-permute-start | bytes 184328 | tf_op jit(solution)/shard_map/ppermute | solution.py:446
  119.7 6.4 %collective-permute-start.10 = (bf16[80,384]{1,0:T(8,128)(2,1)}, bf16[80,384]{1,0:T(8,128)(2,1)S(1)}, u32[]{:S(2)}, u32[]{:S(2)}) collective-permute-start(bf16[80,384]{1,0:T(8,128)(2,1)} %shard_map.79), channel_id=1, source_target_pairs={{0,1},{1,0},{2,3},{3,2},{4,5},{5,4},{6,7},{7,6},{8,9},{9,8},{10,11... | collective-permute-start | bytes 184328 | tf_op jit(solution)/shard_map/ppermute | solution.py:446
  123.3 7.6 %collective-permute-start.20 = (bf16[2,2,80,384]{3,2,1,0:T(8,128)(2,1)S(1)}, bf16[2,2,80,384]{3,2,1,0:T(8,128)(2,1)S(1)}, u32[]{:S(2)}, u32[]{:S(2)}) collective-permute-start(bf16[2,2,80,384]{3,2,1,0:T(8,128)(2,1)S(1)} %fusion), channel_id=1, source_target_pairs={{0,8},{8,0},{16,24},{24,16},{1,9},{9,1},{17,25},{25,17},{2,10},{10... | collective-permute-start | bytes 737288 | tf_op jit(solution)/shard_map/ppermute | solution.py:446
  126.1 16.9 %copy-start.2 = (bf16[4,80,384]{2,1,0:T(8,128)(2,1)}, bf16[4,80,384]{2,1,0:T(8,128)(2,1)S(1)}, u32[]{:S(2)}) copy-start(bf16[4,80,384]{2,1,0:T(8,128)(2,1)S(1)} %get-tuple-element.59.mine) | copy-start | bytes 737284
  126.1 4.7 %collective-permute-start.13 = (bf16[4,80,384]{2,1,0:T(8,128)(2,1)S(1)}, bf16[4,80,384]{2,1,0:T(8,128)(2,1)S(1)}, u32[]{:S(2)}, u32[]{:S(2)}) collective-permute-start(bf16[4,80,384]{2,1,0:T(8,128)(2,1)S(1)} %get-tuple-element.59.mine), channel_id=1, source_target_pairs={{0,4},{4,0},{1,5},{5,1},{2,6},{6,2},{3,7},{7,3},{8,12},{12,8},{9,1... | collective-permute-start | bytes 737288 | tf_op jit(solution)/shard_map/ppermute | solution.py:442
  126.2 14.1 %collective-permute-start.21 = (bf16[2,2,80,384]{3,2,1,0:T(8,128)(2,1)S(1)}, bf16[2,2,80,384]{3,2,1,0:T(8,128)(2,1)S(1)}, u32[]{:S(2)}, u32[]{:S(2)}) collective-permute-start(bf16[2,2,80,384]{3,2,1,0:T(8,128)(2,1)S(1)} %fusion), channel_id=1, source_target_pairs={{0,16},{8,24},{16,0},{24,8},{1,17},{9,25},{17,1},{25,9},{2,18},{10... | collective-permute-start | bytes 737288 | tf_op jit(solution)/shard_map/ppermute | solution.py:446
  127.7 14.1 %collective-permute-start.22 = (bf16[2,2,80,384]{3,2,1,0:T(8,128)(2,1)S(1)}, bf16[2,2,80,384]{3,2,1,0:T(8,128)(2,1)}, u32[]{:S(2)}, u32[]{:S(2)}) collective-permute-start(bf16[2,2,80,384]{3,2,1,0:T(8,128)(2,1)S(1)} %fusion), channel_id=1, source_target_pairs={{0,24},{8,16},{16,8},{24,0},{1,25},{9,17},{17,9},{25,1},{2,26},{10... | collective-permute-start | bytes 737288 | tf_op jit(solution)/shard_map/ppermute | solution.py:446
  130.8 12.2 %copy-start.9 = (bf16[2,2,80,384]{3,2,1,0:T(8,128)(2,1)}, bf16[2,2,80,384]{3,2,1,0:T(8,128)(2,1)S(1)}, u32[]{:S(2)}) copy-start(bf16[2,2,80,384]{3,2,1,0:T(8,128)(2,1)S(1)} %collective-permute-done.20.n1) | copy-start | bytes 737284
  130.8 11.0 %collective-permute-start.23 = (bf16[2,2,80,384]{3,2,1,0:T(8,128)(2,1)S(1)}, bf16[2,2,80,384]{3,2,1,0:T(8,128)(2,1)S(1)}, u32[]{:S(2)}, u32[]{:S(2)}) collective-permute-start(bf16[2,2,80,384]{3,2,1,0:T(8,128)(2,1)S(1)} %collective-permute-done.20.n1), channel_id=1, source_target_pairs={{0,4},{4,0},{1,5},{5,1},{2,6},{6,2},{3,7},{7,3},{8,12},{12,8},{9,1... | collective-permute-start | bytes 737288 | tf_op jit(solution)/shard_map/ppermute | solution.py:442
  130.8 12.2 %copy-start.3 = (bf16[4,80,384]{2,1,0:T(8,128)(2,1)}, bf16[4,80,384]{2,1,0:T(8,128)(2,1)S(1)}, u32[]{:S(2)}) copy-start(bf16[4,80,384]{2,1,0:T(8,128)(2,1)S(1)} %collective-permute-done.13.theirs) | copy-start | bytes 737284
  130.9 14.6 %collective-permute-start.14 = (bf16[2,2,80,384]{3,2,1,0:T(8,128)(2,1)S(1)}, bf16[2,2,80,384]{3,2,1,0:T(8,128)(2,1)}, u32[]{:S(2)}, u32[]{:S(2)}) collective-permute-start(bf16[2,2,80,384]{3,2,1,0:T(8,128)(2,1)S(1)} %fusion.1), channel_id=1, source_target_pairs={{0,8},{8,0},{16,24},{24,16},{1,9},{9,1},{17,25},{25,17},{2,10},{10... | collective-permute-start | bytes 737288 | tf_op jit(solution)/shard_map/ppermute | solution.py:446
  132.3 18.2 %collective-permute-start.15 = (bf16[2,2,80,384]{3,2,1,0:T(8,128)(2,1)S(1)}, bf16[2,2,80,384]{3,2,1,0:T(8,128)(2,1)}, u32[]{:S(2)}, u32[]{:S(2)}) collective-permute-start(bf16[2,2,80,384]{3,2,1,0:T(8,128)(2,1)S(1)} %fusion.1), channel_id=1, source_target_pairs={{0,16},{8,24},{16,0},{24,8},{1,17},{9,25},{17,1},{25,9},{2,18},{10... | collective-permute-start | bytes 737288 | tf_op jit(solution)/shard_map/ppermute | solution.py:446
  140.3 4.6 %copy-start.10 = (bf16[2,2,80,384]{3,2,1,0:T(8,128)(2,1)}, bf16[2,2,80,384]{3,2,1,0:T(8,128)(2,1)S(1)}, u32[]{:S(2)}) copy-start(bf16[2,2,80,384]{3,2,1,0:T(8,128)(2,1)S(1)} %collective-permute-done.21.n2) | copy-start | bytes 737284
  140.3 10.2 %collective-permute-start.16 = (bf16[2,2,80,384]{3,2,1,0:T(8,128)(2,1)S(1)}, bf16[2,2,80,384]{3,2,1,0:T(8,128)(2,1)}, u32[]{:S(2)}, u32[]{:S(2)}) collective-permute-start(bf16[2,2,80,384]{3,2,1,0:T(8,128)(2,1)S(1)} %fusion.1), channel_id=1, source_target_pairs={{0,24},{8,16},{16,8},{24,0},{1,25},{9,17},{17,9},{25,1},{2,26},{10... | collective-permute-start | bytes 737288 | tf_op jit(solution)/shard_map/ppermute | solution.py:446
  141.8 9.2 %collective-permute-start.24 = (bf16[2,2,80,384]{3,2,1,0:T(8,128)(2,1)S(1)}, bf16[2,2,80,384]{3,2,1,0:T(8,128)(2,1)}, u32[]{:S(2)}, u32[]{:S(2)}) collective-permute-start(bf16[2,2,80,384]{3,2,1,0:T(8,128)(2,1)S(1)} %collective-permute-done.21.n2), channel_id=1, source_target_pairs={{0,4},{4,0},{1,5},{5,1},{2,6},{6,2},{3,7},{7,3},{8,12},{12,8},{9,1... | collective-permute-start | bytes 737288 | tf_op jit(solution)/shard_map/ppermute | solution.py:442
  141.8 0.7 copy-start.11
  141.8 9.2 %collective-permute-start.25 = (bf16[2,2,80,384]{3,2,1,0:T(8,128)(2,1)}, bf16[2,2,80,384]{3,2,1,0:T(8,128)(2,1)}, u32[]{:S(2)}, u32[]{:S(2)}) collective-permute-start(bf16[2,2,80,384]{3,2,1,0:T(8,128)(2,1)} %collective-permute-done.22.n3), channel_id=1, source_target_pairs={{0,4},{4,0},{1,5},{5,1},{2,6},{6,2},{3,7},{7,3},{8,12},{12,8},{9,1... | collective-permute-start | bytes 737288 | tf_op jit(solution)/shard_map/ppermute | solution.py:442
  143.1 1.8 %copy-start.8 = (bf16[80,384]{1,0:T(8,128)(2,1)S(1)}, bf16[80,384]{1,0:T(8,128)(2,1)}, u32[]{:S(2)}) copy-start(bf16[80,384]{1,0:T(8,128)(2,1)} %get-tuple-element.29) | copy-start | bytes 184324
  145.5 13.9 %collective-permute-start.17 = (bf16[2,2,80,384]{3,2,1,0:T(8,128)(2,1)}, bf16[2,2,80,384]{3,2,1,0:T(8,128)(2,1)S(1)}, u32[]{:S(2)}, u32[]{:S(2)}) collective-permute-start(bf16[2,2,80,384]{3,2,1,0:T(8,128)(2,1)} %collective-permute-done.14.n1), channel_id=1, source_target_pairs={{0,4},{4,0},{1,5},{5,1},{2,6},{6,2},{3,7},{7,3},{8,12},{12,8},{9,1... | collective-permute-start | bytes 737288 | tf_op jit(solution)/shard_map/ppermute | solution.py:442
  150.5 8.9 %collective-permute-start.18 = (bf16[2,2,80,384]{3,2,1,0:T(8,128)(2,1)}, bf16[2,2,80,384]{3,2,1,0:T(8,128)(2,1)S(1)}, u32[]{:S(2)}, u32[]{:S(2)}) collective-permute-start(bf16[2,2,80,384]{3,2,1,0:T(8,128)(2,1)} %collective-permute-done.15.n2), channel_id=1, source_target_pairs={{0,4},{4,0},{1,5},{5,1},{2,6},{6,2},{3,7},{7,3},{8,12},{12,8},{9,1... | collective-permute-start | bytes 737288 | tf_op jit(solution)/shard_map/ppermute | solution.py:442
  150.5 9.0 %collective-permute-start.19 = (bf16[2,2,80,384]{3,2,1,0:T(8,128)(2,1)}, bf16[2,2,80,384]{3,2,1,0:T(8,128)(2,1)S(1)}, u32[]{:S(2)}, u32[]{:S(2)}) collective-permute-start(bf16[2,2,80,384]{3,2,1,0:T(8,128)(2,1)} %collective-permute-done.16.n3), channel_id=1, source_target_pairs={{0,4},{4,0},{1,5},{5,1},{2,6},{6,2},{3,7},{7,3},{8,12},{12,8},{9,1... | collective-permute-start | bytes 737288 | tf_op jit(solution)/shard_map/ppermute | solution.py:442
  159.4 0.7 copy-start.12
  159.4 0.8 copy-start.13
  160.2 0.7 copy-start.14

commit v2 on v0

--- a/solution.py
+++ b/solution.py
@@ -1,6 +1,11 @@
+import functools
+
 import jax
 import jax.numpy as jnp
+import numpy as np
 from jax import lax
+from jax.experimental import pallas as pl
+from jax.experimental.pallas import tpu as pltpu
 from jax.sharding import PartitionSpec as P
 
 C = 320
@@ -8,6 +13,7 @@
 
 
 EPSILON = 1e-05
+LINK = jnp.bfloat16
 
 
 def with_halo(cells, sides, width):
@@ -121,7 +127,7 @@
     return lax.psum(weight_grad, ("frame", "row"))
 
 
-def shards(activations, conv_first, conv_second, cotangent):
+def shards_general(activations, conv_first, conv_second, cotangent):
     layout = activations.shape
     channels_local = layout[0]
     first_sum, first_patches = forward_conv(activations, conv_first)
@@ -153,9 +159,446 @@
     return (result, input_grad, first_total, second_total)
 
 
+BF16 = jnp.bfloat16
+F32 = jnp.float32
+LANES = 128
+HIGH = lax.Precision.HIGHEST
+SIDES = [(slot, side) for slot in range(4) for side in range(2)]
+
+
+def call(kernel, outs, args, scratch=(), grid=None, specs=None, flops=0, reads=0, grant=16, after=()):
+    vmem = pl.BlockSpec(memory_space=pltpu.VMEM)
+    in_specs = [pl.BlockSpec(memory_space=pltpu.SMEM)] + [vmem] * (len(args) - 1)
+    if after:
+        inner, taken = kernel, len(args)
+        kernel = lambda *refs: inner(*refs[:taken], *refs[taken + len(after) :])
+        in_specs += [pl.BlockSpec(memory_space=pl.ANY)] * len(after)
+        args = (*args, *after)
+    params = dict(vmem_limit_bytes=grant * 1024 * 1024)
+    if grid is not None:
+        params["dimension_semantics"] = ("arbitrary",) * len(grid)
+    extra = {} if grid is None else {"grid": grid}
+    return pl.pallas_call(
+        kernel,
+        out_shape=outs,
+        in_specs=in_specs,
+        out_specs=[vmem] * len(outs) if specs is None else specs,
+        scratch_shapes=list(scratch),
+        compiler_params=pltpu.CompilerParams(**params),
+        cost_estimate=pl.CostEstimate(flops=flops, bytes_accessed=reads, transcendentals=0),
+        **extra,
+    )(*args)
+
+
+def shift(block, step):
+    if step == 1:
+        return block
+    lane = lax.broadcasted_iota(jnp.int32, block.shape, 1)
+    if step == 0:
+        moved = pltpu.roll(block, 1, 1)
+        return jnp.where(lane == 0, jnp.zeros_like(moved), moved)
+    moved = pltpu.roll(block, block.shape[1] - 1, 1)
+    return jnp.where(lane == block.shape[1] - 1, jnp.zeros_like(moved), moved)
+
+
+def fill_shifted(shifted, block, channels, frames, mirrored, base=0, stride=None):
+    stride = channels if stride is None else stride
+    for place in range(frames + 2):
+        for side in range(2):
+            cells = block(place, side)
+            for tap_col in range(3):
+                start = (side * 3 + tap_col) * stride + base
+                if not isinstance(start, int):
+                    start = pl.multiple_of(start, 16)
+                lanes = pl.ds(place * LANES, LANES)
+                shifted[pl.ds(start, channels), lanes] = shift(cells, 2 - tap_col if mirrored else tap_col)
+
+
+def neighbour_block(pieces, place, side, frames, where):
+    my_frame = where[0]
+    if place == 0:
+        cells = jnp.where(my_frame == 2, pieces(3, side, frames - 1), pieces(1, side, frames - 1))
+        return jnp.where(my_frame > 0, cells, jnp.zeros_like(cells))
+    if place == frames + 1:
+        cells = jnp.where(my_frame == 1, pieces(3, side, 0), pieces(1, side, 0))
+        return jnp.where(my_frame < 3, cells, jnp.zeros_like(cells))
+    return pieces(0, side, place - 1)
+
+
+def pick(refs):
+    return lambda slot, side, frame: refs[2 * slot + side][frame]
+
+
+def other_tap(where, mirrored):
+    return 2 * where[1] if mirrored else 2 - 2 * where[1]
+
+
+def prepare_kernel(where, first, second, behind_first, behind_second):
+    for weight, behind in ((first, behind_first), (second, behind_second)):
+        for tap_frame in range(3):
+            for side in range(2):
+                row = other_tap(where, True) if side else 1
+                taps = [weight[9 * tap_frame + 3 * row + tap_col] for tap_col in range(3)]
+                behind[tap_frame * 2 + side] = jnp.concatenate(taps, axis=1)
+
+
+def forward_product(where, weight, shifted, parts, scratch, frames):
+    channels, wide = weight.shape[1:]
+    out = None
+    for tap_frame in range(3):
+        for side in range(2):
+            row = other_tap(where, False) if side else 1
+            taps = weight[pl.ds(9 * tap_frame + 3 * row, 3)].reshape(3 * channels, wide)
+            window = shifted[
+                pl.ds(side * 3 * channels, 3 * channels), pl.ds(tap_frame * LANES, frames * LANES)
+            ]
+            term = lax.dot_general(
+                taps, window, (((0,), (0,)), ((), ())), preferred_element_type=F32
+            )
+            out = term if out is None else out + term
+    scratch[...] = out
+    for slot in range(4):
+        owner = jnp.bitwise_xor(where[2], slot)
+        rows = pl.ds(pl.multiple_of(owner * channels, 16), channels)
+        for frame in range(frames):
+            cells = scratch[rows, pl.ds(frame * LANES, LANES)]
+            parts[slot][frame] = cells.astype(parts[slot].dtype)
+
+
+def group_total(mixer, sums):
+    wide = jnp.broadcast_to(sums, (sums.shape[0], LANES))
+    return jnp.dot(mixer, wide, precision=HIGH, preferred_element_type=F32)
+
+
+def first_kernel(frames, where, weight, *rest):
+    pieces, parts, (shifted, total) = rest[:8], rest[8:12], rest[12:]
+    block = lambda place, side: neighbour_block(pick(pieces), place, side, frames, where)
+    fill_shifted(shifted, block, weight.shape[1], frames, False)
+    forward_product(where, weight, shifted, parts, total, frames)
+
+
+def statistics(sums, mixer, members):
+    acc = None
+    for block in sums:
+        for frame in range(block.shape[0]):
+            acc = block[frame] if acc is None else acc + block[frame]
+    mean = group_total(mixer, jnp.sum(acc, axis=1, keepdims=True))[:, :1] / members
+    acc = None
+    for block in sums:
+        for frame in range(block.shape[0]):
+            centered = block[frame] - mean
+            acc = centered * centered if acc is None else acc + centered * centered
+    variance = group_total(mixer, jnp.sum(acc, axis=1, keepdims=True))[:, :1] / members
+    return mean, lax.rsqrt(variance + EPSILON)
+
+
+def second_kernel(frames, members, where, weight, mixer, *rest):
+    sums, (hidden, norm, scale), parts, (shifted, total) = rest[:8], rest[8:11], rest[11:15], rest[15:]
+    mean, inv = statistics(sums, mixer[...], members)
+    for slot, side in SIDES:
+        for frame in range(frames):
+            normed = (sums[2 * slot + side][frame] - mean) * inv
+            hidden[slot, side, frame] = (normed * jax.nn.sigmoid(normed)).astype(BF16)
+            if slot == 0 and side == 0:
+                norm[frame] = normed
+    lane = lax.broadcasted_iota(jnp.int32, scale.shape, 1)
+    scale[...] = jnp.where(lane == 0, mean, inv)
+    at = lambda slot, side, frame: hidden[slot, side, frame]
+    block = lambda place, side: neighbour_block(at, place, side, frames, where)
+    fill_shifted(shifted, block, mixer.shape[0], frames, False)
+    forward_product(where, weight, shifted, parts, total, frames)
+
+
+def third_kernel(frames, members, where, mixer, *rest):
+    sums, given, own, (result, halo, every, grads, norms) = rest[:8], rest[8:16], rest[16], rest[17:]
+    mean, inv = statistics(sums, mixer[...], members)
+    first = second = None
+    for slot, side in SIDES:
+        for frame in range(frames):
+            normed = (sums[2 * slot + side][frame] - mean) * inv
+            gate = jax.nn.sigmoid(normed)
+            grad = given[2 * slot + side][frame].astype(F32) * gate * (1.0 + normed * (1.0 - gate))
+            first = grad if first is None else first + grad
+            second = grad * normed if second is None else second + grad * normed
+            norms[slot, side, frame] = normed
+            grads[slot, side, frame] = grad
+            if slot == 0 and side == 0:
+                result[frame] = (own[frame].astype(F32) + normed * gate).astype(BF16)
+    first = group_total(mixer[...], jnp.sum(first, axis=1, keepdims=True))[:, :1] / members
+    second = group_total(mixer[...], jnp.sum(second, axis=1, keepdims=True))[:, :1] / members
+    for slot, side in SIDES:
+        for frame in range(frames):
+            cells = grads[slot, side, frame] - first - norms[slot, side, frame] * second
+            every[slot, side, frame] = (cells * inv).astype(BF16)
+    ready = lambda slot, side, frame: every[slot, side, frame]
+    for place in range(frames + 2):
+        halo[place] = neighbour_block(ready, place, 0, frames, where)
+
+
+def fourth_kernel(frames, where, weight, norm, *rest):
+    halos, (grad, shifted) = rest[:8], rest[8:]
+    channels = norm.shape[1]
+    for part in range(4):
+        owner = jnp.bitwise_xor(where[2], part)
+        block = lambda place, side: halos[2 * part + side][place]
+        fill_shifted(shifted, block, channels, frames, True, owner * channels, 4 * channels)
+    out = back_product(weight, shifted, frames)
+    for frame in range(frames):
+        normed = norm[frame]
+        gate = jax.nn.sigmoid(normed)
+        cells = out[:, frame * LANES : (frame + 1) * LANES]
+        grad[frame] = cells * gate * (1.0 + normed * (1.0 - gate))
+
+
+def back_product(weight, shifted, frames):
+    depth = weight.shape[2]
+    out = None
+    for tap_frame in range(3):
+        for side in range(2):
+            window = shifted[
+                pl.ds(side * depth, depth), pl.ds((2 - tap_frame) * LANES, frames * LANES)
+            ]
+            term = jnp.dot(weight[tap_frame * 2 + side], window, preferred_element_type=F32)
+            out = term if out is None else out + term
+    return out
+
+
+def fifth_kernel(frames, members, where, mixer, scale, *rest):
+    sums, grads, (out, every) = rest[:8], rest[8:16], rest[16:]
+    mean, inv = scale[:, :1], scale[:, 1:2]
+    norm = lambda slot, side, frame: (sums[2 * slot + side][frame] - mean) * inv
+    first = second = None
+    for slot, side in SIDES:
+        for frame in range(frames):
+            cells = grads[2 * slot + side][frame]
+            first = cells if first is None else first + cells
+            term = cells * norm(slot, side, frame)
+            second = term if second is None else second + term
+    first = group_total(mixer[...], jnp.sum(first, axis=1, keepdims=True))[:, :1] / members
+    second = group_total(mixer[...], jnp.sum(second, axis=1, keepdims=True))[:, :1] / members
+    for slot, side in SIDES:
+        for frame in range(frames):
+            cells = grads[2 * slot + side][frame] - first - norm(slot, side, frame) * second
+            cells = (cells * inv).astype(BF16)
+            every[slot, side, frame] = cells
+            if slot == 0 and side == 0:
+                out[frame] = cells
+
+
+def pad_kernel(frames, where, *rest):
+    pieces, padded = rest[:8], rest[8]
+    fill_padded(padded, pick(pieces), frames, where, pieces[0].shape[1])
+
+
+def lanes_of(where, slot, frames, frame):
+    start = jnp.bitwise_xor(where[0], slot) * frames + frame
+    return pl.ds(pl.multiple_of(start * LANES, LANES), LANES)
+
+
+def fill_padded(padded, inputs, frames, where, channels):
+    zeros = jnp.zeros((padded.shape[0], LANES), padded.dtype)
+    padded[:, pl.ds(0, LANES)] = zeros
+    padded[:, pl.ds(padded.shape[1] - LANES, LANES)] = zeros
+    for slot, side in SIDES:
+        for frame in range(frames):
+            cells = inputs(slot, side, frame)
+            for tap_col in range(3):
+                rows = pl.ds((side * 3 + tap_col) * channels, channels)
+                padded[rows, lanes_of(where, slot, frames, frame + 1)] = shift(cells, tap_col)
+
+
+def weight_step(grads, frames, where, channels, out, padded, full, prologue):
+    tap_frame = pl.program_id(0)
+    under_rows = -(-4 * channels // LANES) * LANES
+
+    @pl.when(tap_frame == 0)
+    def _():
+        prologue()
+        gap = under_rows - 4 * channels
+        full[pl.ds(4 * channels, gap), :] = jnp.zeros((gap, full.shape[1]), full.dtype)
+        for slot, side in SIDES:
+            for frame in range(frames):
+                for part in range(4):
+                    owner = jnp.bitwise_xor(where[2], part)
+                    rows = pl.ds(pl.multiple_of(side * under_rows + owner * channels, 16), channels)
+                    full[rows, lanes_of(where, slot, frames, frame)] = grads(slot, side, part, frame)
+
+    window = padded[:, pl.ds(pl.multiple_of(tap_frame * LANES, LANES), full.shape[1])]
+    both = lax.dot_general(window, full[...], (((1,), (1,)), ((), ())), preferred_element_type=F32)
+    mine, theirs = both[:, : 4 * channels], both[:, under_rows:]
+    for tap_col in range(3):
+        upper = slice(tap_col * channels, (tap_col + 1) * channels)
+        under = slice((3 + tap_col) * channels, (4 + tap_col) * channels)
+        out[3 + tap_col] = mine[upper] + theirs[under]
+        out[3 * other_tap(where, False) + tap_col] = mine[under]
+        out[3 * other_tap(where, True) + tap_col] = theirs[upper]
+
+
+def weight_kernel(frames, where, hidden, every, *rest):
+    own, far, (out, padded, full) = rest[:6], rest[6:12], rest[12:]
+    channels = hidden.shape[3]
+
+    def grads(slot, side, part, frame):
+        if part == 0:
+            return every[slot, side, frame]
+        if slot == 0:
+            return own[2 * (part - 1) + side][frame + 1]
+        return far[2 * (slot - 1) + side][part - 1, frame]
+
+    inputs = lambda slot, side, frame: hidden[slot, side, frame]
+    prologue = lambda: fill_padded(padded, inputs, frames, where, channels)
+    weight_step(grads, frames, where, channels, out, padded, full, prologue)
+
+
+def last_kernel(frames, where, weight, cotangent, padded, every, *rest):
+    far, (out, back, full, shifted) = rest[:8], rest[8:]
+    channels = weight.shape[1]
+
+    def grads(slot, side, part, frame):
+        if part == 0:
+            return every[slot, side, frame]
+        return far[2 * slot + side][part - 1, frame]
+
+    def prologue():
+        for part in range(4):
+            pieces = lambda slot, side, frame: grads(slot, side, part, frame)
+            block = lambda place, side: neighbour_block(pieces, place, side, frames, where)
+            owner = jnp.bitwise_xor(where[2], part)
+            fill_shifted(shifted, block, channels, frames, True, owner * channels, 4 * channels)
+        grown = back_product(weight, shifted, frames)
+        for frame in range(frames):
+            cells = cotangent[frame].astype(F32) + grown[:, frame * LANES : (frame + 1) * LANES]
+            back[frame] = cells.astype(BF16)
+
+    weight_step(grads, frames, where, channels, out, padded, full, prologue)
+
+
+def swap(values):
+    return lax.ppermute(values, "row", [(0, 1), (1, 0)])
+
+
+def hop(values, axis, step):
+    return lax.ppermute(values, axis, [(i, i ^ step) for i in range(4)])
+
+
+def over_channels(parts):
+    return parts[0] + sum(hop(parts[k], "chan", k).astype(F32) for k in range(1, 4))
+
+
+def hops(values):
+    return [hop(values, "frame", k) for k in range(1, 4)]
+
+
+def with_sides(pieces):
+    return [values for piece in pieces for values in (piece, swap(piece))]
+
+
+def around(values):
+    return with_sides([values] + hops(values))
+
+
+def shards_paired(activations, conv_first, conv_second, cotangent):
+    channels, frames = activations.shape[:2]
+    cells = frames * LANES
+    count = lax.axis_size("frame")
+    wide = 4 * channels
+    members = (C // GROUPS) * cells * count * 2
+    my_frame, my_row, place = (lax.axis_index(a) for a in ("frame", "row", "chan"))
+    where = jnp.stack([my_frame, my_row, place]).astype(jnp.int32)
+    group = np.arange(channels) // (C // GROUPS)
+    mixer = jnp.asarray((group[:, None] == group[None, :]).astype(np.float32))
+    conv_cost = dict(flops=2 * channels * wide * 18 * cells, reads=18 * channels * wide * 2)
+
+    block = (frames, channels, LANES)
+    sums_shape = jax.ShapeDtypeStruct(block, F32)
+    cells_shape = jax.ShapeDtypeStruct(block, BF16)
+    parts_shape = [sums_shape] + [jax.ShapeDtypeStruct(block, LINK)] * 3
+    span = (frames + 2) * LANES
+    shifted = pltpu.VMEM((6 * channels, span), BF16)
+    wide_shifted = pltpu.VMEM((6 * wide, span), BF16)
+    total = pltpu.VMEM((wide, cells), F32)
+
+    by_frame = lambda values: values.transpose(1, 2, 0, 3).reshape(block)
+    restore = lambda values: values.reshape(frames, 1, channels, LANES).transpose(2, 0, 1, 3)
+    inputs, given = by_frame(activations), by_frame(cotangent)
+    behind_shape = jax.ShapeDtypeStruct((6, channels, 3 * wide), BF16)
+    prepared = call(
+        prepare_kernel, [behind_shape, behind_shape], (where, conv_first, conv_second), reads=6000000
+    )
+    near, (behind_first, behind_second) = lax.optimization_barrier((hops(inputs), prepared))
+    every_input = with_sides([inputs] + near)
+    parts = call(
+        functools.partial(first_kernel, frames), parts_shape,
+        (where, conv_first, *every_input), (shifted, total), **conv_cost,
+    )
+    given, parts = lax.optimization_barrier((given, parts))
+    near, sums = lax.optimization_barrier((hops(given), over_channels(parts)))
+    every_given = with_sides([given] + near)
+    first_sums = around(sums)
+    hidden, norm, scale, *parts = call(
+        functools.partial(second_kernel, frames, members),
+        [
+            jax.ShapeDtypeStruct((count, 2, *block), BF16),
+            sums_shape,
+            jax.ShapeDtypeStruct((channels, LANES), F32),
+            *parts_shape,
+        ],
+        (where, conv_second, mixer, *first_sums), (shifted, total), **conv_cost,
+    )
+    second_sums = around(over_channels(parts))
+    every_shape = jax.ShapeDtypeStruct((count, 2, *block), BF16)
+    result, halo, every_second = call(
+        functools.partial(third_kernel, frames, members),
+        [cells_shape, jax.ShapeDtypeStruct((frames + 2, channels, LANES), BF16), every_shape],
+        (where, mixer, *second_sums, *every_given, inputs),
+        (pltpu.VMEM((4, 2, *block), F32), pltpu.VMEM((4, 2, *block), F32)), grant=24,
+    )
+    halos = [halo] + [hop(halo, "chan", k) for k in range(1, 4)]
+    sides = with_sides(halos)
+    (grad,) = call(
+        functools.partial(fourth_kernel, frames), [sums_shape],
+        (where, behind_second, norm, *sides), (wide_shifted,), **conv_cost,
+    )
+    grad_first, every_first = call(
+        functools.partial(fifth_kernel, frames, members), [cells_shape, every_shape],
+        (where, mixer, scale, *first_sums, *around(grad)),
+    )
+    rest = jnp.stack([values[1:-1] for values in halos[1:]])
+    rest, grad_first = lax.optimization_barrier((rest, grad_first))
+    padded_shape = jax.ShapeDtypeStruct((6 * channels, (frames * count + 2) * LANES), BF16)
+    padded = pltpu.VMEM(padded_shape.shape, BF16)
+    full = pltpu.VMEM((-(-wide // LANES) * LANES + wide, cells * count), BF16)
+    grad_shape = jax.ShapeDtypeStruct((27, channels, wide), F32)
+    grad_spec = pl.BlockSpec((9, channels, wide), lambda a: (a, 0, 0))
+    grad_cost = dict(flops=2 * 18 * channels * wide * cells * count * 2, reads=8000000)
+    (second_grad,) = call(
+        functools.partial(weight_kernel, frames), [grad_shape],
+        (where, hidden, every_second, *sides[2:], *with_sides(hops(rest))), (padded, full),
+        grid=(3,), specs=[grad_spec], grant=32, **grad_cost,
+    )
+    (padded_inputs,) = call(
+        functools.partial(pad_kernel, frames), [padded_shape], (where, *every_input), reads=2000000
+    )
+    rest = jnp.stack([hop(grad_first, "chan", k) for k in range(1, 4)])
+    near, (second_grad, padded_inputs) = lax.optimization_barrier(
+        (hops(rest), (second_grad, padded_inputs))
+    )
+    first_grad, input_grad = call(
+        functools.partial(last_kernel, frames), [grad_shape, cells_shape],
+        (where, behind_first, given, padded_inputs, every_first, *with_sides([rest] + near)),
+        (full, wide_shifted), grid=(3,),
+        specs=[grad_spec, pl.BlockSpec(block, lambda a: (0, 0, 0))], grant=32, **grad_cost,
+    )
+    return (restore(result), restore(input_grad), first_grad, second_grad)
+
+
+def paired(mesh):
+    return mesh.shape["frame"] == 4 and mesh.shape["row"] == 2 and mesh.shape["chan"] == 4
+
+
 def solution(mesh):
     return jax.shard_map(
-        shards,
+        shards_paired if paired(mesh) else shards_general,
         mesh=mesh,
         in_specs=(
             P("chan", "frame", "row", None),

time: 796 us -> 126 us (0.16); the launches traced: 781 us -> 126 us
  local copies, waits for them, and re-layouts: 385 us -> 2.92 us
  waiting for transfers between devices: 210 us -> 47 us
  blocking collectives: 73.3 us -> 0 us
  Pallas kernels: 0 us -> 25.3 us
  matrix products: 24.4 us -> 0 us
  other arithmetic: 18.7 us -> 0.19 us
  between operations: 14.9 us -> 0.85 us
    another operation x111 -> x3, local copies, waits for them, and re-layouts: 139 us -> 0.02 us  [shards_paired(): rest = jnp.stack([values[1:-1] for values in halos[1:]])]
    slice x94 -> x0, local copies, waits for them, and re-layouts: 131 us -> none  [the longest x90 130 us: collect(): padded[:, anchor[0]:anchor[0] + frames, anchor[1]:anchor[1] + height, anc...]
    unnamed x259 -> x12, local copies, waits for them, and re-layouts: 111 us -> 2.9 us
    psum x1 -> x0, waiting for transfers between devices: 87.7 us -> none  [reduce_weights(): return lax.psum(weight_grad, ('frame', 'row'))]
    psum x6 -> x0, blocking collectives: 73.3 us -> none  [the longest x2 25.4 us: norm_back(): lax.psum((jnp.sum(grouped_grad, axis=1), jnp.sum(grouped_grad * grouped_n...]
    all_gather x2 -> x0, waiting for transfers between devices: 68 us -> none  [back_conv(): portion = lax.all_gather(rimmed, 'chan', axis=0, tiled=True)]
    reduce_scatter x2 -> x0, waiting for transfers between devices: 42.7 us -> none  [forward_conv(): lax.psum_scatter(lax.dot_general(flat_weight, flat_own, (((0,), (0,)), ((...]
    ppermute x16 -> x64, waiting for transfers between devices: 11.3 us -> 47 us  [the longest x33 39.7 us: hop(): return lax.ppermute(values, axis, [(i, i ^ step) for i in range(4)])]
  transfers between devices with their start and end apart: 21 -> 64, of which waited for: 12 -> 34; matrix products, arithmetic and copies ran while one was open for 4% -> 0% of each run, Pallas kernels for 0% -> 6%
where the time goes in v2:
time: 126 us
  starting transfers between devices  49.9 us (40%)
  waiting for transfers between devices  47 us (37%)
  Pallas kernels  25.3 us (20%)
  local copies, waits for them, and re-layouts  2.92 us (2%)
    ppermute x33, starting transfers between devices, hop(): return lax.ppermute(values, axis, [(i, i ^ step) for i in range(4)])  45 us
    ppermute x33, waiting for transfers between devices, hop(): return lax.ppermute(values, axis, [(i, i ^ step) for i in range(4)])  39.7 us
    pallas_call x9, Pallas kernels, call(): pl.pallas_call(kernel, out_shape=outs, in_specs=in_specs, out_specs=[vmem...  25.3 us
    ppermute x31, waiting for transfers between devices, swap(): return lax.ppermute(values, 'row', [(0, 1), (1, 0)])  7.3 us
    ppermute x31, starting transfers between devices, swap(): return lax.ppermute(values, 'row', [(0, 1), (1, 0)])  4.96 us
    unnamed x12, local copies, waits for them, and re-layouts  2.9 us
  transfers between devices with their start and end apart: 64, of which 34 were waited for; matrix products, arithmetic and copies ran while one was open for 0% of the time, Pallas kernels for 6%

profile of v2, /device:TPU:0, one launch (start us, length us, event | category | flops | bytes accessed | tf_op | source)
XLA Modules:
  0.0 126.2 jit_solution(7805599565666412417)
XLA Ops:
  0.6 4.0 %collective-permute-start.3 = (bf16[3,80,128]{2,1,0:T(8,128)(2,1)}, bf16[3,80,128]{2,1,0:T(8,128)(2,1)S(1)}, u32[]{:S(2)}, u32[]{:S(2)}) collective-permute-start(bf16[3,80,128]{2,1,0:T(8,128)(2,1)} %bitcast.32), channel_id=1, source_target_pairs={{0,24},{8,16},{16,8},{24,0},{1,25},{9,17},{17,9},{25,1},{2,26},{10... | collective-permute-start | bytes 184328 | tf_op jit(solution)/shard_map/ppermute | solution.py:481
  5.3 1.4 %copy-done = bf16[27,80,320]{2,1,0:T(8,128)(2,1)S(1)} copy-done((bf16[27,80,320]{2,1,0:T(8,128)(2,1)S(1)}, bf16[27,80,320]{2,1,0:T(8,128)(2,1)}, u32[]{:S(2)}) %copy-start) | copy-done | bytes 1382424
  6.8 1.4 %copy-done.1 = bf16[27,80,320]{2,1,0:T(8,128)(2,1)S(1)} copy-done((bf16[27,80,320]{2,1,0:T(8,128)(2,1)S(1)}, bf16[27,80,320]{2,1,0:T(8,128)(2,1)}, u32[]{:S(2)}) %copy-start.1) | copy-done | bytes 1382424
  11.3 1.4 %shard_map.85 = (f32[3,80,128]{2,1,0:T(8,128)S(1)}, bf16[3,80,128]{2,1,0:T(8,128)(2,1)S(1)}, bf16[3,80,128]{2,1,0:T(8,128)(2,1)S(1)}, bf16[3,80,128]{2,1,0:T(8,128)(2,1)S(1)}) custom-call(s32[3]{0:T(128)S(1)} %pad_add_fusion.where, bf16[27,80,320]{2,1,0:T(8,128)(2,1)S(1)} %copy-done, bf16[3,80,128]{2,1,0:T(8,128)(2,1)S(1)} %bitcast.36, ...), custom_call_target="tpu_custom_call" | custom-call | flops 353894400 | bytes 921600 | tf_op jit(solution)/shard_map/pallas_call | solution.py:181
  12.7 1.9 %collective-permute-start.10 = (bf16[3,80,128]{2,1,0:T(8,128)(2,1)S(1)}, bf16[3,80,128]{2,1,0:T(8,128)(2,1)S(1)}, u32[]{:S(2)}, u32[]{:S(2)}) collective-permute-start(bf16[3,80,128]{2,1,0:T(8,128)(2,1)S(1)} %get-tuple-element.56), channel_id=1, source_target_pairs={{0,1},{1,0},{2,3},{3,2},{4,5},{5,4},{6,7},{7,6},{8,9},{9,8},{10,11... | collective-permute-start | bytes 184328 | tf_op jit(solution)/shard_map/ppermute | solution.py:481
  14.6 2.6 %collective-permute-start.11 = (bf16[3,80,128]{2,1,0:T(8,128)(2,1)S(1)}, bf16[3,80,128]{2,1,0:T(8,128)(2,1)S(1)}, u32[]{:S(2)}, u32[]{:S(2)}) collective-permute-start(bf16[3,80,128]{2,1,0:T(8,128)(2,1)S(1)} %get-tuple-element.57), channel_id=1, source_target_pairs={{0,2},{1,3},{2,0},{3,1},{4,6},{5,7},{6,4},{7,5},{8,10},{9,11},{10,... | collective-permute-start | bytes 184328 | tf_op jit(solution)/shard_map/ppermute | solution.py:481
  17.2 2.7 %collective-permute-start.9 = (bf16[3,80,128]{2,1,0:T(8,128)(2,1)S(1)}, bf16[3,80,128]{2,1,0:T(8,128)(2,1)S(1)}, u32[]{:S(2)}, u32[]{:S(2)}) collective-permute-start(bf16[3,80,128]{2,1,0:T(8,128)(2,1)S(1)} %bitcast.39), channel_id=1, source_target_pairs={{0,24},{8,16},{16,8},{24,0},{1,25},{9,17},{17,9},{25,1},{2,26},{10... | collective-permute-start | bytes 184328 | tf_op jit(solution)/shard_map/ppermute | solution.py:481
  21.3 1.9 %collective-permute-done.12 = bf16[3,80,128]{2,1,0:T(8,128)(2,1)S(1)} collective-permute-done((bf16[3,80,128]{2,1,0:T(8,128)(2,1)S(1)}, bf16[3,80,128]{2,1,0:T(8,128)(2,1)S(1)}, u32[]{:S(2)}, u32[]{:S(2)}) %collective-permute-start.12) | collective-permute-done | bytes 61472 | tf_op jit(solution)/shard_map/ppermute | solution.py:481
  24.6 1.5 %collective-permute-start.18 = (f32[3,80,128]{2,1,0:T(8,128)S(1)}, f32[3,80,128]{2,1,0:T(8,128)S(1)}, u32[]{:S(2)}, u32[]{:S(2)}) collective-permute-start(f32[3,80,128]{2,1,0:T(8,128)S(1)} %add_add_fusion.1.rest_0_), channel_id=1, source_target_pairs={{0,24},{8,16},{16,8},{24,0},{1,25},{9,17},{17,9},{25,1},{2,26},{10... | collective-permute-start | bytes 368648 | tf_op jit(solution)/shard_map/ppermute | solution.py:481
  26.4 1.7 %collective-permute-start.14 = (f32[3,80,128]{2,1,0:T(8,128)S(1)}, f32[3,80,128]{2,1,0:T(8,128)S(1)}, u32[]{:S(2)}, u32[]{:S(2)}) collective-permute-start(f32[3,80,128]{2,1,0:T(8,128)S(1)} %add_add_fusion.1.rest_0_), channel_id=1, source_target_pairs={{0,8},{8,0},{16,24},{24,16},{1,9},{9,1},{17,25},{25,17},{2,10},{10... | collective-permute-start | bytes 368648 | tf_op jit(solution)/shard_map/ppermute | solution.py:481
  28.0 2.9 %collective-permute-done.18.rest_6_ = f32[3,80,128]{2,1,0:T(8,128)S(1)} collective-permute-done((f32[3,80,128]{2,1,0:T(8,128)S(1)}, f32[3,80,128]{2,1,0:T(8,128)S(1)}, u32[]{:S(2)}, u32[]{:S(2)}) %collective-permute-start.18) | collective-permute-done | bytes 122912 | tf_op jit(solution)/shard_map/ppermute | solution.py:481
  30.9 1.1 collective-permute-done.16.rest_4_
  33.6 2.4 %shard_map.86 = (bf16[4,2,3,80,128]{4,3,2,1,0:T(8,128)(2,1)S(1)}, f32[3,80,128]{2,1,0:T(8,128)S(1)}, f32[80,128]{1,0:T(8,128)S(1)}, f32[3,80,128]{2,1,0:T(8,128)...) custom-call(s32[3]{0:T(128)S(1)} %pad_add_fusion.where, ...), custom_call_target="tpu_custom_call" | custom-call | flops 353894400 | bytes 921600 | tf_op jit(solution)/shard_map/pallas_call | solution.py:181
  36.7 3.4 %collective-permute-start.21 = (bf16[3,80,128]{2,1,0:T(8,128)(2,1)S(1)}, bf16[3,80,128]{2,1,0:T(8,128)(2,1)S(1)}, u32[]{:S(2)}, u32[]{:S(2)}) collective-permute-start(bf16[3,80,128]{2,1,0:T(8,128)(2,1)S(1)} %get-tuple-element.62), channel_id=1, source_target_pairs={{0,2},{1,3},{2,0},{3,1},{4,6},{5,7},{6,4},{7,5},{8,10},{9,11},{10,... | collective-permute-start | bytes 184328 | tf_op jit(solution)/shard_map/ppermute | solution.py:481
  40.4 3.5 %collective-permute-done.21 = bf16[3,80,128]{2,1,0:T(8,128)(2,1)S(1)} collective-permute-done((bf16[3,80,128]{2,1,0:T(8,128)(2,1)S(1)}, bf16[3,80,128]{2,1,0:T(8,128)(2,1)S(1)}, u32[]{:S(2)}, u32[]{:S(2)}) %collective-permute-start.21) | collective-permute-done | bytes 61472 | tf_op jit(solution)/shard_map/ppermute | solution.py:481
  43.9 2.2 %collective-permute-done.22 = bf16[3,80,128]{2,1,0:T(8,128)(2,1)S(1)} collective-permute-done((bf16[3,80,128]{2,1,0:T(8,128)(2,1)S(1)}, bf16[3,80,128]{2,1,0:T(8,128)(2,1)S(1)}, u32[]{:S(2)}, u32[]{:S(2)}) %collective-permute-start.22) | collective-permute-done | bytes 61472 | tf_op jit(solution)/shard_map/ppermute | solution.py:481
  46.2 1.8 %collective-permute-start.28 = (f32[3,80,128]{2,1,0:T(8,128)S(1)}, f32[3,80,128]{2,1,0:T(8,128)S(1)}, u32[]{:S(2)}, u32[]{:S(2)}) collective-permute-start(f32[3,80,128]{2,1,0:T(8,128)S(1)} %add_add_fusion.rest_0_), channel_id=1, source_target_pairs={{0,24},{8,16},{16,8},{24,0},{1,25},{9,17},{17,9},{25,1},{2,26},{10... | collective-permute-start | bytes 368648 | tf_op jit(solution)/shard_map/ppermute | solution.py:481
  48.7 1.0 collective-permute-start.24
  51.5 1.2 collective-permute-done.28.rest_6_
  52.7 1.0 collective-permute-done.26.rest_4_
  54.3 1.2 collective-permute-done.33.rest_15_
  55.5 2.8 %shard_map.87 = (bf16[3,80,128]{2,1,0:T(8,128)(2,1)}, bf16[5,80,128]{2,1,0:T(8,128)(2,1)S(1)}, bf16[4,2,3,80,128]{4,3,2,1,0:T(8,128)(2,1)S(1)}) custom-call(s32[3]{0:T(128)S(1)} %pad_add_fusion.where, f32[80,80]{1,0:T(8,128)S(1)} %copy-done.4, f32[3,80,128]{2,1,0:T(8,128)S(1)} %add_add_fusion.rest_0_, f32[3,80,128]{2,1,0:T(8,128)S(1)} %collective-permute-done.23.rest_1_, ...), custom_call_target="tpu_custom_call" | custom-call | tf_op jit(solution)/shard_map/pallas_call | solution.py:181
  58.3 1.4 %collective-permute-start.36 = (bf16[5,80,128]{2,1,0:T(8,128)(2,1)S(1)}, bf16[5,80,128]{2,1,0:T(8,128)(2,1)S(1)}, u32[]{:S(2)}, u32[]{:S(2)}) collective-permute-start(bf16[5,80,128]{2,1,0:T(8,128)(2,1)S(1)} %get-tuple-element.69.rest_0_), channel_id=1, source_target_pairs={{0,3},{1,2},{2,1},{3,0},{4,7},{5,6},{6,5},{7,4},{8,11},{9,10},{10,... | collective-permute-start | bytes 307208 | tf_op jit(solution)/shard_map/ppermute | solution.py:481
  59.7 1.1 collective-permute-start.35
  60.8 1.9 %collective-permute-start.34 = (bf16[5,80,128]{2,1,0:T(8,128)(2,1)S(1)}, bf16[5,80,128]{2,1,0:T(8,128)(2,1)S(1)}, u32[]{:S(2)}, u32[]{:S(2)}) collective-permute-start(bf16[5,80,128]{2,1,0:T(8,128)(2,1)S(1)} %get-tuple-element.69.rest_0_), channel_id=1, source_target_pairs={{0,1},{1,0},{2,3},{3,2},{4,5},{5,4},{6,7},{7,6},{8,9},{9,8},{10,11... | collective-permute-start | bytes 307208 | tf_op jit(solution)/shard_map/ppermute | solution.py:481
  62.7 3.2 %collective-permute-done.36.rest_6_.rest_4_ = bf16[5,80,128]{2,1,0:T(8,128)(2,1)S(1)} collective-permute-done((bf16[5,80,128]{2,1,0:T(8,128)(2,1)S(1)}, bf16[5,80,128]{2,1,0:T(8,128)(2,1)S(1)}, u32[]{:S(2)}, u32[]{:S(2)}) %collective-permute-start.36) | collective-permute-done | bytes 102432 | tf_op jit(solution)/shard_map/ppermute | solution.py:481
  65.9 4.5 %collective-permute-done.35.rest_4_.rest_2_ = bf16[5,80,128]{2,1,0:T(8,128)(2,1)S(1)} collective-permute-done((bf16[5,80,128]{2,1,0:T(8,128)(2,1)S(1)}, bf16[5,80,128]{2,1,0:T(8,128)(2,1)S(1)}, u32[]{:S(2)}, u32[]{:S(2)}) %collective-permute-start.35) | collective-permute-done | bytes 102432 | tf_op jit(solution)/shard_map/ppermute | solution.py:481
  71.9 2.0 %shard_map.88.rest_8_ = f32[3,80,128]{2,1,0:T(8,128)S(1)} custom-call(s32[3]{0:T(128)S(1)} %pad_add_fusion.where, bf16[6,80,960]{2,1,0:T(8,128)(2,1)S(1)} %get-tuple-element.71.weight, f32[3,80,128]{2,1,0:T(8,128)S(1)} %get-tuple-element.72.norm, bf16[5,80,128]{2,1,0:T(8,128)(2,1)S(1)} %get-tuple-element.69.rest_0_, ...), custom_call_target="tpu_custom_call" | custom-call | flops 353894400 | bytes 921600 | tf_op jit(solution)/shard_map/pallas_call | solution.py:181
  73.9 1.5 %collective-permute-start.46 = (f32[3,80,128]{2,1,0:T(8,128)S(1)}, f32[3,80,128]{2,1,0:T(8,128)S(1)}, u32[]{:S(2)}, u32[]{:S(2)}) collective-permute-start(f32[3,80,128]{2,1,0:T(8,128)S(1)} %shard_map.88.rest_8_), channel_id=1, source_target_pairs={{0,24},{8,16},{16,8},{24,0},{1,25},{9,17},{17,9},{25,1},{2,26},{10... | collective-permute-start | bytes 368648 | tf_op jit(solution)/shard_map/ppermute | solution.py:481
  75.4 1.2 collective-permute-start.44
  76.5 0.9 collective-permute-start.42
  77.5 3.6 %collective-permute-done.46.rest_14_ = f32[3,80,128]{2,1,0:T(8,128)S(1)} collective-permute-done((f32[3,80,128]{2,1,0:T(8,128)S(1)}, f32[3,80,128]{2,1,0:T(8,128)S(1)}, u32[]{:S(2)}, u32[]{:S(2)}) %collective-permute-start.46) | collective-permute-done | bytes 122912 | tf_op jit(solution)/shard_map/ppermute | solution.py:481
  81.0 2.0 %collective-permute-done.44.rest_12_ = f32[3,80,128]{2,1,0:T(8,128)S(1)} collective-permute-done((f32[3,80,128]{2,1,0:T(8,128)S(1)}, f32[3,80,128]{2,1,0:T(8,128)S(1)}, u32[]{:S(2)}, u32[]{:S(2)}) %collective-permute-start.44) | collective-permute-done | bytes 122912 | tf_op jit(solution)/shard_map/ppermute | solution.py:481
  84.6 1.3 %shard_map.89 = (bf16[3,80,128]{2,1,0:T(8,128)(2,1)S(1)}, bf16[4,2,3,80,128]{4,3,2,1,0:T(8,128)(2,1)S(1)}) custom-call(s32[3]{0:T(128)S(1)} %pad_add_fusion.where, f32[80,80]{1,0:T(8,128)S(1)} %copy-done.4, f32[80,128]{1,0:T(8,128)S(1)} %get-tuple-element.70.scale, f32[3,80,128]{2,1,0:T(8,128)S(1)} %add_add_fusion.1.rest_0_, ...), custom_call_target="tpu_custom_call" | custom-call | tf_op jit(solution)/shard_map/pallas_call | solution.py:181
  85.9 1.5 %collective-permute-start.58 = (bf16[3,3,80,128]{3,2,1,0:T(8,128)(2,1)S(1)}, bf16[3,3,80,128]{3,2,1,0:T(8,128)(2,1)S(1)}, u32[]{:S(2)}, u32[]{:S(2)}) collective-permute-start(bf16[3,3,80,128]{3,2,1,0:T(8,128)(2,1)S(1)} %pad_maximum_fusion), channel_id=1, source_target_pairs={{0,24},{8,16},{16,8},{24,0},{1,25},{9,17},{17,9},{25,1},{2,26},{10... | collective-permute-start | bytes 552968 | tf_op jit(solution)/shard_map/ppermute | solution.py:481
  87.3 1.2 collective-permute-start.56
  88.5 0.9 collective-permute-start.54
  89.4 2.6 %collective-permute-start.50 = (bf16[3,80,128]{2,1,0:T(8,128)(2,1)S(1)}, bf16[3,80,128]{2,1,0:T(8,128)(2,1)S(1)}, u32[]{:S(2)}, u32[]{:S(2)}) collective-permute-start(bf16[3,80,128]{2,1,0:T(8,128)(2,1)S(1)} %get-tuple-element.74), channel_id=1, source_target_pairs={{0,3},{1,2},{2,1},{3,0},{4,7},{5,6},{6,5},{7,4},{8,11},{9,10},{10,... | collective-permute-start | bytes 184328 | tf_op jit(solution)/shard_map/ppermute | solution.py:481
  92.1 2.3 %collective-permute-done.58.rest_10_ = bf16[3,3,80,128]{3,2,1,0:T(8,128)(2,1)S(1)} collective-permute-done((bf16[3,3,80,128]{3,2,1,0:T(8,128)(2,1)S(1)}, bf16[3,3,80,128]{3,2,1,0:T(8,128)(2,1)S(1)}, u32[]{:S(2)}, u32[]{:S(2)}) %collective-permute-start.58) | collective-permute-done | bytes 184352 | tf_op jit(solution)/shard_map/ppermute | solution.py:481
  94.3 3.3 %collective-permute-done.56.rest_8_ = bf16[3,3,80,128]{3,2,1,0:T(8,128)(2,1)S(1)} collective-permute-done((bf16[3,3,80,128]{3,2,1,0:T(8,128)(2,1)S(1)}, bf16[3,3,80,128]{3,2,1,0:T(8,128)(2,1)S(1)}, u32[]{:S(2)}, u32[]{:S(2)}) %collective-permute-start.56) | collective-permute-done | bytes 184352 | tf_op jit(solution)/shard_map/ppermute | solution.py:481
  98.2 3.2 %collective-permute-start.48 = (bf16[3,80,128]{2,1,0:T(8,128)(2,1)S(1)}, bf16[3,80,128]{2,1,0:T(8,128)(2,1)S(1)}, u32[]{:S(2)}, u32[]{:S(2)}) collective-permute-start(bf16[3,80,128]{2,1,0:T(8,128)(2,1)S(1)} %get-tuple-element.74), channel_id=1, source_target_pairs={{0,1},{1,0},{2,3},{3,2},{4,5},{5,4},{6,7},{7,6},{8,9},{9,8},{10,11... | collective-permute-start | bytes 184328 | tf_op jit(solution)/shard_map/ppermute | solution.py:481
  102.3 2.1 %collective-permute-done.49 = bf16[3,80,128]{2,1,0:T(8,128)(2,1)S(1)} collective-permute-done((bf16[3,80,128]{2,1,0:T(8,128)(2,1)S(1)}, bf16[3,80,128]{2,1,0:T(8,128)(2,1)S(1)}, u32[]{:S(2)}, u32[]{:S(2)}) %collective-permute-start.49) | collective-permute-done | bytes 61472 | tf_op jit(solution)/shard_map/ppermute | solution.py:481
  104.9 1.2 collective-permute-start.53
  106.2 1.3 %collective-permute-start.52 = (bf16[3,3,80,128]{3,2,1,0:T(8,128)(2,1)S(1)}, bf16[3,3,80,128]{3,2,1,0:T(8,128)(2,1)S(1)}, u32[]{:S(2)}, u32[]{:S(2)}) collective-permute-start(bf16[3,3,80,128]{3,2,1,0:T(8,128)(2,1)S(1)} %pad_maximum_fusion.1.rest_0_), channel_id=1, source_target_pairs={{0,16},{8,24},{16,0},{24,8},{1,17},{9,25},{17,1},{25,9},{2,18},{10... | collective-permute-start | bytes 552968 | tf_op jit(solution)/shard_map/ppermute | solution.py:481
  107.5 1.0 collective-permute-start.51
  108.5 6.4 %shard_map.90 = f32[27,80,320]{2,1,0:T(8,128)} custom-call(s32[3]{0:T(128)S(1)} %pad_add_fusion.where, bf16[4,2,3,80,128]{4,3,2,1,0:T(8,128)(2,1)S(1)} %get-tuple-element.75.hidden, bf16[4,2,3,80,128]{4,3,2,1,0:T(8,128)(2,1)S(1)} %get-tuple-element.76.every, bf16[5,80,128]{2,1,0:T(8,128)(2,1)S(1)} %collective-permute-done.34.rest_2_.rest_0_, ...), custom_call_target="tpu_custom_call" | custom-call | flops 2831155200 | bytes 8000000 | tf_op jit(solution)/shard_map/pallas_call | solution.py:181
  114.9 2.0 %collective-permute-done.52.rest_4_ = bf16[3,3,80,128]{3,2,1,0:T(8,128)(2,1)S(1)} collective-permute-done((bf16[3,3,80,128]{3,2,1,0:T(8,128)(2,1)S(1)}, bf16[3,3,80,128]{3,2,1,0:T(8,128)(2,1)S(1)}, u32[]{:S(2)}, u32[]{:S(2)}) %collective-permute-start.52) | collective-permute-done | bytes 184352 | tf_op jit(solution)/shard_map/ppermute | solution.py:481
  118.8 7.5 %shard_map.92 = (f32[27,80,320]{2,1,0:T(8,128)}, bf16[3,80,128]{2,1,0:T(8,128)(2,1)}) custom-call(s32[3]{0:T(128)S(1)} %pad_add_fusion.where, bf16[6,80,960]{2,1,0:T(8,128)(2,1)S(1)} %get-tuple-element.68.weight, bf16[3,80,128]{2,1,0:T(8,128)(2,1)S(1)} %bitcast.44, bf16[480,1792]{1,0:T(8,128)(2,1)S(1)} %shard_map.91.padded, ...), custom_call_target="tpu_custom_call" | custom-call | flops 2831155200 | bytes 8000000 | tf_op jit(solution)/shard_map/pallas_call | solution.py:181
  (109 shorter events, 19.4 us)
Async XLA Ops:
  0.6 8.5 %collective-permute-start.3 = (bf16[3,80,128]{2,1,0:T(8,128)(2,1)}, bf16[3,80,128]{2,1,0:T(8,128)(2,1)S(1)}, u32[]{:S(2)}, u32[]{:S(2)}) collective-permute-start(bf16[3,80,128]{2,1,0:T(8,128)(2,1)} %bitcast.32), channel_id=1, source_target_pairs={{0,24},{8,16},{16,8},{24,0},{1,25},{9,17},{17,9},{25,1},{2,26},{10... | collective-permute-start | bytes 184328 | tf_op jit(solution)/shard_map/ppermute | solution.py:481
  4.6 4.5 %collective-permute-start.2 = (bf16[3,80,128]{2,1,0:T(8,128)(2,1)}, bf16[3,80,128]{2,1,0:T(8,128)(2,1)S(1)}, u32[]{:S(2)}, u32[]{:S(2)}) collective-permute-start(bf16[3,80,128]{2,1,0:T(8,128)(2,1)} %bitcast.33), channel_id=1, source_target_pairs={{0,16},{8,24},{16,0},{24,8},{1,17},{9,25},{17,1},{25,9},{2,18},{10... | collective-permute-start | bytes 184328 | tf_op jit(solution)/shard_map/ppermute | solution.py:481
  5.1 4.4 %collective-permute-start.1 = (bf16[3,80,128]{2,1,0:T(8,128)(2,1)}, bf16[3,80,128]{2,1,0:T(8,128)(2,1)S(1)}, u32[]{:S(2)}, u32[]{:S(2)}) collective-permute-start(bf16[3,80,128]{2,1,0:T(8,128)(2,1)} %bitcast.34), channel_id=1, source_target_pairs={{0,8},{8,0},{16,24},{24,16},{1,9},{9,1},{17,25},{25,17},{2,10},{10... | collective-permute-start | bytes 184328 | tf_op jit(solution)/shard_map/ppermute | solution.py:481
  5.2 5.0 %collective-permute-start = (bf16[3,80,128]{2,1,0:T(8,128)(2,1)}, bf16[3,80,128]{2,1,0:T(8,128)(2,1)S(1)}, u32[]{:S(2)}, u32[]{:S(2)}) collective-permute-start(bf16[3,80,128]{2,1,0:T(8,128)(2,1)} %bitcast.35), channel_id=1, source_target_pairs={{0,4},{4,0},{1,5},{5,1},{2,6},{6,2},{3,7},{7,3},{8,12},{12,8},{9,1... | collective-permute-start | bytes 184328 | tf_op jit(solution)/shard_map/ppermute | solution.py:477
  12.7 7.6 %collective-permute-start.10 = (bf16[3,80,128]{2,1,0:T(8,128)(2,1)S(1)}, bf16[3,80,128]{2,1,0:T(8,128)(2,1)S(1)}, u32[]{:S(2)}, u32[]{:S(2)}) collective-permute-start(bf16[3,80,128]{2,1,0:T(8,128)(2,1)S(1)} %get-tuple-element.56), channel_id=1, source_target_pairs={{0,1},{1,0},{2,3},{3,2},{4,5},{5,4},{6,7},{7,6},{8,9},{9,8},{10,11... | collective-permute-start | bytes 184328 | tf_op jit(solution)/shard_map/ppermute | solution.py:481
  14.6 6.7 %collective-permute-start.11 = (bf16[3,80,128]{2,1,0:T(8,128)(2,1)S(1)}, bf16[3,80,128]{2,1,0:T(8,128)(2,1)S(1)}, u32[]{:S(2)}, u32[]{:S(2)}) collective-permute-start(bf16[3,80,128]{2,1,0:T(8,128)(2,1)S(1)} %get-tuple-element.57), channel_id=1, source_target_pairs={{0,2},{1,3},{2,0},{3,1},{4,6},{5,7},{6,4},{7,5},{8,10},{9,11},{10,... | collective-permute-start | bytes 184328 | tf_op jit(solution)/shard_map/ppermute | solution.py:481
  17.2 6.1 %collective-permute-start.12 = (bf16[3,80,128]{2,1,0:T(8,128)(2,1)S(1)}, bf16[3,80,128]{2,1,0:T(8,128)(2,1)S(1)}, u32[]{:S(2)}, u32[]{:S(2)}) collective-permute-start(bf16[3,80,128]{2,1,0:T(8,128)(2,1)S(1)} %get-tuple-element.58), channel_id=1, source_target_pairs={{0,3},{1,2},{2,1},{3,0},{4,7},{5,6},{6,5},{7,4},{8,11},{9,10},{10,... | collective-permute-start | bytes 184328 | tf_op jit(solution)/shard_map/ppermute | solution.py:481
  17.2 6.1 %collective-permute-start.9 = (bf16[3,80,128]{2,1,0:T(8,128)(2,1)S(1)}, bf16[3,80,128]{2,1,0:T(8,128)(2,1)S(1)}, u32[]{:S(2)}, u32[]{:S(2)}) collective-permute-start(bf16[3,80,128]{2,1,0:T(8,128)(2,1)S(1)} %bitcast.39), channel_id=1, source_target_pairs={{0,24},{8,16},{16,8},{24,0},{1,25},{9,17},{17,9},{25,1},{2,26},{10... | collective-permute-start | bytes 184328 | tf_op jit(solution)/shard_map/ppermute | solution.py:481
  19.8 4.2 %collective-permute-start.8 = (bf16[3,80,128]{2,1,0:T(8,128)(2,1)S(1)}, bf16[3,80,128]{2,1,0:T(8,128)(2,1)S(1)}, u32[]{:S(2)}, u32[]{:S(2)}) collective-permute-start(bf16[3,80,128]{2,1,0:T(8,128)(2,1)S(1)} %bitcast.40), channel_id=1, source_target_pairs={{0,16},{8,24},{16,0},{24,8},{1,17},{9,25},{17,1},{25,9},{2,18},{10... | collective-permute-start | bytes 184328 | tf_op jit(solution)/shard_map/ppermute | solution.py:481
  20.3 4.2 %collective-permute-start.7 = (bf16[3,80,128]{2,1,0:T(8,128)(2,1)S(1)}, bf16[3,80,128]{2,1,0:T(8,128)(2,1)S(1)}, u32[]{:S(2)}, u32[]{:S(2)}) collective-permute-start(bf16[3,80,128]{2,1,0:T(8,128)(2,1)S(1)} %bitcast.41), channel_id=1, source_target_pairs={{0,8},{8,0},{16,24},{24,16},{1,9},{9,1},{17,25},{25,17},{2,10},{10... | collective-permute-start | bytes 184328 | tf_op jit(solution)/shard_map/ppermute | solution.py:481
  24.6 6.4 %collective-permute-start.18 = (f32[3,80,128]{2,1,0:T(8,128)S(1)}, f32[3,80,128]{2,1,0:T(8,128)S(1)}, u32[]{:S(2)}, u32[]{:S(2)}) collective-permute-start(f32[3,80,128]{2,1,0:T(8,128)S(1)} %add_add_fusion.1.rest_0_), channel_id=1, source_target_pairs={{0,24},{8,16},{16,8},{24,0},{1,25},{9,17},{17,9},{25,1},{2,26},{10... | collective-permute-start | bytes 368648 | tf_op jit(solution)/shard_map/ppermute | solution.py:481
  26.0 6.0 %collective-permute-start.16 = (f32[3,80,128]{2,1,0:T(8,128)S(1)}, f32[3,80,128]{2,1,0:T(8,128)S(1)}, u32[]{:S(2)}, u32[]{:S(2)}) collective-permute-start(f32[3,80,128]{2,1,0:T(8,128)S(1)} %add_add_fusion.1.rest_0_), channel_id=1, source_target_pairs={{0,16},{8,24},{16,0},{24,8},{1,17},{9,25},{17,1},{25,9},{2,18},{10... | collective-permute-start | bytes 368648 | tf_op jit(solution)/shard_map/ppermute | solution.py:481
  26.4 5.7 %collective-permute-start.14 = (f32[3,80,128]{2,1,0:T(8,128)S(1)}, f32[3,80,128]{2,1,0:T(8,128)S(1)}, u32[]{:S(2)}, u32[]{:S(2)}) collective-permute-start(f32[3,80,128]{2,1,0:T(8,128)S(1)} %add_add_fusion.1.rest_0_), channel_id=1, source_target_pairs={{0,8},{8,0},{16,24},{24,16},{1,9},{9,1},{17,25},{25,17},{2,10},{10... | collective-permute-start | bytes 368648 | tf_op jit(solution)/shard_map/ppermute | solution.py:481
  28.0 4.5 %collective-permute-start.13 = (f32[3,80,128]{2,1,0:T(8,128)S(1)}, f32[3,80,128]{2,1,0:T(8,128)S(1)}, u32[]{:S(2)}, u32[]{:S(2)}) collective-permute-start(f32[3,80,128]{2,1,0:T(8,128)S(1)} %add_add_fusion.1.rest_0_), channel_id=1, source_target_pairs={{0,4},{4,0},{1,5},{5,1},{2,6},{6,2},{3,7},{7,3},{8,12},{12,8},{9,1... | collective-permute-start | bytes 368648 | tf_op jit(solution)/shard_map/ppermute | solution.py:477
  35.9 4.5 %collective-permute-start.20 = (bf16[3,80,128]{2,1,0:T(8,128)(2,1)S(1)}, bf16[3,80,128]{2,1,0:T(8,128)(2,1)S(1)}, u32[]{:S(2)}, u32[]{:S(2)}) collective-permute-start(bf16[3,80,128]{2,1,0:T(8,128)(2,1)S(1)} %get-tuple-element.61), channel_id=1, source_target_pairs={{0,1},{1,0},{2,3},{3,2},{4,5},{5,4},{6,7},{7,6},{8,9},{9,8},{10,11... | collective-permute-start | bytes 184328 | tf_op jit(solution)/shard_map/ppermute | solution.py:481
  36.7 7.3 %collective-permute-start.21 = (bf16[3,80,128]{2,1,0:T(8,128)(2,1)S(1)}, bf16[3,80,128]{2,1,0:T(8,128)(2,1)S(1)}, u32[]{:S(2)}, u32[]{:S(2)}) collective-permute-start(bf16[3,80,128]{2,1,0:T(8,128)(2,1)S(1)} %get-tuple-element.62), channel_id=1, source_target_pairs={{0,2},{1,3},{2,0},{3,1},{4,6},{5,7},{6,4},{7,5},{8,10},{9,11},{10,... | collective-permute-start | bytes 184328 | tf_op jit(solution)/shard_map/ppermute | solution.py:481
  40.0 6.1 %collective-permute-start.22 = (bf16[3,80,128]{2,1,0:T(8,128)(2,1)S(1)}, bf16[3,80,128]{2,1,0:T(8,128)(2,1)S(1)}, u32[]{:S(2)}, u32[]{:S(2)}) collective-permute-start(bf16[3,80,128]{2,1,0:T(8,128)(2,1)S(1)} %get-tuple-element.63), channel_id=1, source_target_pairs={{0,3},{1,2},{2,1},{3,0},{4,7},{5,6},{6,5},{7,4},{8,11},{9,10},{10,... | collective-permute-start | bytes 184328 | tf_op jit(solution)/shard_map/ppermute | solution.py:481
  46.2 6.5 %collective-permute-start.28 = (f32[3,80,128]{2,1,0:T(8,128)S(1)}, f32[3,80,128]{2,1,0:T(8,128)S(1)}, u32[]{:S(2)}, u32[]{:S(2)}) collective-permute-start(f32[3,80,128]{2,1,0:T(8,128)S(1)} %add_add_fusion.rest_0_), channel_id=1, source_target_pairs={{0,24},{8,16},{16,8},{24,0},{1,25},{9,17},{17,9},{25,1},{2,26},{10... | collective-permute-start | bytes 368648 | tf_op jit(solution)/shard_map/ppermute | solution.py:481
  47.9 5.8 %collective-permute-start.26 = (f32[3,80,128]{2,1,0:T(8,128)S(1)}, f32[3,80,128]{2,1,0:T(8,128)S(1)}, u32[]{:S(2)}, u32[]{:S(2)}) collective-permute-start(f32[3,80,128]{2,1,0:T(8,128)S(1)} %add_add_fusion.rest_0_), channel_id=1, source_target_pairs={{0,16},{8,24},{16,0},{24,8},{1,17},{9,25},{17,1},{25,9},{2,18},{10... | collective-permute-start | bytes 368648 | tf_op jit(solution)/shard_map/ppermute | solution.py:481
  48.7 5.0 %collective-permute-start.24 = (f32[3,80,128]{2,1,0:T(8,128)S(1)}, f32[3,80,128]{2,1,0:T(8,128)S(1)}, u32[]{:S(2)}, u32[]{:S(2)}) collective-permute-start(f32[3,80,128]{2,1,0:T(8,128)S(1)} %add_add_fusion.rest_0_), channel_id=1, source_target_pairs={{0,8},{8,0},{16,24},{24,16},{1,9},{9,1},{17,25},{25,17},{2,10},{10... | collective-permute-start | bytes 368648 | tf_op jit(solution)/shard_map/ppermute | solution.py:481
  51.0 3.3 %collective-permute-start.32 = (bf16[3,80,128]{2,1,0:T(8,128)(2,1)S(1)}, bf16[3,80,128]{2,1,0:T(8,128)(2,1)S(1)}, u32[]{:S(2)}, u32[]{:S(2)}) collective-permute-start(bf16[3,80,128]{2,1,0:T(8,128)(2,1)S(1)} %collective-permute-done.8.rest_12_), channel_id=1, source_target_pairs={{0,4},{4,0},{1,5},{5,1},{2,6},{6,2},{3,7},{7,3},{8,12},{12,8},{9,1... | collective-permute-start | bytes 184328 | tf_op jit(solution)/shard_map/ppermute | solution.py:477
  51.1 4.4 %collective-permute-start.23 = (f32[3,80,128]{2,1,0:T(8,128)S(1)}, f32[3,80,128]{2,1,0:T(8,128)S(1)}, u32[]{:S(2)}, u32[]{:S(2)}) collective-permute-start(f32[3,80,128]{2,1,0:T(8,128)S(1)} %add_add_fusion.rest_0_), channel_id=1, source_target_pairs={{0,4},{4,0},{1,5},{5,1},{2,6},{6,2},{3,7},{7,3},{8,12},{12,8},{9,1... | collective-permute-start | bytes 368648 | tf_op jit(solution)/shard_map/ppermute | solution.py:477
  52.7 2.8 %collective-permute-start.29 = (f32[3,80,128]{2,1,0:T(8,128)S(1)}, f32[3,80,128]{2,1,0:T(8,128)S(1)}, u32[]{:S(2)}, u32[]{:S(2)}) collective-permute-start(f32[3,80,128]{2,1,0:T(8,128)S(1)} %collective-permute-done.28.rest_6_), channel_id=1, source_target_pairs={{0,4},{4,0},{1,5},{5,1},{2,6},{6,2},{3,7},{7,3},{8,12},{12,8},{9,1... | collective-permute-start | bytes 368648 | tf_op jit(solution)/shard_map/ppermute | solution.py:477
  53.7 1.8 %collective-permute-start.27 = (f32[3,80,128]{2,1,0:T(8,128)S(1)}, f32[3,80,128]{2,1,0:T(8,128)S(1)}, u32[]{:S(2)}, u32[]{:S(2)}) collective-permute-start(f32[3,80,128]{2,1,0:T(8,128)S(1)} %collective-permute-done.26.rest_4_), channel_id=1, source_target_pairs={{0,4},{4,0},{1,5},{5,1},{2,6},{6,2},{3,7},{7,3},{8,12},{12,8},{9,1... | collective-permute-start | bytes 368648 | tf_op jit(solution)/shard_map/ppermute | solution.py:477
  53.7 1.8 %collective-permute-start.25 = (f32[3,80,128]{2,1,0:T(8,128)S(1)}, f32[3,80,128]{2,1,0:T(8,128)S(1)}, u32[]{:S(2)}, u32[]{:S(2)}) collective-permute-start(f32[3,80,128]{2,1,0:T(8,128)S(1)} %collective-permute-done.24.rest_2_), channel_id=1, source_target_pairs={{0,4},{4,0},{1,5},{5,1},{2,6},{6,2},{3,7},{7,3},{8,12},{12,8},{9,1... | collective-permute-start | bytes 368648 | tf_op jit(solution)/shard_map/ppermute | solution.py:477
  58.3 7.6 %collective-permute-start.36 = (bf16[5,80,128]{2,1,0:T(8,128)(2,1)S(1)}, bf16[5,80,128]{2,1,0:T(8,128)(2,1)S(1)}, u32[]{:S(2)}, u32[]{:S(2)}) collective-permute-start(bf16[5,80,128]{2,1,0:T(8,128)(2,1)S(1)} %get-tuple-element.69.rest_0_), channel_id=1, source_target_pairs={{0,3},{1,2},{2,1},{3,0},{4,7},{5,6},{6,5},{7,4},{8,11},{9,10},{10,... | collective-permute-start | bytes 307208 | tf_op jit(solution)/shard_map/ppermute | solution.py:481
  59.7 10.7 %collective-permute-start.35 = (bf16[5,80,128]{2,1,0:T(8,128)(2,1)S(1)}, bf16[5,80,128]{2,1,0:T(8,128)(2,1)S(1)}, u32[]{:S(2)}, u32[]{:S(2)}) collective-permute-start(bf16[5,80,128]{2,1,0:T(8,128)(2,1)S(1)} %get-tuple-element.69.rest_0_), channel_id=1, source_target_pairs={{0,2},{1,3},{2,0},{3,1},{4,6},{5,7},{6,4},{7,5},{8,10},{9,11},{10,... | collective-permute-start | bytes 307208 | tf_op jit(solution)/shard_map/ppermute | solution.py:481
  60.8 9.6 %collective-permute-start.34 = (bf16[5,80,128]{2,1,0:T(8,128)(2,1)S(1)}, bf16[5,80,128]{2,1,0:T(8,128)(2,1)S(1)}, u32[]{:S(2)}, u32[]{:S(2)}) collective-permute-start(bf16[5,80,128]{2,1,0:T(8,128)(2,1)S(1)} %get-tuple-element.69.rest_0_), channel_id=1, source_target_pairs={{0,1},{1,0},{2,3},{3,2},{4,5},{5,4},{6,7},{7,6},{8,9},{9,8},{10,11... | collective-permute-start | bytes 307208 | tf_op jit(solution)/shard_map/ppermute | solution.py:481
  62.7 8.3 %collective-permute-start.37 = (bf16[5,80,128]{2,1,0:T(8,128)(2,1)S(1)}, bf16[5,80,128]{2,1,0:T(8,128)(2,1)S(1)}, u32[]{:S(2)}, u32[]{:S(2)}) collective-permute-start(bf16[5,80,128]{2,1,0:T(8,128)(2,1)S(1)} %get-tuple-element.69.rest_0_), channel_id=1, source_target_pairs={{0,4},{4,0},{1,5},{5,1},{2,6},{6,2},{3,7},{7,3},{8,12},{12,8},{9,1... | collective-permute-start | bytes 307208 | tf_op jit(solution)/shard_map/ppermute | solution.py:477
  65.9 5.0 %collective-permute-start.40 = (bf16[5,80,128]{2,1,0:T(8,128)(2,1)S(1)}, bf16[5,80,128]{2,1,0:T(8,128)(2,1)S(1)}, u32[]{:S(2)}, u32[]{:S(2)}) collective-permute-start(bf16[5,80,128]{2,1,0:T(8,128)(2,1)S(1)} %collective-permute-done.36.rest_6_.rest_4_), channel_id=1, source_target_pairs={{0,4},{4,0},{1,5},{5,1},{2,6},{6,2},{3,7},{7,3},{8,12},{12,8},{9,1... | collective-permute-start | bytes 307208 | tf_op jit(solution)/shard_map/ppermute | solution.py:477
  73.9 7.2 %collective-permute-start.46 = (f32[3,80,128]{2,1,0:T(8,128)S(1)}, f32[3,80,128]{2,1,0:T(8,128)S(1)}, u32[]{:S(2)}, u32[]{:S(2)}) collective-permute-start(f32[3,80,128]{2,1,0:T(8,128)S(1)} %shard_map.88.rest_8_), channel_id=1, source_target_pairs={{0,24},{8,16},{16,8},{24,0},{1,25},{9,17},{17,9},{25,1},{2,26},{10... | collective-permute-start | bytes 368648 | tf_op jit(solution)/shard_map/ppermute | solution.py:481
  75.4 7.7 %collective-permute-start.44 = (f32[3,80,128]{2,1,0:T(8,128)S(1)}, f32[3,80,128]{2,1,0:T(8,128)S(1)}, u32[]{:S(2)}, u32[]{:S(2)}) collective-permute-start(f32[3,80,128]{2,1,0:T(8,128)S(1)} %shard_map.88.rest_8_), channel_id=1, source_target_pairs={{0,16},{8,24},{16,0},{24,8},{1,17},{9,25},{17,1},{25,9},{2,18},{10... | collective-permute-start | bytes 368648 | tf_op jit(solution)/shard_map/ppermute | solution.py:481
  76.5 6.6 %collective-permute-start.42 = (f32[3,80,128]{2,1,0:T(8,128)S(1)}, f32[3,80,128]{2,1,0:T(8,128)S(1)}, u32[]{:S(2)}, u32[]{:S(2)}) collective-permute-start(f32[3,80,128]{2,1,0:T(8,128)S(1)} %shard_map.88.rest_8_), channel_id=1, source_target_pairs={{0,8},{8,0},{16,24},{24,16},{1,9},{9,1},{17,25},{25,17},{2,10},{10... | collective-permute-start | bytes 368648 | tf_op jit(solution)/shard_map/ppermute | solution.py:481
  77.5 6.2 %collective-permute-start.41 = (f32[3,80,128]{2,1,0:T(8,128)S(1)}, f32[3,80,128]{2,1,0:T(8,128)S(1)}, u32[]{:S(2)}, u32[]{:S(2)}) collective-permute-start(f32[3,80,128]{2,1,0:T(8,128)S(1)} %shard_map.88.rest_8_), channel_id=1, source_target_pairs={{0,4},{4,0},{1,5},{5,1},{2,6},{6,2},{3,7},{7,3},{8,12},{12,8},{9,1... | collective-permute-start | bytes 368648 | tf_op jit(solution)/shard_map/ppermute | solution.py:477
  81.0 2.6 %collective-permute-start.47 = (f32[3,80,128]{2,1,0:T(8,128)S(1)}, f32[3,80,128]{2,1,0:T(8,128)S(1)}, u32[]{:S(2)}, u32[]{:S(2)}) collective-permute-start(f32[3,80,128]{2,1,0:T(8,128)S(1)} %collective-permute-done.46.rest_14_), channel_id=1, source_target_pairs={{0,4},{4,0},{1,5},{5,1},{2,6},{6,2},{3,7},{7,3},{8,12},{12,8},{9,1... | collective-permute-start | bytes 368648 | tf_op jit(solution)/shard_map/ppermute | solution.py:477
  85.9 8.5 %collective-permute-start.58 = (bf16[3,3,80,128]{3,2,1,0:T(8,128)(2,1)S(1)}, bf16[3,3,80,128]{3,2,1,0:T(8,128)(2,1)S(1)}, u32[]{:S(2)}, u32[]{:S(2)}) collective-permute-start(bf16[3,3,80,128]{3,2,1,0:T(8,128)(2,1)S(1)} %pad_maximum_fusion), channel_id=1, source_target_pairs={{0,24},{8,16},{16,8},{24,0},{1,25},{9,17},{17,9},{25,1},{2,26},{10... | collective-permute-start | bytes 552968 | tf_op jit(solution)/shard_map/ppermute | solution.py:481
  87.3 10.3 %collective-permute-start.56 = (bf16[3,3,80,128]{3,2,1,0:T(8,128)(2,1)S(1)}, bf16[3,3,80,128]{3,2,1,0:T(8,128)(2,1)S(1)}, u32[]{:S(2)}, u32[]{:S(2)}) collective-permute-start(bf16[3,3,80,128]{3,2,1,0:T(8,128)(2,1)S(1)} %pad_maximum_fusion), channel_id=1, source_target_pairs={{0,16},{8,24},{16,0},{24,8},{1,17},{9,25},{17,1},{25,9},{2,18},{10... | collective-permute-start | bytes 552968 | tf_op jit(solution)/shard_map/ppermute | solution.py:481
  88.5 9.2 %collective-permute-start.54 = (bf16[3,3,80,128]{3,2,1,0:T(8,128)(2,1)S(1)}, bf16[3,3,80,128]{3,2,1,0:T(8,128)(2,1)S(1)}, u32[]{:S(2)}, u32[]{:S(2)}) collective-permute-start(bf16[3,3,80,128]{3,2,1,0:T(8,128)(2,1)S(1)} %pad_maximum_fusion), channel_id=1, source_target_pairs={{0,8},{8,0},{16,24},{24,16},{1,9},{9,1},{17,25},{25,17},{2,10},{10... | collective-permute-start | bytes 552968 | tf_op jit(solution)/shard_map/ppermute | solution.py:481
  89.4 8.8 %collective-permute-start.50 = (bf16[3,80,128]{2,1,0:T(8,128)(2,1)S(1)}, bf16[3,80,128]{2,1,0:T(8,128)(2,1)S(1)}, u32[]{:S(2)}, u32[]{:S(2)}) collective-permute-start(bf16[3,80,128]{2,1,0:T(8,128)(2,1)S(1)} %get-tuple-element.74), channel_id=1, source_target_pairs={{0,3},{1,2},{2,1},{3,0},{4,7},{5,6},{6,5},{7,4},{8,11},{9,10},{10,... | collective-permute-start | bytes 184328 | tf_op jit(solution)/shard_map/ppermute | solution.py:481
  94.3 11.8 %collective-permute-start.59 = (bf16[3,3,80,128]{3,2,1,0:T(8,128)(2,1)S(1)}, bf16[3,3,80,128]{3,2,1,0:T(8,128)(2,1)S(1)}, u32[]{:S(2)}, u32[]{:S(2)}) collective-permute-start(bf16[3,3,80,128]{3,2,1,0:T(8,128)(2,1)S(1)} %collective-permute-done.58.rest_10_), channel_id=1, source_target_pairs={{0,4},{4,0},{1,5},{5,1},{2,6},{6,2},{3,7},{7,3},{8,12},{12,8},{9,1... | collective-permute-start | bytes 552968 | tf_op jit(solution)/shard_map/ppermute | solution.py:477
  97.7 9.8 %collective-permute-start.57 = (bf16[3,3,80,128]{3,2,1,0:T(8,128)(2,1)S(1)}, bf16[3,3,80,128]{3,2,1,0:T(8,128)(2,1)S(1)}, u32[]{:S(2)}, u32[]{:S(2)}) collective-permute-start(bf16[3,3,80,128]{3,2,1,0:T(8,128)(2,1)S(1)} %collective-permute-done.56.rest_8_), channel_id=1, source_target_pairs={{0,4},{4,0},{1,5},{5,1},{2,6},{6,2},{3,7},{7,3},{8,12},{12,8},{9,1... | collective-permute-start | bytes 552968 | tf_op jit(solution)/shard_map/ppermute | solution.py:477
  97.7 10.8 %collective-permute-start.55 = (bf16[3,3,80,128]{3,2,1,0:T(8,128)(2,1)S(1)}, bf16[3,3,80,128]{3,2,1,0:T(8,128)(2,1)S(1)}, u32[]{:S(2)}, u32[]{:S(2)}) collective-permute-start(bf16[3,3,80,128]{3,2,1,0:T(8,128)(2,1)S(1)} %collective-permute-done.54.rest_6_), channel_id=1, source_target_pairs={{0,4},{4,0},{1,5},{5,1},{2,6},{6,2},{3,7},{7,3},{8,12},{12,8},{9,1... | collective-permute-start | bytes 552968 | tf_op jit(solution)/shard_map/ppermute | solution.py:477
  98.2 6.2 %collective-permute-start.49 = (bf16[3,80,128]{2,1,0:T(8,128)(2,1)S(1)}, bf16[3,80,128]{2,1,0:T(8,128)(2,1)S(1)}, u32[]{:S(2)}, u32[]{:S(2)}) collective-permute-start(bf16[3,80,128]{2,1,0:T(8,128)(2,1)S(1)} %get-tuple-element.74), channel_id=1, source_target_pairs={{0,2},{1,3},{2,0},{3,1},{4,6},{5,7},{6,4},{7,5},{8,10},{9,11},{10,... | collective-permute-start | bytes 184328 | tf_op jit(solution)/shard_map/ppermute | solution.py:481
  98.2 6.6 %collective-permute-start.48 = (bf16[3,80,128]{2,1,0:T(8,128)(2,1)S(1)}, bf16[3,80,128]{2,1,0:T(8,128)(2,1)S(1)}, u32[]{:S(2)}, u32[]{:S(2)}) collective-permute-start(bf16[3,80,128]{2,1,0:T(8,128)(2,1)S(1)} %get-tuple-element.74), channel_id=1, source_target_pairs={{0,1},{1,0},{2,3},{3,2},{4,5},{5,4},{6,7},{7,6},{8,9},{9,8},{10,11... | collective-permute-start | bytes 184328 | tf_op jit(solution)/shard_map/ppermute | solution.py:481
  104.8 12.5 %collective-permute-start.60 = (bf16[3,3,80,128]{3,2,1,0:T(8,128)(2,1)S(1)}, bf16[3,3,80,128]{3,2,1,0:T(8,128)(2,1)S(1)}, u32[]{:S(2)}, u32[]{:S(2)}) collective-permute-start(bf16[3,3,80,128]{3,2,1,0:T(8,128)(2,1)S(1)} %pad_maximum_fusion.1.rest_0_), channel_id=1, source_target_pairs={{0,4},{4,0},{1,5},{5,1},{2,6},{6,2},{3,7},{7,3},{8,12},{12,8},{9,1... | collective-permute-start | bytes 552968 | tf_op jit(solution)/shard_map/ppermute | solution.py:477
  104.9 9.9 %collective-permute-start.53 = (bf16[3,3,80,128]{3,2,1,0:T(8,128)(2,1)S(1)}, bf16[3,3,80,128]{3,2,1,0:T(8,128)(2,1)S(1)}, u32[]{:S(2)}, u32[]{:S(2)}) collective-permute-start(bf16[3,3,80,128]{3,2,1,0:T(8,128)(2,1)S(1)} %pad_maximum_fusion.1.rest_0_), channel_id=1, source_target_pairs={{0,24},{8,16},{16,8},{24,0},{1,25},{9,17},{17,9},{25,1},{2,26},{10... | collective-permute-start | bytes 552968 | tf_op jit(solution)/shard_map/ppermute | solution.py:481
  106.2 10.7 %collective-permute-start.52 = (bf16[3,3,80,128]{3,2,1,0:T(8,128)(2,1)S(1)}, bf16[3,3,80,128]{3,2,1,0:T(8,128)(2,1)S(1)}, u32[]{:S(2)}, u32[]{:S(2)}) collective-permute-start(bf16[3,3,80,128]{3,2,1,0:T(8,128)(2,1)S(1)} %pad_maximum_fusion.1.rest_0_), channel_id=1, source_target_pairs={{0,16},{8,24},{16,0},{24,8},{1,17},{9,25},{17,1},{25,9},{2,18},{10... | collective-permute-start | bytes 552968 | tf_op jit(solution)/shard_map/ppermute | solution.py:481
  107.5 9.3 %collective-permute-start.51 = (bf16[3,3,80,128]{3,2,1,0:T(8,128)(2,1)S(1)}, bf16[3,3,80,128]{3,2,1,0:T(8,128)(2,1)S(1)}, u32[]{:S(2)}, u32[]{:S(2)}) collective-permute-start(bf16[3,3,80,128]{3,2,1,0:T(8,128)(2,1)S(1)} %pad_maximum_fusion.1.rest_0_), channel_id=1, source_target_pairs={{0,8},{8,0},{16,24},{24,16},{1,9},{9,1},{17,25},{25,17},{2,10},{10... | collective-permute-start | bytes 552968 | tf_op jit(solution)/shard_map/ppermute | solution.py:481
  (22 other events, 85.3 us)

commit v3 on v2

--- a/solution.py
+++ b/solution.py
@@ -166,14 +166,12 @@
 SIDES = [(slot, side) for slot in range(4) for side in range(2)]
 
 
-def call(kernel, outs, args, scratch=(), grid=None, specs=None, flops=0, reads=0, grant=16, after=()):
+def call(kernel, outs, args, scratch=(), grid=None, specs=None, flops=0, reads=0, grant=16):
     vmem = pl.BlockSpec(memory_space=pltpu.VMEM)
     in_specs = [pl.BlockSpec(memory_space=pltpu.SMEM)] + [vmem] * (len(args) - 1)
-    if after:
-        inner, taken = kernel, len(args)
-        kernel = lambda *refs: inner(*refs[:taken], *refs[taken + len(after) :])
-        in_specs += [pl.BlockSpec(memory_space=pl.ANY)] * len(after)
-        args = (*args, *after)
+    inner, taken = kernel, len(args)
+    kernel = lambda where, *refs: inner(where, *refs[: taken - 1][::-1], *refs[taken - 1 :])
+    args = (args[0], *args[:0:-1])
     params = dict(vmem_limit_bytes=grant * 1024 * 1024)
     if grid is not None:
         params["dimension_semantics"] = ("arbitrary",) * len(grid)
@@ -347,7 +345,7 @@
         normed = norm[frame]
         gate = jax.nn.sigmoid(normed)
         cells = out[:, frame * LANES : (frame + 1) * LANES]
-        grad[frame] = cells * gate * (1.0 + normed * (1.0 - gate))
+        grad[frame] = (cells * gate * (1.0 + normed * (1.0 - gate))).astype(BF16)
 
 
 def back_product(weight, shifted, frames):
@@ -370,7 +368,7 @@
     first = second = None
     for slot, side in SIDES:
         for frame in range(frames):
-            cells = grads[2 * slot + side][frame]
+            cells = grads[2 * slot + side][frame].astype(F32)
             first = cells if first is None else first + cells
             term = cells * norm(slot, side, frame)
             second = term if second is None else second + term
@@ -378,11 +376,12 @@
     second = group_total(mixer[...], jnp.sum(second, axis=1, keepdims=True))[:, :1] / members
     for slot, side in SIDES:
         for frame in range(frames):
-            cells = grads[2 * slot + side][frame] - first - norm(slot, side, frame) * second
+            cells = grads[2 * slot + side][frame].astype(F32)
+            cells = cells - first - norm(slot, side, frame) * second
             cells = (cells * inv).astype(BF16)
             every[slot, side, frame] = cells
-            if slot == 0 and side == 0:
-                out[frame] = cells
+            if slot in (0, 3) and side == 0:
+                out[slot // 3, frame] = cells
 
 
 def pad_kernel(frames, where, *rest):
@@ -407,36 +406,45 @@
                 padded[rows, lanes_of(where, slot, frames, frame + 1)] = shift(cells, tap_col)
 
 
-def weight_step(grads, frames, where, channels, out, padded, full, prologue):
-    tap_frame = pl.program_id(0)
+def weight_step(grads, frames, where, channels, out, padded, full, ready, sent, finish=None):
     under_rows = -(-4 * channels // LANES) * LANES
-
-    @pl.when(tap_frame == 0)
-    def _():
-        prologue()
-        gap = under_rows - 4 * channels
-        full[pl.ds(4 * channels, gap), :] = jnp.zeros((gap, full.shape[1]), full.dtype)
-        for slot, side in SIDES:
-            for frame in range(frames):
-                for part in range(4):
-                    owner = jnp.bitwise_xor(where[2], part)
-                    rows = pl.ds(pl.multiple_of(side * under_rows + owner * channels, 16), channels)
-                    full[rows, lanes_of(where, slot, frames, frame)] = grads(slot, side, part, frame)
-
-    window = padded[:, pl.ds(pl.multiple_of(tap_frame * LANES, LANES), full.shape[1])]
-    both = lax.dot_general(window, full[...], (((1,), (1,)), ((), ())), preferred_element_type=F32)
-    mine, theirs = both[:, : 4 * channels], both[:, under_rows:]
-    for tap_col in range(3):
-        upper = slice(tap_col * channels, (tap_col + 1) * channels)
-        under = slice((3 + tap_col) * channels, (4 + tap_col) * channels)
-        out[3 + tap_col] = mine[upper] + theirs[under]
-        out[3 * other_tap(where, False) + tap_col] = mine[under]
-        out[3 * other_tap(where, True) + tap_col] = theirs[upper]
-
-
-def weight_kernel(frames, where, hidden, every, *rest):
-    own, far, (out, padded, full) = rest[:6], rest[6:12], rest[12:]
-    channels = hidden.shape[3]
+    gap = under_rows - 4 * channels
+    full[pl.ds(4 * channels, gap), :] = jnp.zeros((gap, full.shape[1]), full.dtype)
+    for slot, side in SIDES:
+        for frame in range(frames):
+            for part in range(4):
+                owner = jnp.bitwise_xor(where[2], part)
+                rows = pl.ds(pl.multiple_of(side * under_rows + owner * channels, 16), channels)
+                full[rows, lanes_of(where, slot, frames, frame)] = grads(slot, side, part, frame)
+    copies = []
+    for tap_frame in range(3):
+        window = padded[:, pl.ds(tap_frame * LANES, full.shape[1])]
+        both = lax.dot_general(window, full[...], (((1,), (1,)), ((), ())), preferred_element_type=F32)
+        mine, theirs = both[:, : 4 * channels], both[:, under_rows:]
+        for tap_col in range(3):
+            upper = slice(tap_col * channels, (tap_col + 1) * channels)
+            under = slice((3 + tap_col) * channels, (4 + tap_col) * channels)
+            ready[tap_frame, 3 + tap_col] = mine[upper] + theirs[under]
+            ready[tap_frame, 3 * other_tap(where, False) + tap_col] = mine[under]
+            ready[tap_frame, 3 * other_tap(where, True) + tap_col] = theirs[upper]
+        copies.append(
+            pltpu.make_async_copy(ready.at[tap_frame], out.at[pl.ds(9 * tap_frame, 9)], sent.at[tap_frame])
+        )
+        copies[-1].start()
+    if finish is not None:
+        finish()
+    for copy in copies:
+        copy.wait()
+
+
+def pad_hidden_kernel(frames, where, hidden, padded):
+    inputs = lambda slot, side, frame: hidden[slot, side, frame]
+    fill_padded(padded, inputs, frames, where, hidden.shape[3])
+
+
+def weight_kernel(frames, where, padded, every, *rest):
+    own, far, (out, full, ready, sent) = rest[:6], rest[6:12], rest[12:]
+    channels = every.shape[3]
 
     def grads(slot, side, part, frame):
         if part == 0:
@@ -445,13 +453,11 @@
             return own[2 * (part - 1) + side][frame + 1]
         return far[2 * (slot - 1) + side][part - 1, frame]
 
-    inputs = lambda slot, side, frame: hidden[slot, side, frame]
-    prologue = lambda: fill_padded(padded, inputs, frames, where, channels)
-    weight_step(grads, frames, where, channels, out, padded, full, prologue)
+    weight_step(grads, frames, where, channels, out, padded, full, ready, sent)
 
 
 def last_kernel(frames, where, weight, cotangent, padded, every, *rest):
-    far, (out, back, full, shifted) = rest[:8], rest[8:]
+    far, (out, back, full, shifted, ready, sent) = rest[:8], rest[8:]
     channels = weight.shape[1]
 
     def grads(slot, side, part, frame):
@@ -459,7 +465,7 @@
             return every[slot, side, frame]
         return far[2 * slot + side][part - 1, frame]
 
-    def prologue():
+    def finish():
         for part in range(4):
             pieces = lambda slot, side, frame: grads(slot, side, part, frame)
             block = lambda place, side: neighbour_block(pieces, place, side, frames, where)
@@ -470,7 +476,7 @@
             cells = cotangent[frame].astype(F32) + grown[:, frame * LANES : (frame + 1) * LANES]
             back[frame] = cells.astype(BF16)
 
-    weight_step(grads, frames, where, channels, out, padded, full, prologue)
+    weight_step(grads, frames, where, channels, out, padded, full, ready, sent, finish)
 
 
 def swap(values):
@@ -545,7 +551,13 @@
         ],
         (where, conv_second, mixer, *first_sums), (shifted, total), **conv_cost,
     )
-    second_sums = around(over_channels(parts))
+    padded_shape = jax.ShapeDtypeStruct((6 * channels, (frames * count + 2) * LANES), BF16)
+    (padded_inputs,) = call(
+        functools.partial(pad_kernel, frames), [padded_shape], (where, *every_input), reads=2000000
+    )
+    far = [hop(parts[k], "chan", k) for k in range(1, 4)]
+    far, padded_inputs = lax.optimization_barrier((far, padded_inputs))
+    second_sums = around(parts[0] + sum(values.astype(F32) for values in far))
     every_shape = jax.ShapeDtypeStruct((count, 2, *block), BF16)
     result, halo, every_second = call(
         functools.partial(third_kernel, frames, members),
@@ -553,41 +565,43 @@
         (where, mixer, *second_sums, *every_given, inputs),
         (pltpu.VMEM((4, 2, *block), F32), pltpu.VMEM((4, 2, *block), F32)), grant=24,
     )
-    halos = [halo] + [hop(halo, "chan", k) for k in range(1, 4)]
+    (padded_hidden,) = call(
+        functools.partial(pad_hidden_kernel, frames), [padded_shape], (where, hidden), reads=2000000
+    )
+    far = [hop(halo, "chan", k) for k in range(1, 4)]
+    far, padded_hidden = lax.optimization_barrier((far, padded_hidden))
+    halos = [halo] + far
     sides = with_sides(halos)
     (grad,) = call(
-        functools.partial(fourth_kernel, frames), [sums_shape],
+        functools.partial(fourth_kernel, frames), [cells_shape],
         (where, behind_second, norm, *sides), (wide_shifted,), **conv_cost,
     )
     grad_first, every_first = call(
-        functools.partial(fifth_kernel, frames, members), [cells_shape, every_shape],
+        functools.partial(fifth_kernel, frames, members),
+        [jax.ShapeDtypeStruct((2, *block), BF16), every_shape],
         (where, mixer, scale, *first_sums, *around(grad)),
     )
     rest = jnp.stack([values[1:-1] for values in halos[1:]])
     rest, grad_first = lax.optimization_barrier((rest, grad_first))
-    padded_shape = jax.ShapeDtypeStruct((6 * channels, (frames * count + 2) * LANES), BF16)
-    padded = pltpu.VMEM(padded_shape.shape, BF16)
+    far = [hop(grad_first, "chan", k) for k in range(1, 4)]
+    far = [jnp.stack([values[k] for values in far]) for k in range(2)]
+    near, _ = lax.optimization_barrier((hops(rest), far))
     full = pltpu.VMEM((-(-wide // LANES) * LANES + wide, cells * count), BF16)
     grad_shape = jax.ShapeDtypeStruct((27, channels, wide), F32)
-    grad_spec = pl.BlockSpec((9, channels, wide), lambda a: (a, 0, 0))
+    grad_spec = pl.BlockSpec(memory_space=pl.ANY)
+    staging = (pltpu.VMEM((3, 9, channels, wide), F32), pltpu.SemaphoreType.DMA((3,)))
     grad_cost = dict(flops=2 * 18 * channels * wide * cells * count * 2, reads=8000000)
     (second_grad,) = call(
         functools.partial(weight_kernel, frames), [grad_shape],
-        (where, hidden, every_second, *sides[2:], *with_sides(hops(rest))), (padded, full),
-        grid=(3,), specs=[grad_spec], grant=32, **grad_cost,
-    )
-    (padded_inputs,) = call(
-        functools.partial(pad_kernel, frames), [padded_shape], (where, *every_input), reads=2000000
-    )
-    rest = jnp.stack([hop(grad_first, "chan", k) for k in range(1, 4)])
-    near, (second_grad, padded_inputs) = lax.optimization_barrier(
-        (hops(rest), (second_grad, padded_inputs))
-    )
+        (where, padded_hidden, every_second, *sides[2:], *with_sides(near)), (full, *staging),
+        specs=[grad_spec], grant=32, **grad_cost,
+    )
+    near, second_grad = lax.optimization_barrier(([hop(far[0], "frame", k) for k in (1, 2)], second_grad))
     first_grad, input_grad = call(
         functools.partial(last_kernel, frames), [grad_shape, cells_shape],
-        (where, behind_first, given, padded_inputs, every_first, *with_sides([rest] + near)),
-        (full, wide_shifted), grid=(3,),
-        specs=[grad_spec, pl.BlockSpec(block, lambda a: (0, 0, 0))], grant=32, **grad_cost,
+        (where, behind_first, given, padded_inputs, every_first, *with_sides([far[0], *near, far[1]])),
+        (full, wide_shifted, *staging),
+        specs=[grad_spec, pl.BlockSpec(memory_space=pltpu.VMEM)], grant=32, **grad_cost,
     )
     return (restore(result), restore(input_grad), first_grad, second_grad)
 

time: 126 us -> 118 us (0.937)
  waiting for transfers between devices: 47 us -> 41.5 us
  starting transfers between devices: 49.9 us -> 46.1 us
    ppermute x33 -> x32, waiting for transfers between devices: 39.7 us -> 33.7 us  [hop(): return lax.ppermute(values, axis, [(i, i ^ step) for i in range(4)])]
    ppermute x33 -> x32, starting transfers between devices: 45 us -> 41.3 us  [hop(): return lax.ppermute(values, axis, [(i, i ^ step) for i in range(4)])]
    pallas_call x9 -> x10, Pallas kernels: 25.3 us -> 25.5 us  [call(): pl.pallas_call(kernel, out_shape=outs, in_specs=in_specs, out_specs=[vmem...]
    unnamed x12 -> x14, local copies, waits for them, and re-layouts: 2.9 us -> 2.9 us
  transfers between devices with their start and end apart: 64 -> 63, of which waited for: 34 -> 32; matrix products, arithmetic and copies ran while one was open for 0% -> 0% of each run, Pallas kernels for 6% -> 7%
where the time goes in v3:
time: 118 us; the launch traced here: 117 us
  starting transfers between devices  46.1 us (39%)
  waiting for transfers between devices  41.5 us (35%)
  Pallas kernels  25.5 us (22%)
  local copies, waits for them, and re-layouts  2.95 us (2%)
    ppermute x32, starting transfers between devices, hop(): return lax.ppermute(values, axis, [(i, i ^ step) for i in range(4)])  41.3 us
    ppermute x32, waiting for transfers between devices, hop(): return lax.ppermute(values, axis, [(i, i ^ step) for i in range(4)])  33.7 us
    pallas_call x10, Pallas kernels, call(): pl.pallas_call(kernel, out_shape=outs, in_specs=in_specs, out_specs=[vmem...  25.5 us
    ppermute x31, waiting for transfers between devices, swap(): return lax.ppermute(values, 'row', [(0, 1), (1, 0)])  7.84 us
    ppermute x31, starting transfers between devices, swap(): return lax.ppermute(values, 'row', [(0, 1), (1, 0)])  4.83 us
    unnamed x14, local copies, waits for them, and re-layouts  2.9 us
  transfers between devices with their start and end apart: 63, of which 32 were waited for; matrix products, arithmetic and copies ran while one was open for 0% of the time, Pallas kernels for 7%

profile of v3, /device:TPU:0, one launch (start us, length us, event | category | flops | bytes accessed | tf_op | source)
XLA Modules:
  0.0 117.4 jit_solution(6781975975783767060)
XLA Ops:
  0.6 3.0 %collective-permute-start = (bf16[3,80,128]{2,1,0:T(8,128)(2,1)}, bf16[3,80,128]{2,1,0:T(8,128)(2,1)S(1)}, u32[]{:S(2)}, u32[]{:S(2)}) collective-permute-start(bf16[3,80,128]{2,1,0:T(8,128)(2,1)} %bitcast.29), channel_id=1, source_target_pairs={{0,8},{8,0},{16,24},{24,16},{1,9},{9,1},{17,25},{25,17},{2,10},{10... | collective-permute-start | bytes 184328 | tf_op jit(solution)/shard_map/ppermute | solution.py:487
  3.6 1.5 %collective-permute-start.1 = (bf16[3,80,128]{2,1,0:T(8,128)(2,1)}, bf16[3,80,128]{2,1,0:T(8,128)(2,1)S(1)}, u32[]{:S(2)}, u32[]{:S(2)}) collective-permute-start(bf16[3,80,128]{2,1,0:T(8,128)(2,1)} %bitcast.30), channel_id=1, source_target_pairs={{0,16},{8,24},{16,0},{24,8},{1,17},{9,25},{17,1},{25,9},{2,18},{10... | collective-permute-start | bytes 184328 | tf_op jit(solution)/shard_map/ppermute | solution.py:487
  5.3 1.4 %copy-done = bf16[27,80,320]{2,1,0:T(8,128)(2,1)S(1)} copy-done((bf16[27,80,320]{2,1,0:T(8,128)(2,1)S(1)}, bf16[27,80,320]{2,1,0:T(8,128)(2,1)}, u32[]{:S(2)}) %copy-start) | copy-done | bytes 1382424
  6.7 1.4 %copy-done.2 = bf16[27,80,320]{2,1,0:T(8,128)(2,1)S(1)} copy-done((bf16[27,80,320]{2,1,0:T(8,128)(2,1)S(1)}, bf16[27,80,320]{2,1,0:T(8,128)(2,1)}, u32[]{:S(2)}) %copy-start.2) | copy-done | bytes 1382424
  9.1 1.4 %collective-permute-done.2.refs_1_ = bf16[3,80,128]{2,1,0:T(8,128)(2,1)S(1)} collective-permute-done((bf16[3,80,128]{2,1,0:T(8,128)(2,1)}, bf16[3,80,128]{2,1,0:T(8,128)(2,1)S(1)}, u32[]{:S(2)}, u32[]{:S(2)}) %collective-permute-start.2) | collective-permute-done | bytes 61472 | tf_op jit(solution)/shard_map/ppermute | solution.py:487
  12.3 1.4 %shard_map.85 = (f32[3,80,128]{2,1,0:T(8,128)S(1)}, bf16[3,80,128]{2,1,0:T(8,128)(2,1)S(1)}, bf16[3,80,128]{2,1,0:T(8,128)(2,1)S(1)}, bf16[3,80,128]{2,1,0:T(8,128)(2,1)S(1)}) custom-call(s32[3]{0:T(128)S(1)} %pad_add_fusion.where, bf16[3,80,128]{2,1,0:T(8,128)(2,1)S(1)} %collective-permute-done.3.refs_0_, ...), custom_call_target="tpu_custom_call" | custom-call | flops 353894400 | bytes 921600 | tf_op jit(solution)/shard_map/pallas_call | solution.py:179
  13.7 1.6 %collective-permute-start.10 = (bf16[3,80,128]{2,1,0:T(8,128)(2,1)S(1)}, bf16[3,80,128]{2,1,0:T(8,128)(2,1)S(1)}, u32[]{:S(2)}, u32[]{:S(2)}) collective-permute-start(bf16[3,80,128]{2,1,0:T(8,128)(2,1)S(1)} %get-tuple-element.65), channel_id=1, source_target_pairs={{0,1},{1,0},{2,3},{3,2},{4,5},{5,4},{6,7},{7,6},{8,9},{9,8},{10,11... | collective-permute-start | bytes 184328 | tf_op jit(solution)/shard_map/ppermute | solution.py:487
  15.3 2.6 %collective-permute-start.11 = (bf16[3,80,128]{2,1,0:T(8,128)(2,1)S(1)}, bf16[3,80,128]{2,1,0:T(8,128)(2,1)S(1)}, u32[]{:S(2)}, u32[]{:S(2)}) collective-permute-start(bf16[3,80,128]{2,1,0:T(8,128)(2,1)S(1)} %get-tuple-element.66), channel_id=1, source_target_pairs={{0,2},{1,3},{2,0},{3,1},{4,6},{5,7},{6,4},{7,5},{8,10},{9,11},{10,... | collective-permute-start | bytes 184328 | tf_op jit(solution)/shard_map/ppermute | solution.py:487
  18.9 1.5 %collective-permute-start.8 = (bf16[3,80,128]{2,1,0:T(8,128)(2,1)S(1)}, bf16[3,80,128]{2,1,0:T(8,128)(2,1)S(1)}, u32[]{:S(2)}, u32[]{:S(2)}) collective-permute-start(bf16[3,80,128]{2,1,0:T(8,128)(2,1)S(1)} %bitcast.37), channel_id=1, source_target_pairs={{0,16},{8,24},{16,0},{24,8},{1,17},{9,25},{17,1},{25,9},{2,18},{10... | collective-permute-start | bytes 184328 | tf_op jit(solution)/shard_map/ppermute | solution.py:487
  20.4 1.2 %collective-permute-start.9 = (bf16[3,80,128]{2,1,0:T(8,128)(2,1)S(1)}, bf16[3,80,128]{2,1,0:T(8,128)(2,1)S(1)}, u32[]{:S(2)}, u32[]{:S(2)}) collective-permute-start(bf16[3,80,128]{2,1,0:T(8,128)(2,1)S(1)} %bitcast.38), channel_id=1, source_target_pairs={{0,24},{8,16},{16,8},{24,0},{1,25},{9,17},{17,9},{25,1},{2,26},{10... | collective-permute-start | bytes 184328 | tf_op jit(solution)/shard_map/ppermute | solution.py:487
  21.9 2.1 %collective-permute-done.12 = bf16[3,80,128]{2,1,0:T(8,128)(2,1)S(1)} collective-permute-done((bf16[3,80,128]{2,1,0:T(8,128)(2,1)S(1)}, bf16[3,80,128]{2,1,0:T(8,128)(2,1)S(1)}, u32[]{:S(2)}, u32[]{:S(2)}) %collective-permute-start.12) | collective-permute-done | bytes 61472 | tf_op jit(solution)/shard_map/ppermute | solution.py:487
  24.1 1.5 %collective-permute-done.9.refs_2_ = bf16[3,80,128]{2,1,0:T(8,128)(2,1)S(1)} collective-permute-done((bf16[3,80,128]{2,1,0:T(8,128)(2,1)S(1)}, bf16[3,80,128]{2,1,0:T(8,128)(2,1)S(1)}, u32[]{:S(2)}, u32[]{:S(2)}) %collective-permute-start.9) | collective-permute-done | bytes 61472 | tf_op jit(solution)/shard_map/ppermute | solution.py:487
  25.5 1.2 %collective-permute-start.17 = (f32[3,80,128]{2,1,0:T(8,128)S(1)}, f32[3,80,128]{2,1,0:T(8,128)S(1)}, u32[]{:S(2)}, u32[]{:S(2)}) collective-permute-start(f32[3,80,128]{2,1,0:T(8,128)S(1)} %add_add_fusion.1.refs_7_.refs_15_), channel_id=1, source_target_pairs={{0,24},{8,16},{16,8},{24,0},{1,25},{9,17},{17,9},{25,1},{2,26},{10... | collective-permute-start | bytes 368648 | tf_op jit(solution)/shard_map/ppermute | solution.py:487
  27.5 1.5 %collective-permute-start.21 = (f32[3,80,128]{2,1,0:T(8,128)S(1)}, f32[3,80,128]{2,1,0:T(8,128)S(1)}, u32[]{:S(2)}, u32[]{:S(2)}) collective-permute-start(f32[3,80,128]{2,1,0:T(8,128)S(1)} %add_add_fusion.1.refs_7_.refs_15_), channel_id=1, source_target_pairs={{0,8},{8,0},{16,24},{24,16},{1,9},{9,1},{17,25},{25,17},{2,10},{10... | collective-permute-start | bytes 368648 | tf_op jit(solution)/shard_map/ppermute | solution.py:487
  29.0 2.4 %collective-permute-done.17.refs_1_.refs_9_ = f32[3,80,128]{2,1,0:T(8,128)S(1)} collective-permute-done((f32[3,80,128]{2,1,0:T(8,128)S(1)}, f32[3,80,128]{2,1,0:T(8,128)S(1)}, u32[]{:S(2)}, u32[]{:S(2)}) %collective-permute-start.17) | collective-permute-done | bytes 122912 | tf_op jit(solution)/shard_map/ppermute | solution.py:487
  31.4 1.2 %collective-permute-done.19.refs_3_.refs_11_ = f32[3,80,128]{2,1,0:T(8,128)S(1)} collective-permute-done((f32[3,80,128]{2,1,0:T(8,128)S(1)}, f32[3,80,128]{2,1,0:T(8,128)S(1)}, u32[]{:S(2)}, u32[]{:S(2)}) %collective-permute-start.19) | collective-permute-done | bytes 122912 | tf_op jit(solution)/shard_map/ppermute | solution.py:487
  34.1 2.4 %shard_map.86 = (bf16[4,2,3,80,128]{4,3,2,1,0:T(8,128)(2,1)S(1)}, f32[3,80,128]{2,1,0:T(8,128)S(1)}, f32[80,128]{1,0:T(8,128)S(1)}, f32[3,80,128]{2,1,0:T(8,128)...) custom-call(s32[3]{0:T(128)S(1)} %pad_add_fusion.where, ...), custom_call_target="tpu_custom_call" | custom-call | flops 353894400 | bytes 921600 | tf_op jit(solution)/shard_map/pallas_call | solution.py:179
  37.3 3.5 %collective-permute-start.25 = (bf16[3,80,128]{2,1,0:T(8,128)(2,1)S(1)}, bf16[3,80,128]{2,1,0:T(8,128)(2,1)S(1)}, u32[]{:S(2)}, u32[]{:S(2)}) collective-permute-start(bf16[3,80,128]{2,1,0:T(8,128)(2,1)S(1)} %get-tuple-element.74), channel_id=1, source_target_pairs={{0,2},{1,3},{2,0},{3,1},{4,6},{5,7},{6,4},{7,5},{8,10},{9,11},{10,... | collective-permute-start | bytes 184328 | tf_op jit(solution)/shard_map/ppermute | solution.py:487
  41.8 2.8 %collective-permute-done.25 = bf16[3,80,128]{2,1,0:T(8,128)(2,1)S(1)} collective-permute-done((bf16[3,80,128]{2,1,0:T(8,128)(2,1)S(1)}, bf16[3,80,128]{2,1,0:T(8,128)(2,1)S(1)}, u32[]{:S(2)}, u32[]{:S(2)}) %collective-permute-start.25) | collective-permute-done | bytes 61472 | tf_op jit(solution)/shard_map/ppermute | solution.py:487
  44.6 2.2 %collective-permute-done.26 = bf16[3,80,128]{2,1,0:T(8,128)(2,1)S(1)} collective-permute-done((bf16[3,80,128]{2,1,0:T(8,128)(2,1)S(1)}, bf16[3,80,128]{2,1,0:T(8,128)(2,1)S(1)}, u32[]{:S(2)}, u32[]{:S(2)}) %collective-permute-start.26) | collective-permute-done | bytes 61472 | tf_op jit(solution)/shard_map/ppermute | solution.py:487
  46.9 1.3 %collective-permute-start.27 = (f32[3,80,128]{2,1,0:T(8,128)S(1)}, f32[3,80,128]{2,1,0:T(8,128)S(1)}, u32[]{:S(2)}, u32[]{:S(2)}) collective-permute-start(f32[3,80,128]{2,1,0:T(8,128)S(1)} %add_add_fusion.refs_16_), channel_id=1, source_target_pairs={{0,24},{8,16},{16,8},{24,0},{1,25},{9,17},{17,9},{25,1},{2,26},{10... | collective-permute-start | bytes 368648 | tf_op jit(solution)/shard_map/ppermute | solution.py:487
  48.1 1.3 %collective-permute-start.29 = (f32[3,80,128]{2,1,0:T(8,128)S(1)}, f32[3,80,128]{2,1,0:T(8,128)S(1)}, u32[]{:S(2)}, u32[]{:S(2)}) collective-permute-start(f32[3,80,128]{2,1,0:T(8,128)S(1)} %add_add_fusion.refs_16_), channel_id=1, source_target_pairs={{0,16},{8,24},{16,0},{24,8},{1,17},{9,25},{17,1},{25,9},{2,18},{10... | collective-permute-start | bytes 368648 | tf_op jit(solution)/shard_map/ppermute | solution.py:487
  49.4 1.0 collective-permute-start.31
  52.2 1.0 collective-permute-done.27.refs_10_
  53.1 1.2 %collective-permute-done.29.refs_12_ = f32[3,80,128]{2,1,0:T(8,128)S(1)} collective-permute-done((f32[3,80,128]{2,1,0:T(8,128)S(1)}, f32[3,80,128]{2,1,0:T(8,128)S(1)}, u32[]{:S(2)}, u32[]{:S(2)}) %collective-permute-start.29) | collective-permute-done | bytes 122912 | tf_op jit(solution)/shard_map/ppermute | solution.py:487
  54.9 1.2 %collective-permute-done.15.refs_5_ = bf16[3,80,128]{2,1,0:T(8,128)(2,1)S(1)} collective-permute-done((bf16[3,80,128]{2,1,0:T(8,128)(2,1)S(1)}, bf16[3,80,128]{2,1,0:T(8,128)(2,1)S(1)}, u32[]{:S(2)}, u32[]{:S(2)}) %collective-permute-start.15) | collective-permute-done | bytes 61472 | tf_op jit(solution)/shard_map/ppermute | solution.py:483
  56.1 2.8 %shard_map.88 = (bf16[3,80,128]{2,1,0:T(8,128)(2,1)}, bf16[5,80,128]{2,1,0:T(8,128)(2,1)S(1)}, bf16[4,2,3,80,128]{4,3,2,1,0:T(8,128)(2,1)S(1)}) custom-call(s32[3]{0:T(128)S(1)} %pad_add_fusion.where, bf16[3,80,128]{2,1,0:T(8,128)(2,1)S(1)} %bitcast.35, bf16[3,80,128]{2,1,0:T(8,128)(2,1)S(1)} %collective-permute-done.13.refs_1_, ...), custom_call_target="tpu_custom_call" | custom-call | tf_op jit(solution)/shard_map/pallas_call | solution.py:179
  58.9 1.1 collective-permute-start.34
  60.0 1.4 %collective-permute-start.35 = (bf16[5,80,128]{2,1,0:T(8,128)(2,1)S(1)}, bf16[5,80,128]{2,1,0:T(8,128)(2,1)S(1)}, u32[]{:S(2)}, u32[]{:S(2)}) collective-permute-start(bf16[5,80,128]{2,1,0:T(8,128)(2,1)S(1)} %get-tuple-element.80.refs_7_), channel_id=1, source_target_pairs={{0,2},{1,3},{2,0},{3,1},{4,6},{5,7},{6,4},{7,5},{8,10},{9,11},{10,... | collective-permute-start | bytes 307208 | tf_op jit(solution)/shard_map/ppermute | solution.py:487
  61.4 1.9 %collective-permute-start.36 = (bf16[5,80,128]{2,1,0:T(8,128)(2,1)S(1)}, bf16[5,80,128]{2,1,0:T(8,128)(2,1)S(1)}, u32[]{:S(2)}, u32[]{:S(2)}) collective-permute-start(bf16[5,80,128]{2,1,0:T(8,128)(2,1)S(1)} %get-tuple-element.80.refs_7_), channel_id=1, source_target_pairs={{0,3},{1,2},{2,1},{3,0},{4,7},{5,6},{6,5},{7,4},{8,11},{9,10},{10,... | collective-permute-start | bytes 307208 | tf_op jit(solution)/shard_map/ppermute | solution.py:487
  64.3 1.4 %collective-permute-done.34.refs_5_.refs_11_ = bf16[5,80,128]{2,1,0:T(8,128)(2,1)S(1)} collective-permute-done((bf16[5,80,128]{2,1,0:T(8,128)(2,1)S(1)}, bf16[5,80,128]{2,1,0:T(8,128)(2,1)S(1)}, u32[]{:S(2)}, u32[]{:S(2)}) %collective-permute-start.34) | collective-permute-done | bytes 102432 | tf_op jit(solution)/shard_map/ppermute | solution.py:487
  65.6 5.0 %collective-permute-done.35.refs_3_.refs_9_ = bf16[5,80,128]{2,1,0:T(8,128)(2,1)S(1)} collective-permute-done((bf16[5,80,128]{2,1,0:T(8,128)(2,1)S(1)}, bf16[5,80,128]{2,1,0:T(8,128)(2,1)S(1)}, u32[]{:S(2)}, u32[]{:S(2)}) %collective-permute-start.35) | collective-permute-done | bytes 102432 | tf_op jit(solution)/shard_map/ppermute | solution.py:487
  72.5 2.0 %shard_map.90.refs_7_ = bf16[3,80,128]{2,1,0:T(8,128)(2,1)S(1)} custom-call(s32[3]{0:T(128)S(1)} %pad_add_fusion.where, bf16[5,80,128]{2,1,0:T(8,128)(2,1)S(1)} %collective-permute-done.37.refs_0_.refs_6_, bf16[5,80,128]{2,1,0:T(8,128)(2,1)S(1)} %collective-permute-done.36.refs_1_.refs_7_, bf16[5,80,128]{2,1,0:T(8,128)(2,1)S(1)} %collective-permute-done.38.refs_2_.refs_8_, ...), custom_call_target="tpu_custom_call" | custom-call | flops 353894400 | bytes 921600 | tf_op jit(solution)/shard_map/pallas_call | solution.py:179
  74.5 1.3 %collective-permute-start.41 = (bf16[3,80,128]{2,1,0:T(8,128)(2,1)S(1)}, bf16[3,80,128]{2,1,0:T(8,128)(2,1)S(1)}, u32[]{:S(2)}, u32[]{:S(2)}) collective-permute-start(bf16[3,80,128]{2,1,0:T(8,128)(2,1)S(1)} %shard_map.90.refs_7_), channel_id=1, source_target_pairs={{0,24},{8,16},{16,8},{24,0},{1,25},{9,17},{17,9},{25,1},{2,26},{10... | collective-permute-start | bytes 184328 | tf_op jit(solution)/shard_map/ppermute | solution.py:487
  75.8 1.5 %collective-permute-start.43 = (bf16[3,80,128]{2,1,0:T(8,128)(2,1)S(1)}, bf16[3,80,128]{2,1,0:T(8,128)(2,1)S(1)}, u32[]{:S(2)}, u32[]{:S(2)}) collective-permute-start(bf16[3,80,128]{2,1,0:T(8,128)(2,1)S(1)} %shard_map.90.refs_7_), channel_id=1, source_target_pairs={{0,16},{8,24},{16,0},{24,8},{1,17},{9,25},{17,1},{25,9},{2,18},{10... | collective-permute-start | bytes 184328 | tf_op jit(solution)/shard_map/ppermute | solution.py:487
  78.0 1.9 %collective-permute-done.41.refs_1_ = bf16[3,80,128]{2,1,0:T(8,128)(2,1)S(1)} collective-permute-done((bf16[3,80,128]{2,1,0:T(8,128)(2,1)S(1)}, bf16[3,80,128]{2,1,0:T(8,128)(2,1)S(1)}, u32[]{:S(2)}, u32[]{:S(2)}) %collective-permute-start.41) | collective-permute-done | bytes 61472 | tf_op jit(solution)/shard_map/ppermute | solution.py:487
  82.7 1.3 %shard_map.91 = (bf16[2,3,80,128]{3,2,1,0:T(8,128)(2,1)S(1)}, bf16[4,2,3,80,128]{4,3,2,1,0:T(8,128)(2,1)S(1)}) custom-call(s32[3]{0:T(128)S(1)} %pad_add_fusion.where, bf16[3,80,128]{2,1,0:T(8,128)(2,1)S(1)} %collective-permute-done.42.refs_0_, bf16[3,80,128]{2,1,0:T(8,128)(2,1)S(1)} %collective-permute-done.41.refs_1_, ...), custom_call_target="tpu_custom_call" | custom-call | tf_op jit(solution)/shard_map/pallas_call | solution.py:179
  84.0 1.8 %collective-permute-start.48 = (bf16[2,3,80,128]{3,2,1,0:T(8,128)(2,1)S(1)}, bf16[2,3,80,128]{3,2,1,0:T(8,128)(2,1)S(1)}, u32[]{:S(2)}, u32[]{:S(2)}) collective-permute-start(bf16[2,3,80,128]{3,2,1,0:T(8,128)(2,1)S(1)} %get-tuple-element.89), channel_id=1, source_target_pairs={{0,1},{1,0},{2,3},{3,2},{4,5},{5,4},{6,7},{7,6},{8,9},{9,8},{10,11... | collective-permute-start | bytes 368648 | tf_op jit(solution)/shard_map/ppermute | solution.py:487
  85.8 1.2 %collective-permute-start.49 = (bf16[2,3,80,128]{3,2,1,0:T(8,128)(2,1)S(1)}, bf16[2,3,80,128]{3,2,1,0:T(8,128)(2,1)S(1)}, u32[]{:S(2)}, u32[]{:S(2)}) collective-permute-start(bf16[2,3,80,128]{3,2,1,0:T(8,128)(2,1)S(1)} %get-tuple-element.89), channel_id=1, source_target_pairs={{0,2},{1,3},{2,0},{3,1},{4,6},{5,7},{6,4},{7,5},{8,10},{9,11},{10,... | collective-permute-start | bytes 368648 | tf_op jit(solution)/shard_map/ppermute | solution.py:487
  87.0 1.4 %collective-permute-start.50 = (bf16[2,3,80,128]{3,2,1,0:T(8,128)(2,1)S(1)}, bf16[2,3,80,128]{3,2,1,0:T(8,128)(2,1)S(1)}, u32[]{:S(2)}, u32[]{:S(2)}) collective-permute-start(bf16[2,3,80,128]{3,2,1,0:T(8,128)(2,1)S(1)} %get-tuple-element.89), channel_id=1, source_target_pairs={{0,3},{1,2},{2,1},{3,0},{4,7},{5,6},{6,5},{7,4},{8,11},{9,10},{10,... | collective-permute-start | bytes 368648 | tf_op jit(solution)/shard_map/ppermute | solution.py:487
  88.5 1.2 %collective-permute-start.54 = (bf16[3,3,80,128]{3,2,1,0:T(8,128)(2,1)S(1)}, bf16[3,3,80,128]{3,2,1,0:T(8,128)(2,1)S(1)}, u32[]{:S(2)}, u32[]{:S(2)}) collective-permute-start(bf16[3,3,80,128]{3,2,1,0:T(8,128)(2,1)S(1)} %pad_maximum_fusion), channel_id=1, source_target_pairs={{0,8},{8,0},{16,24},{24,16},{1,9},{9,1},{17,25},{25,17},{2,10},{10... | collective-permute-start | bytes 552968 | tf_op jit(solution)/shard_map/ppermute | solution.py:487
  90.4 1.1 collective-permute-done.48
  91.4 1.2 %collective-permute-start.56 = (bf16[3,3,80,128]{3,2,1,0:T(8,128)(2,1)S(1)}, bf16[3,3,80,128]{3,2,1,0:T(8,128)(2,1)S(1)}, u32[]{:S(2)}, u32[]{:S(2)}) collective-permute-start(bf16[3,3,80,128]{3,2,1,0:T(8,128)(2,1)S(1)} %pad_maximum_fusion), channel_id=1, source_target_pairs={{0,24},{8,16},{16,8},{24,0},{1,25},{9,17},{17,9},{25,1},{2,26},{10... | collective-permute-start | bytes 552968 | tf_op jit(solution)/shard_map/ppermute | solution.py:487
  92.6 5.5 %collective-permute-done.49 = bf16[2,3,80,128]{3,2,1,0:T(8,128)(2,1)S(1)} collective-permute-done((bf16[2,3,80,128]{3,2,1,0:T(8,128)(2,1)S(1)}, bf16[2,3,80,128]{3,2,1,0:T(8,128)(2,1)S(1)}, u32[]{:S(2)}, u32[]{:S(2)}) %collective-permute-start.49) | collective-permute-done | bytes 122912 | tf_op jit(solution)/shard_map/ppermute | solution.py:487
  98.3 1.2 %collective-permute-done.55.refs_3_ = bf16[3,3,80,128]{3,2,1,0:T(8,128)(2,1)S(1)} collective-permute-done((bf16[3,3,80,128]{3,2,1,0:T(8,128)(2,1)S(1)}, bf16[3,3,80,128]{3,2,1,0:T(8,128)(2,1)S(1)}, u32[]{:S(2)}, u32[]{:S(2)}) %collective-permute-start.55) | collective-permute-done | bytes 184352 | tf_op jit(solution)/shard_map/ppermute | solution.py:487
  100.0 1.0 collective-permute-start.52
  102.3 5.8 %shard_map.92 = f32[27,80,320]{2,1,0:T(8,128)} custom-call(s32[3]{0:T(128)S(1)} %pad_add_fusion.where, bf16[3,3,80,128]{3,2,1,0:T(8,128)(2,1)S(1)} %collective-permute-done.57.refs_0_, bf16[3,3,80,128]{3,2,1,0:T(8,128)(2,1)S(1)} %collective-permute-done.56.refs_1_, bf16[3,3,80,128]{3,2,1,0:T(8,128)(2,1)S(1)} %collective-permute-done.58.refs_2_, ...), custom_call_target="tpu_custom_call" | custom-call | flops 2831155200 | bytes 8000000 | tf_op jit(solution)/shard_map/pallas_call | solution.py:179
  109.9 7.3 %shard_map.93 = (f32[27,80,320]{2,1,0:T(8,128)}, bf16[3,80,128]{2,1,0:T(8,128)(2,1)}) custom-call(s32[3]{0:T(128)S(1)} %pad_add_fusion.where, bf16[3,3,80,128]{3,2,1,0:T(8,128)(2,1)S(1)} %collective-permute-done.51.refs_0_, bf16[3,3,80,128]{3,2,1,0:T(8,128)(2,1)S(1)} %pad_maximum_fusion.1.refs_1_, ...), custom_call_target="tpu_custom_call" | custom-call | flops 2831155200 | bytes 8000000 | tf_op jit(solution)/shard_map/pallas_call | solution.py:179
  (113 shorter events, 21.2 us)
Async XLA Ops:
  0.6 8.4 %collective-permute-start = (bf16[3,80,128]{2,1,0:T(8,128)(2,1)}, bf16[3,80,128]{2,1,0:T(8,128)(2,1)S(1)}, u32[]{:S(2)}, u32[]{:S(2)}) collective-permute-start(bf16[3,80,128]{2,1,0:T(8,128)(2,1)} %bitcast.29), channel_id=1, source_target_pairs={{0,8},{8,0},{16,24},{24,16},{1,9},{9,1},{17,25},{25,17},{2,10},{10... | collective-permute-start | bytes 184328 | tf_op jit(solution)/shard_map/ppermute | solution.py:487
  3.6 5.4 %collective-permute-start.1 = (bf16[3,80,128]{2,1,0:T(8,128)(2,1)}, bf16[3,80,128]{2,1,0:T(8,128)(2,1)S(1)}, u32[]{:S(2)}, u32[]{:S(2)}) collective-permute-start(bf16[3,80,128]{2,1,0:T(8,128)(2,1)} %bitcast.30), channel_id=1, source_target_pairs={{0,16},{8,24},{16,0},{24,8},{1,17},{9,25},{17,1},{25,9},{2,18},{10... | collective-permute-start | bytes 184328 | tf_op jit(solution)/shard_map/ppermute | solution.py:487
  5.2 5.3 %collective-permute-start.2 = (bf16[3,80,128]{2,1,0:T(8,128)(2,1)}, bf16[3,80,128]{2,1,0:T(8,128)(2,1)S(1)}, u32[]{:S(2)}, u32[]{:S(2)}) collective-permute-start(bf16[3,80,128]{2,1,0:T(8,128)(2,1)} %bitcast.31), channel_id=1, source_target_pairs={{0,24},{8,16},{16,8},{24,0},{1,25},{9,17},{17,9},{25,1},{2,26},{10... | collective-permute-start | bytes 184328 | tf_op jit(solution)/shard_map/ppermute | solution.py:487
  5.2 5.8 %collective-permute-start.6 = (bf16[3,80,128]{2,1,0:T(8,128)(2,1)}, bf16[3,80,128]{2,1,0:T(8,128)(2,1)S(1)}, u32[]{:S(2)}, u32[]{:S(2)}) collective-permute-start(bf16[3,80,128]{2,1,0:T(8,128)(2,1)} %bitcast.32), channel_id=1, source_target_pairs={{0,4},{4,0},{1,5},{5,1},{2,6},{6,2},{3,7},{7,3},{8,12},{12,8},{9,1... | collective-permute-start | bytes 184328 | tf_op jit(solution)/shard_map/ppermute | solution.py:483
  13.7 6.7 %collective-permute-start.10 = (bf16[3,80,128]{2,1,0:T(8,128)(2,1)S(1)}, bf16[3,80,128]{2,1,0:T(8,128)(2,1)S(1)}, u32[]{:S(2)}, u32[]{:S(2)}) collective-permute-start(bf16[3,80,128]{2,1,0:T(8,128)(2,1)S(1)} %get-tuple-element.65), channel_id=1, source_target_pairs={{0,1},{1,0},{2,3},{3,2},{4,5},{5,4},{6,7},{7,6},{8,9},{9,8},{10,11... | collective-permute-start | bytes 184328 | tf_op jit(solution)/shard_map/ppermute | solution.py:487
  15.3 6.6 %collective-permute-start.11 = (bf16[3,80,128]{2,1,0:T(8,128)(2,1)S(1)}, bf16[3,80,128]{2,1,0:T(8,128)(2,1)S(1)}, u32[]{:S(2)}, u32[]{:S(2)}) collective-permute-start(bf16[3,80,128]{2,1,0:T(8,128)(2,1)S(1)} %get-tuple-element.66), channel_id=1, source_target_pairs={{0,2},{1,3},{2,0},{3,1},{4,6},{5,7},{6,4},{7,5},{8,10},{9,11},{10,... | collective-permute-start | bytes 184328 | tf_op jit(solution)/shard_map/ppermute | solution.py:487
  17.9 6.1 %collective-permute-start.12 = (bf16[3,80,128]{2,1,0:T(8,128)(2,1)S(1)}, bf16[3,80,128]{2,1,0:T(8,128)(2,1)S(1)}, u32[]{:S(2)}, u32[]{:S(2)}) collective-permute-start(bf16[3,80,128]{2,1,0:T(8,128)(2,1)S(1)} %get-tuple-element.67), channel_id=1, source_target_pairs={{0,3},{1,2},{2,1},{3,0},{4,7},{5,6},{6,5},{7,4},{8,11},{9,10},{10,... | collective-permute-start | bytes 184328 | tf_op jit(solution)/shard_map/ppermute | solution.py:487
  18.1 5.9 %collective-permute-start.7 = (bf16[3,80,128]{2,1,0:T(8,128)(2,1)S(1)}, bf16[3,80,128]{2,1,0:T(8,128)(2,1)S(1)}, u32[]{:S(2)}, u32[]{:S(2)}) collective-permute-start(bf16[3,80,128]{2,1,0:T(8,128)(2,1)S(1)} %bitcast.36), channel_id=1, source_target_pairs={{0,8},{8,0},{16,24},{24,16},{1,9},{9,1},{17,25},{25,17},{2,10},{10... | collective-permute-start | bytes 184328 | tf_op jit(solution)/shard_map/ppermute | solution.py:487
  18.9 5.2 %collective-permute-start.8 = (bf16[3,80,128]{2,1,0:T(8,128)(2,1)S(1)}, bf16[3,80,128]{2,1,0:T(8,128)(2,1)S(1)}, u32[]{:S(2)}, u32[]{:S(2)}) collective-permute-start(bf16[3,80,128]{2,1,0:T(8,128)(2,1)S(1)} %bitcast.37), channel_id=1, source_target_pairs={{0,16},{8,24},{16,0},{24,8},{1,17},{9,25},{17,1},{25,9},{2,18},{10... | collective-permute-start | bytes 184328 | tf_op jit(solution)/shard_map/ppermute | solution.py:487
  20.4 5.1 %collective-permute-start.9 = (bf16[3,80,128]{2,1,0:T(8,128)(2,1)S(1)}, bf16[3,80,128]{2,1,0:T(8,128)(2,1)S(1)}, u32[]{:S(2)}, u32[]{:S(2)}) collective-permute-start(bf16[3,80,128]{2,1,0:T(8,128)(2,1)S(1)} %bitcast.38), channel_id=1, source_target_pairs={{0,24},{8,16},{16,8},{24,0},{1,25},{9,17},{17,9},{25,1},{2,26},{10... | collective-permute-start | bytes 184328 | tf_op jit(solution)/shard_map/ppermute | solution.py:487
  25.5 5.9 %collective-permute-start.17 = (f32[3,80,128]{2,1,0:T(8,128)S(1)}, f32[3,80,128]{2,1,0:T(8,128)S(1)}, u32[]{:S(2)}, u32[]{:S(2)}) collective-permute-start(f32[3,80,128]{2,1,0:T(8,128)S(1)} %add_add_fusion.1.refs_7_.refs_15_), channel_id=1, source_target_pairs={{0,24},{8,16},{16,8},{24,0},{1,25},{9,17},{17,9},{25,1},{2,26},{10... | collective-permute-start | bytes 368648 | tf_op jit(solution)/shard_map/ppermute | solution.py:487
  26.7 5.9 %collective-permute-start.19 = (f32[3,80,128]{2,1,0:T(8,128)S(1)}, f32[3,80,128]{2,1,0:T(8,128)S(1)}, u32[]{:S(2)}, u32[]{:S(2)}) collective-permute-start(f32[3,80,128]{2,1,0:T(8,128)S(1)} %add_add_fusion.1.refs_7_.refs_15_), channel_id=1, source_target_pairs={{0,16},{8,24},{16,0},{24,8},{1,17},{9,25},{17,1},{25,9},{2,18},{10... | collective-permute-start | bytes 368648 | tf_op jit(solution)/shard_map/ppermute | solution.py:487
  27.5 5.1 %collective-permute-start.21 = (f32[3,80,128]{2,1,0:T(8,128)S(1)}, f32[3,80,128]{2,1,0:T(8,128)S(1)}, u32[]{:S(2)}, u32[]{:S(2)}) collective-permute-start(f32[3,80,128]{2,1,0:T(8,128)S(1)} %add_add_fusion.1.refs_7_.refs_15_), channel_id=1, source_target_pairs={{0,8},{8,0},{16,24},{24,16},{1,9},{9,1},{17,25},{25,17},{2,10},{10... | collective-permute-start | bytes 368648 | tf_op jit(solution)/shard_map/ppermute | solution.py:487
  29.0 4.1 %collective-permute-start.23 = (f32[3,80,128]{2,1,0:T(8,128)S(1)}, f32[3,80,128]{2,1,0:T(8,128)S(1)}, u32[]{:S(2)}, u32[]{:S(2)}) collective-permute-start(f32[3,80,128]{2,1,0:T(8,128)S(1)} %add_add_fusion.1.refs_7_.refs_15_), channel_id=1, source_target_pairs={{0,4},{4,0},{1,5},{5,1},{2,6},{6,2},{3,7},{7,3},{8,12},{12,8},{9,1... | collective-permute-start | bytes 368648 | tf_op jit(solution)/shard_map/ppermute | solution.py:483
  31.4 1.7 %collective-permute-start.18 = (f32[3,80,128]{2,1,0:T(8,128)S(1)}, f32[3,80,128]{2,1,0:T(8,128)S(1)}, u32[]{:S(2)}, u32[]{:S(2)}) collective-permute-start(f32[3,80,128]{2,1,0:T(8,128)S(1)} %collective-permute-done.17.refs_1_.refs_9_), channel_id=1, source_target_pairs={{0,4},{4,0},{1,5},{5,1},{2,6},{6,2},{3,7},{7,3},{8,12},{12,8},{9,1... | collective-permute-start | bytes 368648 | tf_op jit(solution)/shard_map/ppermute | solution.py:483
  36.5 5.3 %collective-permute-start.24 = (bf16[3,80,128]{2,1,0:T(8,128)(2,1)S(1)}, bf16[3,80,128]{2,1,0:T(8,128)(2,1)S(1)}, u32[]{:S(2)}, u32[]{:S(2)}) collective-permute-start(bf16[3,80,128]{2,1,0:T(8,128)(2,1)S(1)} %get-tuple-element.73), channel_id=1, source_target_pairs={{0,1},{1,0},{2,3},{3,2},{4,5},{5,4},{6,7},{7,6},{8,9},{9,8},{10,11... | collective-permute-start | bytes 184328 | tf_op jit(solution)/shard_map/ppermute | solution.py:487
  37.3 7.4 %collective-permute-start.25 = (bf16[3,80,128]{2,1,0:T(8,128)(2,1)S(1)}, bf16[3,80,128]{2,1,0:T(8,128)(2,1)S(1)}, u32[]{:S(2)}, u32[]{:S(2)}) collective-permute-start(bf16[3,80,128]{2,1,0:T(8,128)(2,1)S(1)} %get-tuple-element.74), channel_id=1, source_target_pairs={{0,2},{1,3},{2,0},{3,1},{4,6},{5,7},{6,4},{7,5},{8,10},{9,11},{10,... | collective-permute-start | bytes 184328 | tf_op jit(solution)/shard_map/ppermute | solution.py:487
  40.7 6.1 %collective-permute-start.26 = (bf16[3,80,128]{2,1,0:T(8,128)(2,1)S(1)}, bf16[3,80,128]{2,1,0:T(8,128)(2,1)S(1)}, u32[]{:S(2)}, u32[]{:S(2)}) collective-permute-start(bf16[3,80,128]{2,1,0:T(8,128)(2,1)S(1)} %get-tuple-element.75), channel_id=1, source_target_pairs={{0,3},{1,2},{2,1},{3,0},{4,7},{5,6},{6,5},{7,4},{8,11},{9,10},{10,... | collective-permute-start | bytes 184328 | tf_op jit(solution)/shard_map/ppermute | solution.py:487
  46.9 6.3 %collective-permute-start.27 = (f32[3,80,128]{2,1,0:T(8,128)S(1)}, f32[3,80,128]{2,1,0:T(8,128)S(1)}, u32[]{:S(2)}, u32[]{:S(2)}) collective-permute-start(f32[3,80,128]{2,1,0:T(8,128)S(1)} %add_add_fusion.refs_16_), channel_id=1, source_target_pairs={{0,24},{8,16},{16,8},{24,0},{1,25},{9,17},{17,9},{25,1},{2,26},{10... | collective-permute-start | bytes 368648 | tf_op jit(solution)/shard_map/ppermute | solution.py:487
  48.1 6.2 %collective-permute-start.29 = (f32[3,80,128]{2,1,0:T(8,128)S(1)}, f32[3,80,128]{2,1,0:T(8,128)S(1)}, u32[]{:S(2)}, u32[]{:S(2)}) collective-permute-start(f32[3,80,128]{2,1,0:T(8,128)S(1)} %add_add_fusion.refs_16_), channel_id=1, source_target_pairs={{0,16},{8,24},{16,0},{24,8},{1,17},{9,25},{17,1},{25,9},{2,18},{10... | collective-permute-start | bytes 368648 | tf_op jit(solution)/shard_map/ppermute | solution.py:487
  49.4 4.9 %collective-permute-start.31 = (f32[3,80,128]{2,1,0:T(8,128)S(1)}, f32[3,80,128]{2,1,0:T(8,128)S(1)}, u32[]{:S(2)}, u32[]{:S(2)}) collective-permute-start(f32[3,80,128]{2,1,0:T(8,128)S(1)} %add_add_fusion.refs_16_), channel_id=1, source_target_pairs={{0,8},{8,0},{16,24},{24,16},{1,9},{9,1},{17,25},{25,17},{2,10},{10... | collective-permute-start | bytes 368648 | tf_op jit(solution)/shard_map/ppermute | solution.py:487
  51.7 3.2 %collective-permute-start.14 = (bf16[3,80,128]{2,1,0:T(8,128)(2,1)S(1)}, bf16[3,80,128]{2,1,0:T(8,128)(2,1)S(1)}, u32[]{:S(2)}, u32[]{:S(2)}) collective-permute-start(bf16[3,80,128]{2,1,0:T(8,128)(2,1)S(1)} %collective-permute-done.8.refs_4_), channel_id=1, source_target_pairs={{0,4},{4,0},{1,5},{5,1},{2,6},{6,2},{3,7},{7,3},{8,12},{12,8},{9,1... | collective-permute-start | bytes 184328 | tf_op jit(solution)/shard_map/ppermute | solution.py:483
  51.8 4.3 %collective-permute-start.33 = (f32[3,80,128]{2,1,0:T(8,128)S(1)}, f32[3,80,128]{2,1,0:T(8,128)S(1)}, u32[]{:S(2)}, u32[]{:S(2)}) collective-permute-start(f32[3,80,128]{2,1,0:T(8,128)S(1)} %add_add_fusion.refs_16_), channel_id=1, source_target_pairs={{0,4},{4,0},{1,5},{5,1},{2,6},{6,2},{3,7},{7,3},{8,12},{12,8},{9,1... | collective-permute-start | bytes 368648 | tf_op jit(solution)/shard_map/ppermute | solution.py:483
  53.1 3.0 %collective-permute-start.28 = (f32[3,80,128]{2,1,0:T(8,128)S(1)}, f32[3,80,128]{2,1,0:T(8,128)S(1)}, u32[]{:S(2)}, u32[]{:S(2)}) collective-permute-start(f32[3,80,128]{2,1,0:T(8,128)S(1)} %collective-permute-done.27.refs_10_), channel_id=1, source_target_pairs={{0,4},{4,0},{1,5},{5,1},{2,6},{6,2},{3,7},{7,3},{8,12},{12,8},{9,1... | collective-permute-start | bytes 368648 | tf_op jit(solution)/shard_map/ppermute | solution.py:483
  54.4 1.8 %collective-permute-start.30 = (f32[3,80,128]{2,1,0:T(8,128)S(1)}, f32[3,80,128]{2,1,0:T(8,128)S(1)}, u32[]{:S(2)}, u32[]{:S(2)}) collective-permute-start(f32[3,80,128]{2,1,0:T(8,128)S(1)} %collective-permute-done.29.refs_12_), channel_id=1, source_target_pairs={{0,4},{4,0},{1,5},{5,1},{2,6},{6,2},{3,7},{7,3},{8,12},{12,8},{9,1... | collective-permute-start | bytes 368648 | tf_op jit(solution)/shard_map/ppermute | solution.py:483
  54.4 1.8 %collective-permute-start.32 = (f32[3,80,128]{2,1,0:T(8,128)S(1)}, f32[3,80,128]{2,1,0:T(8,128)S(1)}, u32[]{:S(2)}, u32[]{:S(2)}) collective-permute-start(f32[3,80,128]{2,1,0:T(8,128)S(1)} %collective-permute-done.31.refs_14_), channel_id=1, source_target_pairs={{0,4},{4,0},{1,5},{5,1},{2,6},{6,2},{3,7},{7,3},{8,12},{12,8},{9,1... | collective-permute-start | bytes 368648 | tf_op jit(solution)/shard_map/ppermute | solution.py:483
  58.9 6.7 %collective-permute-start.34 = (bf16[5,80,128]{2,1,0:T(8,128)(2,1)S(1)}, bf16[5,80,128]{2,1,0:T(8,128)(2,1)S(1)}, u32[]{:S(2)}, u32[]{:S(2)}) collective-permute-start(bf16[5,80,128]{2,1,0:T(8,128)(2,1)S(1)} %get-tuple-element.80.refs_7_), channel_id=1, source_target_pairs={{0,1},{1,0},{2,3},{3,2},{4,5},{5,4},{6,7},{7,6},{8,9},{9,8},{10,11... | collective-permute-start | bytes 307208 | tf_op jit(solution)/shard_map/ppermute | solution.py:487
  60.0 10.6 %collective-permute-start.35 = (bf16[5,80,128]{2,1,0:T(8,128)(2,1)S(1)}, bf16[5,80,128]{2,1,0:T(8,128)(2,1)S(1)}, u32[]{:S(2)}, u32[]{:S(2)}) collective-permute-start(bf16[5,80,128]{2,1,0:T(8,128)(2,1)S(1)} %get-tuple-element.80.refs_7_), channel_id=1, source_target_pairs={{0,2},{1,3},{2,0},{3,1},{4,6},{5,7},{6,4},{7,5},{8,10},{9,11},{10,... | collective-permute-start | bytes 307208 | tf_op jit(solution)/shard_map/ppermute | solution.py:487
  61.4 9.2 %collective-permute-start.36 = (bf16[5,80,128]{2,1,0:T(8,128)(2,1)S(1)}, bf16[5,80,128]{2,1,0:T(8,128)(2,1)S(1)}, u32[]{:S(2)}, u32[]{:S(2)}) collective-permute-start(bf16[5,80,128]{2,1,0:T(8,128)(2,1)S(1)} %get-tuple-element.80.refs_7_), channel_id=1, source_target_pairs={{0,3},{1,2},{2,1},{3,0},{4,7},{5,6},{6,5},{7,4},{8,11},{9,10},{10,... | collective-permute-start | bytes 307208 | tf_op jit(solution)/shard_map/ppermute | solution.py:487
  64.2 7.0 %collective-permute-start.40 = (bf16[5,80,128]{2,1,0:T(8,128)(2,1)S(1)}, bf16[5,80,128]{2,1,0:T(8,128)(2,1)S(1)}, u32[]{:S(2)}, u32[]{:S(2)}) collective-permute-start(bf16[5,80,128]{2,1,0:T(8,128)(2,1)S(1)} %get-tuple-element.80.refs_7_), channel_id=1, source_target_pairs={{0,4},{4,0},{1,5},{5,1},{2,6},{6,2},{3,7},{7,3},{8,12},{12,8},{9,1... | collective-permute-start | bytes 307208 | tf_op jit(solution)/shard_map/ppermute | solution.py:483
  74.5 5.5 %collective-permute-start.41 = (bf16[3,80,128]{2,1,0:T(8,128)(2,1)S(1)}, bf16[3,80,128]{2,1,0:T(8,128)(2,1)S(1)}, u32[]{:S(2)}, u32[]{:S(2)}) collective-permute-start(bf16[3,80,128]{2,1,0:T(8,128)(2,1)S(1)} %shard_map.90.refs_7_), channel_id=1, source_target_pairs={{0,24},{8,16},{16,8},{24,0},{1,25},{9,17},{17,9},{25,1},{2,26},{10... | collective-permute-start | bytes 184328 | tf_op jit(solution)/shard_map/ppermute | solution.py:487
  75.8 5.0 %collective-permute-start.43 = (bf16[3,80,128]{2,1,0:T(8,128)(2,1)S(1)}, bf16[3,80,128]{2,1,0:T(8,128)(2,1)S(1)}, u32[]{:S(2)}, u32[]{:S(2)}) collective-permute-start(bf16[3,80,128]{2,1,0:T(8,128)(2,1)S(1)} %shard_map.90.refs_7_), channel_id=1, source_target_pairs={{0,16},{8,24},{16,0},{24,8},{1,17},{9,25},{17,1},{25,9},{2,18},{10... | collective-permute-start | bytes 184328 | tf_op jit(solution)/shard_map/ppermute | solution.py:487
  77.2 4.2 %collective-permute-start.45 = (bf16[3,80,128]{2,1,0:T(8,128)(2,1)S(1)}, bf16[3,80,128]{2,1,0:T(8,128)(2,1)S(1)}, u32[]{:S(2)}, u32[]{:S(2)}) collective-permute-start(bf16[3,80,128]{2,1,0:T(8,128)(2,1)S(1)} %shard_map.90.refs_7_), channel_id=1, source_target_pairs={{0,8},{8,0},{16,24},{24,16},{1,9},{9,1},{17,25},{25,17},{2,10},{10... | collective-permute-start | bytes 184328 | tf_op jit(solution)/shard_map/ppermute | solution.py:487
  78.0 3.5 %collective-permute-start.47 = (bf16[3,80,128]{2,1,0:T(8,128)(2,1)S(1)}, bf16[3,80,128]{2,1,0:T(8,128)(2,1)S(1)}, u32[]{:S(2)}, u32[]{:S(2)}) collective-permute-start(bf16[3,80,128]{2,1,0:T(8,128)(2,1)S(1)} %shard_map.90.refs_7_), channel_id=1, source_target_pairs={{0,4},{4,0},{1,5},{5,1},{2,6},{6,2},{3,7},{7,3},{8,12},{12,8},{9,1... | collective-permute-start | bytes 184328 | tf_op jit(solution)/shard_map/ppermute | solution.py:483
  84.0 7.4 %collective-permute-start.48 = (bf16[2,3,80,128]{3,2,1,0:T(8,128)(2,1)S(1)}, bf16[2,3,80,128]{3,2,1,0:T(8,128)(2,1)S(1)}, u32[]{:S(2)}, u32[]{:S(2)}) collective-permute-start(bf16[2,3,80,128]{3,2,1,0:T(8,128)(2,1)S(1)} %get-tuple-element.89), channel_id=1, source_target_pairs={{0,1},{1,0},{2,3},{3,2},{4,5},{5,4},{6,7},{7,6},{8,9},{9,8},{10,11... | collective-permute-start | bytes 368648 | tf_op jit(solution)/shard_map/ppermute | solution.py:487
  85.8 12.4 %collective-permute-start.49 = (bf16[2,3,80,128]{3,2,1,0:T(8,128)(2,1)S(1)}, bf16[2,3,80,128]{3,2,1,0:T(8,128)(2,1)S(1)}, u32[]{:S(2)}, u32[]{:S(2)}) collective-permute-start(bf16[2,3,80,128]{3,2,1,0:T(8,128)(2,1)S(1)} %get-tuple-element.89), channel_id=1, source_target_pairs={{0,2},{1,3},{2,0},{3,1},{4,6},{5,7},{6,4},{7,5},{8,10},{9,11},{10,... | collective-permute-start | bytes 368648 | tf_op jit(solution)/shard_map/ppermute | solution.py:487
  87.0 11.2 %collective-permute-start.50 = (bf16[2,3,80,128]{3,2,1,0:T(8,128)(2,1)S(1)}, bf16[2,3,80,128]{3,2,1,0:T(8,128)(2,1)S(1)}, u32[]{:S(2)}, u32[]{:S(2)}) collective-permute-start(bf16[2,3,80,128]{3,2,1,0:T(8,128)(2,1)S(1)} %get-tuple-element.89), channel_id=1, source_target_pairs={{0,3},{1,2},{2,1},{3,0},{4,7},{5,6},{6,5},{7,4},{8,11},{9,10},{10,... | collective-permute-start | bytes 368648 | tf_op jit(solution)/shard_map/ppermute | solution.py:487
  88.5 9.8 %collective-permute-start.54 = (bf16[3,3,80,128]{3,2,1,0:T(8,128)(2,1)S(1)}, bf16[3,3,80,128]{3,2,1,0:T(8,128)(2,1)S(1)}, u32[]{:S(2)}, u32[]{:S(2)}) collective-permute-start(bf16[3,3,80,128]{3,2,1,0:T(8,128)(2,1)S(1)} %pad_maximum_fusion), channel_id=1, source_target_pairs={{0,8},{8,0},{16,24},{24,16},{1,9},{9,1},{17,25},{25,17},{2,10},{10... | collective-permute-start | bytes 552968 | tf_op jit(solution)/shard_map/ppermute | solution.py:487
  89.7 9.8 %collective-permute-start.55 = (bf16[3,3,80,128]{3,2,1,0:T(8,128)(2,1)S(1)}, bf16[3,3,80,128]{3,2,1,0:T(8,128)(2,1)S(1)}, u32[]{:S(2)}, u32[]{:S(2)}) collective-permute-start(bf16[3,3,80,128]{3,2,1,0:T(8,128)(2,1)S(1)} %pad_maximum_fusion), channel_id=1, source_target_pairs={{0,16},{8,24},{16,0},{24,8},{1,17},{9,25},{17,1},{25,9},{2,18},{10... | collective-permute-start | bytes 552968 | tf_op jit(solution)/shard_map/ppermute | solution.py:487
  91.4 8.1 %collective-permute-start.56 = (bf16[3,3,80,128]{3,2,1,0:T(8,128)(2,1)S(1)}, bf16[3,3,80,128]{3,2,1,0:T(8,128)(2,1)S(1)}, u32[]{:S(2)}, u32[]{:S(2)}) collective-permute-start(bf16[3,3,80,128]{3,2,1,0:T(8,128)(2,1)S(1)} %pad_maximum_fusion), channel_id=1, source_target_pairs={{0,24},{8,16},{16,8},{24,0},{1,25},{9,17},{17,9},{25,1},{2,26},{10... | collective-permute-start | bytes 552968 | tf_op jit(solution)/shard_map/ppermute | solution.py:487
  99.5 2.3 %collective-permute-start.57 = (bf16[3,3,80,128]{3,2,1,0:T(8,128)(2,1)S(1)}, bf16[3,3,80,128]{3,2,1,0:T(8,128)(2,1)S(1)}, u32[]{:S(2)}, u32[]{:S(2)}) collective-permute-start(bf16[3,3,80,128]{3,2,1,0:T(8,128)(2,1)S(1)} %collective-permute-done.56.refs_1_), channel_id=1, source_target_pairs={{0,4},{4,0},{1,5},{5,1},{2,6},{6,2},{3,7},{7,3},{8,12},{12,8},{9,1... | collective-permute-start | bytes 552968 | tf_op jit(solution)/shard_map/ppermute | solution.py:483
  99.5 2.3 %collective-permute-start.58 = (bf16[3,3,80,128]{3,2,1,0:T(8,128)(2,1)S(1)}, bf16[3,3,80,128]{3,2,1,0:T(8,128)(2,1)S(1)}, u32[]{:S(2)}, u32[]{:S(2)}) collective-permute-start(bf16[3,3,80,128]{3,2,1,0:T(8,128)(2,1)S(1)} %collective-permute-done.55.refs_3_), channel_id=1, source_target_pairs={{0,4},{4,0},{1,5},{5,1},{2,6},{6,2},{3,7},{7,3},{8,12},{12,8},{9,1... | collective-permute-start | bytes 552968 | tf_op jit(solution)/shard_map/ppermute | solution.py:483
  100.0 2.3 %collective-permute-start.59 = (bf16[3,3,80,128]{3,2,1,0:T(8,128)(2,1)S(1)}, bf16[3,3,80,128]{3,2,1,0:T(8,128)(2,1)S(1)}, u32[]{:S(2)}, u32[]{:S(2)}) collective-permute-start(bf16[3,3,80,128]{3,2,1,0:T(8,128)(2,1)S(1)} %collective-permute-done.54.refs_5_), channel_id=1, source_target_pairs={{0,4},{4,0},{1,5},{5,1},{2,6},{6,2},{3,7},{7,3},{8,12},{12,8},{9,1... | collective-permute-start | bytes 552968 | tf_op jit(solution)/shard_map/ppermute | solution.py:483
  100.0 8.1 %collective-permute-start.52 = (bf16[3,3,80,128]{3,2,1,0:T(8,128)(2,1)S(1)}, bf16[3,3,80,128]{3,2,1,0:T(8,128)(2,1)S(1)}, u32[]{:S(2)}, u32[]{:S(2)}) collective-permute-start(bf16[3,3,80,128]{3,2,1,0:T(8,128)(2,1)S(1)} %pad_maximum_fusion.2.refs_7_), channel_id=1, source_target_pairs={{0,8},{8,0},{16,24},{24,16},{1,9},{9,1},{17,25},{25,17},{2,10},{10... | collective-permute-start | bytes 552968 | tf_op jit(solution)/shard_map/ppermute | solution.py:487
  100.9 7.2 %collective-permute-start.53 = (bf16[3,3,80,128]{3,2,1,0:T(8,128)(2,1)S(1)}, bf16[3,3,80,128]{3,2,1,0:T(8,128)(2,1)S(1)}, u32[]{:S(2)}, u32[]{:S(2)}) collective-permute-start(bf16[3,3,80,128]{3,2,1,0:T(8,128)(2,1)S(1)} %pad_maximum_fusion.2.refs_7_), channel_id=1, source_target_pairs={{0,16},{8,24},{16,0},{24,8},{1,17},{9,25},{17,1},{25,9},{2,18},{10... | collective-permute-start | bytes 552968 | tf_op jit(solution)/shard_map/ppermute | solution.py:487
  101.8 6.9 %collective-permute-start.62 = (bf16[3,3,80,128]{3,2,1,0:T(8,128)(2,1)S(1)}, bf16[3,3,80,128]{3,2,1,0:T(8,128)(2,1)S(1)}, u32[]{:S(2)}, u32[]{:S(2)}) collective-permute-start(bf16[3,3,80,128]{3,2,1,0:T(8,128)(2,1)S(1)} %pad_maximum_fusion.2.refs_7_), channel_id=1, source_target_pairs={{0,4},{4,0},{1,5},{5,1},{2,6},{6,2},{3,7},{7,3},{8,12},{12,8},{9,1... | collective-permute-start | bytes 552968 | tf_op jit(solution)/shard_map/ppermute | solution.py:483
  101.8 6.9 %collective-permute-start.51 = (bf16[3,3,80,128]{3,2,1,0:T(8,128)(2,1)S(1)}, bf16[3,3,80,128]{3,2,1,0:T(8,128)(2,1)S(1)}, u32[]{:S(2)}, u32[]{:S(2)}) collective-permute-start(bf16[3,3,80,128]{3,2,1,0:T(8,128)(2,1)S(1)} %pad_maximum_fusion.1.refs_1_), channel_id=1, source_target_pairs={{0,4},{4,0},{1,5},{5,1},{2,6},{6,2},{3,7},{7,3},{8,12},{12,8},{9,1... | collective-permute-start | bytes 552968 | tf_op jit(solution)/shard_map/ppermute | solution.py:483
  108.3 1.6 %collective-permute-start.61 = (bf16[3,3,80,128]{3,2,1,0:T(8,128)(2,1)S(1)}, bf16[3,3,80,128]{3,2,1,0:T(8,128)(2,1)S(1)}, u32[]{:S(2)}, u32[]{:S(2)}) collective-permute-start(bf16[3,3,80,128]{3,2,1,0:T(8,128)(2,1)S(1)} %collective-permute-done.52.refs_5_), channel_id=1, source_target_pairs={{0,4},{4,0},{1,5},{5,1},{2,6},{6,2},{3,7},{7,3},{8,12},{12,8},{9,1... | collective-permute-start | bytes 552968 | tf_op jit(solution)/shard_map/ppermute | solution.py:483
  (22 other events, 90.7 us)

commit v4 on v3

--- a/solution.py
+++ b/solution.py
@@ -279,12 +279,13 @@
     acc = None
     for block in sums:
         for frame in range(block.shape[0]):
-            acc = block[frame] if acc is None else acc + block[frame]
+            cells = block[frame].astype(F32)
+            acc = cells if acc is None else acc + cells
     mean = group_total(mixer, jnp.sum(acc, axis=1, keepdims=True))[:, :1] / members
     acc = None
     for block in sums:
         for frame in range(block.shape[0]):
-            centered = block[frame] - mean
+            centered = block[frame].astype(F32) - mean
             acc = centered * centered if acc is None else acc + centered * centered
     variance = group_total(mixer, jnp.sum(acc, axis=1, keepdims=True))[:, :1] / members
     return mean, lax.rsqrt(variance + EPSILON)
@@ -313,7 +314,7 @@
     first = second = None
     for slot, side in SIDES:
         for frame in range(frames):
-            normed = (sums[2 * slot + side][frame] - mean) * inv
+            normed = (sums[2 * slot + side][frame].astype(F32) - mean) * inv
             gate = jax.nn.sigmoid(normed)
             grad = given[2 * slot + side][frame].astype(F32) * gate * (1.0 + normed * (1.0 - gate))
             first = grad if first is None else first + grad
@@ -557,7 +558,8 @@
     )
     far = [hop(parts[k], "chan", k) for k in range(1, 4)]
     far, padded_inputs = lax.optimization_barrier((far, padded_inputs))
-    second_sums = around(parts[0] + sum(values.astype(F32) for values in far))
+    sums = parts[0] + sum(values.astype(F32) for values in far)
+    second_sums = [sums, *around(sums.astype(BF16))[1:]]
     every_shape = jax.ShapeDtypeStruct((count, 2, *block), BF16)
     result, halo, every_second = call(
         functools.partial(third_kernel, frames, members),

time: 118 us -> 116 us (0.983)
  waiting for transfers between devices: 41.5 us -> 40 us
  transfers between devices with their start and end apart: 63 -> 63, of which waited for: 32 -> 33; matrix products, arithmetic and copies ran while one was open for 0% -> 0% of each run, Pallas kernels for 7% -> 7%
where the time goes in v4:
time: 116 us; the launch traced here: 115 us
  starting transfers between devices  45.7 us (39%)
  waiting for transfers between devices  40 us (34%)
  Pallas kernels  25.5 us (22%)
  local copies, waits for them, and re-layouts  2.95 us (3%)
    ppermute x32, starting transfers between devices, hop(): return lax.ppermute(values, axis, [(i, i ^ step) for i in range(4)])  41.3 us
    ppermute x32, waiting for transfers between devices, hop(): return lax.ppermute(values, axis, [(i, i ^ step) for i in range(4)])  32.8 us
    pallas_call x10, Pallas kernels, call(): pl.pallas_call(kernel, out_shape=outs, in_specs=in_specs, out_specs=[vmem...  25.5 us
    ppermute x31, waiting for transfers between devices, swap(): return lax.ppermute(values, 'row', [(0, 1), (1, 0)])  7.15 us
    ppermute x31, starting transfers between devices, swap(): return lax.ppermute(values, 'row', [(0, 1), (1, 0)])  4.4 us
    unnamed x14, local copies, waits for them, and re-layouts  2.9 us
  transfers between devices with their start and end apart: 63, of which 33 were waited for; matrix products, arithmetic and copies ran while one was open for 0% of the time, Pallas kernels for 7%

profile of v4, /device:TPU:0, one launch (start us, length us, event | category | flops | bytes accessed | tf_op | source)
XLA Modules:
  0.0 115.5 jit_solution(4969810182063929563)
XLA Ops:
  0.6 3.0 %collective-permute-start = (bf16[3,80,128]{2,1,0:T(8,128)(2,1)}, bf16[3,80,128]{2,1,0:T(8,128)(2,1)S(1)}, u32[]{:S(2)}, u32[]{:S(2)}) collective-permute-start(bf16[3,80,128]{2,1,0:T(8,128)(2,1)} %bitcast.29), channel_id=1, source_target_pairs={{0,8},{8,0},{16,24},{24,16},{1,9},{9,1},{17,25},{25,17},{2,10},{10... | collective-permute-start | bytes 184328 | tf_op jit(solution)/shard_map/ppermute | solution.py:488
  3.6 1.5 %collective-permute-start.1 = (bf16[3,80,128]{2,1,0:T(8,128)(2,1)}, bf16[3,80,128]{2,1,0:T(8,128)(2,1)S(1)}, u32[]{:S(2)}, u32[]{:S(2)}) collective-permute-start(bf16[3,80,128]{2,1,0:T(8,128)(2,1)} %bitcast.30), channel_id=1, source_target_pairs={{0,16},{8,24},{16,0},{24,8},{1,17},{9,25},{17,1},{25,9},{2,18},{10... | collective-permute-start | bytes 184328 | tf_op jit(solution)/shard_map/ppermute | solution.py:488
  5.3 1.4 %copy-done = bf16[27,80,320]{2,1,0:T(8,128)(2,1)S(1)} copy-done((bf16[27,80,320]{2,1,0:T(8,128)(2,1)S(1)}, bf16[27,80,320]{2,1,0:T(8,128)(2,1)}, u32[]{:S(2)}) %copy-start) | copy-done | bytes 1382424
  6.7 1.4 %copy-done.2 = bf16[27,80,320]{2,1,0:T(8,128)(2,1)S(1)} copy-done((bf16[27,80,320]{2,1,0:T(8,128)(2,1)S(1)}, bf16[27,80,320]{2,1,0:T(8,128)(2,1)}, u32[]{:S(2)}) %copy-start.2) | copy-done | bytes 1382424
  9.1 1.4 %collective-permute-done.2.refs_1_ = bf16[3,80,128]{2,1,0:T(8,128)(2,1)S(1)} collective-permute-done((bf16[3,80,128]{2,1,0:T(8,128)(2,1)}, bf16[3,80,128]{2,1,0:T(8,128)(2,1)S(1)}, u32[]{:S(2)}, u32[]{:S(2)}) %collective-permute-start.2) | collective-permute-done | bytes 61472 | tf_op jit(solution)/shard_map/ppermute | solution.py:488
  12.3 1.4 %shard_map.85 = (f32[3,80,128]{2,1,0:T(8,128)S(1)}, bf16[3,80,128]{2,1,0:T(8,128)(2,1)S(1)}, bf16[3,80,128]{2,1,0:T(8,128)(2,1)S(1)}, bf16[3,80,128]{2,1,0:T(8,128)(2,1)S(1)}) custom-call(s32[3]{0:T(128)S(1)} %pad_add_fusion.where, bf16[3,80,128]{2,1,0:T(8,128)(2,1)S(1)} %collective-permute-done.3.refs_0_, ...), custom_call_target="tpu_custom_call" | custom-call | flops 353894400 | bytes 921600 | tf_op jit(solution)/shard_map/pallas_call | solution.py:179
  13.7 1.6 %collective-permute-start.10 = (bf16[3,80,128]{2,1,0:T(8,128)(2,1)S(1)}, bf16[3,80,128]{2,1,0:T(8,128)(2,1)S(1)}, u32[]{:S(2)}, u32[]{:S(2)}) collective-permute-start(bf16[3,80,128]{2,1,0:T(8,128)(2,1)S(1)} %get-tuple-element.65), channel_id=1, source_target_pairs={{0,1},{1,0},{2,3},{3,2},{4,5},{5,4},{6,7},{7,6},{8,9},{9,8},{10,11... | collective-permute-start | bytes 184328 | tf_op jit(solution)/shard_map/ppermute | solution.py:488
  15.3 2.6 %collective-permute-start.11 = (bf16[3,80,128]{2,1,0:T(8,128)(2,1)S(1)}, bf16[3,80,128]{2,1,0:T(8,128)(2,1)S(1)}, u32[]{:S(2)}, u32[]{:S(2)}) collective-permute-start(bf16[3,80,128]{2,1,0:T(8,128)(2,1)S(1)} %get-tuple-element.66), channel_id=1, source_target_pairs={{0,2},{1,3},{2,0},{3,1},{4,6},{5,7},{6,4},{7,5},{8,10},{9,11},{10,... | collective-permute-start | bytes 184328 | tf_op jit(solution)/shard_map/ppermute | solution.py:488
  18.9 1.5 %collective-permute-start.8 = (bf16[3,80,128]{2,1,0:T(8,128)(2,1)S(1)}, bf16[3,80,128]{2,1,0:T(8,128)(2,1)S(1)}, u32[]{:S(2)}, u32[]{:S(2)}) collective-permute-start(bf16[3,80,128]{2,1,0:T(8,128)(2,1)S(1)} %bitcast.37), channel_id=1, source_target_pairs={{0,16},{8,24},{16,0},{24,8},{1,17},{9,25},{17,1},{25,9},{2,18},{10... | collective-permute-start | bytes 184328 | tf_op jit(solution)/shard_map/ppermute | solution.py:488
  20.4 1.2 %collective-permute-start.9 = (bf16[3,80,128]{2,1,0:T(8,128)(2,1)S(1)}, bf16[3,80,128]{2,1,0:T(8,128)(2,1)S(1)}, u32[]{:S(2)}, u32[]{:S(2)}) collective-permute-start(bf16[3,80,128]{2,1,0:T(8,128)(2,1)S(1)} %bitcast.38), channel_id=1, source_target_pairs={{0,24},{8,16},{16,8},{24,0},{1,25},{9,17},{17,9},{25,1},{2,26},{10... | collective-permute-start | bytes 184328 | tf_op jit(solution)/shard_map/ppermute | solution.py:488
  21.9 2.1 %collective-permute-done.12 = bf16[3,80,128]{2,1,0:T(8,128)(2,1)S(1)} collective-permute-done((bf16[3,80,128]{2,1,0:T(8,128)(2,1)S(1)}, bf16[3,80,128]{2,1,0:T(8,128)(2,1)S(1)}, u32[]{:S(2)}, u32[]{:S(2)}) %collective-permute-start.12) | collective-permute-done | bytes 61472 | tf_op jit(solution)/shard_map/ppermute | solution.py:488
  24.1 1.5 %collective-permute-done.9.refs_2_ = bf16[3,80,128]{2,1,0:T(8,128)(2,1)S(1)} collective-permute-done((bf16[3,80,128]{2,1,0:T(8,128)(2,1)S(1)}, bf16[3,80,128]{2,1,0:T(8,128)(2,1)S(1)}, u32[]{:S(2)}, u32[]{:S(2)}) %collective-permute-start.9) | collective-permute-done | bytes 61472 | tf_op jit(solution)/shard_map/ppermute | solution.py:488
  25.5 1.2 %collective-permute-start.17 = (f32[3,80,128]{2,1,0:T(8,128)S(1)}, f32[3,80,128]{2,1,0:T(8,128)S(1)}, u32[]{:S(2)}, u32[]{:S(2)}) collective-permute-start(f32[3,80,128]{2,1,0:T(8,128)S(1)} %add_add_fusion.1.refs_7_.refs_15_), channel_id=1, source_target_pairs={{0,24},{8,16},{16,8},{24,0},{1,25},{9,17},{17,9},{25,1},{2,26},{10... | collective-permute-start | bytes 368648 | tf_op jit(solution)/shard_map/ppermute | solution.py:488
  27.5 1.5 %collective-permute-start.21 = (f32[3,80,128]{2,1,0:T(8,128)S(1)}, f32[3,80,128]{2,1,0:T(8,128)S(1)}, u32[]{:S(2)}, u32[]{:S(2)}) collective-permute-start(f32[3,80,128]{2,1,0:T(8,128)S(1)} %add_add_fusion.1.refs_7_.refs_15_), channel_id=1, source_target_pairs={{0,8},{8,0},{16,24},{24,16},{1,9},{9,1},{17,25},{25,17},{2,10},{10... | collective-permute-start | bytes 368648 | tf_op jit(solution)/shard_map/ppermute | solution.py:488
  29.0 2.4 %collective-permute-done.17.refs_1_.refs_9_ = f32[3,80,128]{2,1,0:T(8,128)S(1)} collective-permute-done((f32[3,80,128]{2,1,0:T(8,128)S(1)}, f32[3,80,128]{2,1,0:T(8,128)S(1)}, u32[]{:S(2)}, u32[]{:S(2)}) %collective-permute-start.17) | collective-permute-done | bytes 122912 | tf_op jit(solution)/shard_map/ppermute | solution.py:488
  31.4 1.2 %collective-permute-done.19.refs_3_.refs_11_ = f32[3,80,128]{2,1,0:T(8,128)S(1)} collective-permute-done((f32[3,80,128]{2,1,0:T(8,128)S(1)}, f32[3,80,128]{2,1,0:T(8,128)S(1)}, u32[]{:S(2)}, u32[]{:S(2)}) %collective-permute-start.19) | collective-permute-done | bytes 122912 | tf_op jit(solution)/shard_map/ppermute | solution.py:488
  34.1 2.4 %shard_map.86 = (bf16[4,2,3,80,128]{4,3,2,1,0:T(8,128)(2,1)S(1)}, f32[3,80,128]{2,1,0:T(8,128)S(1)}, f32[80,128]{1,0:T(8,128)S(1)}, f32[3,80,128]{2,1,0:T(8,128)...) custom-call(s32[3]{0:T(128)S(1)} %pad_add_fusion.where, ...), custom_call_target="tpu_custom_call" | custom-call | flops 353894400 | bytes 921600 | tf_op jit(solution)/shard_map/pallas_call | solution.py:179
  37.3 3.5 %collective-permute-start.25 = (bf16[3,80,128]{2,1,0:T(8,128)(2,1)S(1)}, bf16[3,80,128]{2,1,0:T(8,128)(2,1)S(1)}, u32[]{:S(2)}, u32[]{:S(2)}) collective-permute-start(bf16[3,80,128]{2,1,0:T(8,128)(2,1)S(1)} %get-tuple-element.74), channel_id=1, source_target_pairs={{0,2},{1,3},{2,0},{3,1},{4,6},{5,7},{6,4},{7,5},{8,10},{9,11},{10,... | collective-permute-start | bytes 184328 | tf_op jit(solution)/shard_map/ppermute | solution.py:488
  42.5 2.1 %collective-permute-done.25 = bf16[3,80,128]{2,1,0:T(8,128)(2,1)S(1)} collective-permute-done((bf16[3,80,128]{2,1,0:T(8,128)(2,1)S(1)}, bf16[3,80,128]{2,1,0:T(8,128)(2,1)S(1)}, u32[]{:S(2)}, u32[]{:S(2)}) %collective-permute-start.25) | collective-permute-done | bytes 61472 | tf_op jit(solution)/shard_map/ppermute | solution.py:488
  44.6 2.2 %collective-permute-done.26 = bf16[3,80,128]{2,1,0:T(8,128)(2,1)S(1)} collective-permute-done((bf16[3,80,128]{2,1,0:T(8,128)(2,1)S(1)}, bf16[3,80,128]{2,1,0:T(8,128)(2,1)S(1)}, u32[]{:S(2)}, u32[]{:S(2)}) %collective-permute-start.26) | collective-permute-done | bytes 61472 | tf_op jit(solution)/shard_map/ppermute | solution.py:488
  46.9 1.3 %collective-permute-start.27 = (bf16[3,80,128]{2,1,0:T(8,128)(2,1)S(1)}, bf16[3,80,128]{2,1,0:T(8,128)(2,1)S(1)}, u32[]{:S(2)}, u32[]{:S(2)}) collective-permute-start(bf16[3,80,128]{2,1,0:T(8,128)(2,1)S(1)} %get-tuple-element.108), channel_id=1, source_target_pairs={{0,24},{8,16},{16,8},{24,0},{1,25},{9,17},{17,9},{25,1},{2,26},{10... | collective-permute-start | bytes 184328 | tf_op jit(solution)/shard_map/ppermute | solution.py:488
  48.1 1.3 %collective-permute-start.29 = (bf16[3,80,128]{2,1,0:T(8,128)(2,1)S(1)}, bf16[3,80,128]{2,1,0:T(8,128)(2,1)S(1)}, u32[]{:S(2)}, u32[]{:S(2)}) collective-permute-start(bf16[3,80,128]{2,1,0:T(8,128)(2,1)S(1)} %get-tuple-element.108), channel_id=1, source_target_pairs={{0,16},{8,24},{16,0},{24,8},{1,17},{9,25},{17,1},{25,9},{2,18},{10... | collective-permute-start | bytes 184328 | tf_op jit(solution)/shard_map/ppermute | solution.py:488
  49.4 1.0 collective-permute-start.31
  50.9 1.1 collective-permute-done.27.refs_10_
  52.7 0.9 collective-permute-done.31.refs_14_
  54.0 0.9 collective-permute-done.32.refs_13_
  54.9 2.8 %shard_map.88 = (bf16[3,80,128]{2,1,0:T(8,128)(2,1)}, bf16[5,80,128]{2,1,0:T(8,128)(2,1)S(1)}, bf16[4,2,3,80,128]{4,3,2,1,0:T(8,128)(2,1)S(1)}) custom-call(s32[3]{0:T(128)S(1)} %pad_add_fusion.where, bf16[3,80,128]{2,1,0:T(8,128)(2,1)S(1)} %bitcast.35, bf16[3,80,128]{2,1,0:T(8,128)(2,1)S(1)} %collective-permute-done.13.refs_1_, ...), custom_call_target="tpu_custom_call" | custom-call | tf_op jit(solution)/shard_map/pallas_call | solution.py:179
  57.7 2.3 %collective-permute-start.35 = (bf16[5,80,128]{2,1,0:T(8,128)(2,1)S(1)}, bf16[5,80,128]{2,1,0:T(8,128)(2,1)S(1)}, u32[]{:S(2)}, u32[]{:S(2)}) collective-permute-start(bf16[5,80,128]{2,1,0:T(8,128)(2,1)S(1)} %get-tuple-element.80.refs_7_), channel_id=1, source_target_pairs={{0,2},{1,3},{2,0},{3,1},{4,6},{5,7},{6,4},{7,5},{8,10},{9,11},{10,... | collective-permute-start | bytes 307208 | tf_op jit(solution)/shard_map/ppermute | solution.py:488
  60.0 2.1 %collective-permute-start.36 = (bf16[5,80,128]{2,1,0:T(8,128)(2,1)S(1)}, bf16[5,80,128]{2,1,0:T(8,128)(2,1)S(1)}, u32[]{:S(2)}, u32[]{:S(2)}) collective-permute-start(bf16[5,80,128]{2,1,0:T(8,128)(2,1)S(1)} %get-tuple-element.80.refs_7_), channel_id=1, source_target_pairs={{0,3},{1,2},{2,1},{3,0},{4,7},{5,6},{6,5},{7,4},{8,11},{9,10},{10,... | collective-permute-start | bytes 307208 | tf_op jit(solution)/shard_map/ppermute | solution.py:488
  63.0 1.5 %collective-permute-done.34.refs_5_.refs_11_ = bf16[5,80,128]{2,1,0:T(8,128)(2,1)S(1)} collective-permute-done((bf16[5,80,128]{2,1,0:T(8,128)(2,1)S(1)}, bf16[5,80,128]{2,1,0:T(8,128)(2,1)S(1)}, u32[]{:S(2)}, u32[]{:S(2)}) %collective-permute-start.34) | collective-permute-done | bytes 102432 | tf_op jit(solution)/shard_map/ppermute | solution.py:488
  64.5 4.3 %collective-permute-done.35.refs_3_.refs_9_ = bf16[5,80,128]{2,1,0:T(8,128)(2,1)S(1)} collective-permute-done((bf16[5,80,128]{2,1,0:T(8,128)(2,1)S(1)}, bf16[5,80,128]{2,1,0:T(8,128)(2,1)S(1)}, u32[]{:S(2)}, u32[]{:S(2)}) %collective-permute-start.35) | collective-permute-done | bytes 102432 | tf_op jit(solution)/shard_map/ppermute | solution.py:488
  70.6 2.0 %shard_map.90.refs_7_ = bf16[3,80,128]{2,1,0:T(8,128)(2,1)S(1)} custom-call(s32[3]{0:T(128)S(1)} %pad_add_fusion.where, bf16[5,80,128]{2,1,0:T(8,128)(2,1)S(1)} %collective-permute-done.37.refs_0_.refs_6_, bf16[5,80,128]{2,1,0:T(8,128)(2,1)S(1)} %collective-permute-done.36.refs_1_.refs_7_, bf16[5,80,128]{2,1,0:T(8,128)(2,1)S(1)} %collective-permute-done.38.refs_2_.refs_8_, ...), custom_call_target="tpu_custom_call" | custom-call | flops 353894400 | bytes 921600 | tf_op jit(solution)/shard_map/pallas_call | solution.py:179
  72.6 2.0 %collective-permute-start.41 = (bf16[3,80,128]{2,1,0:T(8,128)(2,1)S(1)}, bf16[3,80,128]{2,1,0:T(8,128)(2,1)S(1)}, u32[]{:S(2)}, u32[]{:S(2)}) collective-permute-start(bf16[3,80,128]{2,1,0:T(8,128)(2,1)S(1)} %shard_map.90.refs_7_), channel_id=1, source_target_pairs={{0,24},{8,16},{16,8},{24,0},{1,25},{9,17},{17,9},{25,1},{2,26},{10... | collective-permute-start | bytes 184328 | tf_op jit(solution)/shard_map/ppermute | solution.py:488
  74.5 1.1 collective-permute-start.43
  76.1 1.7 %collective-permute-done.41.refs_1_ = bf16[3,80,128]{2,1,0:T(8,128)(2,1)S(1)} collective-permute-done((bf16[3,80,128]{2,1,0:T(8,128)(2,1)S(1)}, bf16[3,80,128]{2,1,0:T(8,128)(2,1)S(1)}, u32[]{:S(2)}, u32[]{:S(2)}) %collective-permute-start.41) | collective-permute-done | bytes 61472 | tf_op jit(solution)/shard_map/ppermute | solution.py:488
  77.8 1.1 collective-permute-done.43.refs_3_
  79.0 0.9 collective-permute-done.45.refs_5_
  80.2 0.9 collective-permute-done.46.refs_4_
  81.1 1.3 %shard_map.91 = (bf16[2,3,80,128]{3,2,1,0:T(8,128)(2,1)S(1)}, bf16[4,2,3,80,128]{4,3,2,1,0:T(8,128)(2,1)S(1)}) custom-call(s32[3]{0:T(128)S(1)} %pad_add_fusion.where, bf16[3,80,128]{2,1,0:T(8,128)(2,1)S(1)} %collective-permute-done.42.refs_0_, bf16[3,80,128]{2,1,0:T(8,128)(2,1)S(1)} %collective-permute-done.41.refs_1_, ...), custom_call_target="tpu_custom_call" | custom-call | tf_op jit(solution)/shard_map/pallas_call | solution.py:179
  82.4 1.8 %collective-permute-start.48 = (bf16[2,3,80,128]{3,2,1,0:T(8,128)(2,1)S(1)}, bf16[2,3,80,128]{3,2,1,0:T(8,128)(2,1)S(1)}, u32[]{:S(2)}, u32[]{:S(2)}) collective-permute-start(bf16[2,3,80,128]{3,2,1,0:T(8,128)(2,1)S(1)} %get-tuple-element.89), channel_id=1, source_target_pairs={{0,1},{1,0},{2,3},{3,2},{4,5},{5,4},{6,7},{7,6},{8,9},{9,8},{10,11... | collective-permute-start | bytes 368648 | tf_op jit(solution)/shard_map/ppermute | solution.py:488
  84.2 1.0 collective-permute-start.49
  85.3 1.6 %collective-permute-start.50 = (bf16[2,3,80,128]{3,2,1,0:T(8,128)(2,1)S(1)}, bf16[2,3,80,128]{3,2,1,0:T(8,128)(2,1)S(1)}, u32[]{:S(2)}, u32[]{:S(2)}) collective-permute-start(bf16[2,3,80,128]{3,2,1,0:T(8,128)(2,1)S(1)} %get-tuple-element.89), channel_id=1, source_target_pairs={{0,3},{1,2},{2,1},{3,0},{4,7},{5,6},{6,5},{7,4},{8,11},{9,10},{10,... | collective-permute-start | bytes 368648 | tf_op jit(solution)/shard_map/ppermute | solution.py:488
  87.6 1.0 collective-permute-start.55
  89.5 1.2 %collective-permute-start.56 = (bf16[3,3,80,128]{3,2,1,0:T(8,128)(2,1)S(1)}, bf16[3,3,80,128]{3,2,1,0:T(8,128)(2,1)S(1)}, u32[]{:S(2)}, u32[]{:S(2)}) collective-permute-start(bf16[3,3,80,128]{3,2,1,0:T(8,128)(2,1)S(1)} %pad_maximum_fusion), channel_id=1, source_target_pairs={{0,24},{8,16},{16,8},{24,0},{1,25},{9,17},{17,9},{25,1},{2,26},{10... | collective-permute-start | bytes 552968 | tf_op jit(solution)/shard_map/ppermute | solution.py:488
  90.8 5.8 %collective-permute-done.49 = bf16[2,3,80,128]{3,2,1,0:T(8,128)(2,1)S(1)} collective-permute-done((bf16[2,3,80,128]{3,2,1,0:T(8,128)(2,1)S(1)}, bf16[2,3,80,128]{3,2,1,0:T(8,128)(2,1)S(1)}, u32[]{:S(2)}, u32[]{:S(2)}) %collective-permute-start.49) | collective-permute-done | bytes 122912 | tf_op jit(solution)/shard_map/ppermute | solution.py:488
  98.0 1.1 collective-permute-start.52
  100.4 5.8 %shard_map.92 = f32[27,80,320]{2,1,0:T(8,128)} custom-call(s32[3]{0:T(128)S(1)} %pad_add_fusion.where, bf16[3,3,80,128]{3,2,1,0:T(8,128)(2,1)S(1)} %collective-permute-done.57.refs_0_, bf16[3,3,80,128]{3,2,1,0:T(8,128)(2,1)S(1)} %collective-permute-done.56.refs_1_, bf16[3,3,80,128]{3,2,1,0:T(8,128)(2,1)S(1)} %collective-permute-done.58.refs_2_, ...), custom_call_target="tpu_custom_call" | custom-call | flops 2831155200 | bytes 8000000 | tf_op jit(solution)/shard_map/pallas_call | solution.py:179
  108.0 7.3 %shard_map.93 = (f32[27,80,320]{2,1,0:T(8,128)}, bf16[3,80,128]{2,1,0:T(8,128)(2,1)}) custom-call(s32[3]{0:T(128)S(1)} %pad_add_fusion.where, bf16[3,3,80,128]{3,2,1,0:T(8,128)(2,1)S(1)} %collective-permute-done.51.refs_0_, bf16[3,3,80,128]{3,2,1,0:T(8,128)(2,1)S(1)} %pad_maximum_fusion.1.refs_1_, ...), custom_call_target="tpu_custom_call" | custom-call | flops 2831155200 | bytes 8000000 | tf_op jit(solution)/shard_map/pallas_call | solution.py:179
  (113 shorter events, 19.8 us)
Async XLA Ops:
  0.6 8.4 %collective-permute-start = (bf16[3,80,128]{2,1,0:T(8,128)(2,1)}, bf16[3,80,128]{2,1,0:T(8,128)(2,1)S(1)}, u32[]{:S(2)}, u32[]{:S(2)}) collective-permute-start(bf16[3,80,128]{2,1,0:T(8,128)(2,1)} %bitcast.29), channel_id=1, source_target_pairs={{0,8},{8,0},{16,24},{24,16},{1,9},{9,1},{17,25},{25,17},{2,10},{10... | collective-permute-start | bytes 184328 | tf_op jit(solution)/shard_map/ppermute | solution.py:488
  3.6 5.4 %collective-permute-start.1 = (bf16[3,80,128]{2,1,0:T(8,128)(2,1)}, bf16[3,80,128]{2,1,0:T(8,128)(2,1)S(1)}, u32[]{:S(2)}, u32[]{:S(2)}) collective-permute-start(bf16[3,80,128]{2,1,0:T(8,128)(2,1)} %bitcast.30), channel_id=1, source_target_pairs={{0,16},{8,24},{16,0},{24,8},{1,17},{9,25},{17,1},{25,9},{2,18},{10... | collective-permute-start | bytes 184328 | tf_op jit(solution)/shard_map/ppermute | solution.py:488
  5.2 5.3 %collective-permute-start.2 = (bf16[3,80,128]{2,1,0:T(8,128)(2,1)}, bf16[3,80,128]{2,1,0:T(8,128)(2,1)S(1)}, u32[]{:S(2)}, u32[]{:S(2)}) collective-permute-start(bf16[3,80,128]{2,1,0:T(8,128)(2,1)} %bitcast.31), channel_id=1, source_target_pairs={{0,24},{8,16},{16,8},{24,0},{1,25},{9,17},{17,9},{25,1},{2,26},{10... | collective-permute-start | bytes 184328 | tf_op jit(solution)/shard_map/ppermute | solution.py:488
  5.2 5.8 %collective-permute-start.6 = (bf16[3,80,128]{2,1,0:T(8,128)(2,1)}, bf16[3,80,128]{2,1,0:T(8,128)(2,1)S(1)}, u32[]{:S(2)}, u32[]{:S(2)}) collective-permute-start(bf16[3,80,128]{2,1,0:T(8,128)(2,1)} %bitcast.32), channel_id=1, source_target_pairs={{0,4},{4,0},{1,5},{5,1},{2,6},{6,2},{3,7},{7,3},{8,12},{12,8},{9,1... | collective-permute-start | bytes 184328 | tf_op jit(solution)/shard_map/ppermute | solution.py:484
  13.7 6.7 %collective-permute-start.10 = (bf16[3,80,128]{2,1,0:T(8,128)(2,1)S(1)}, bf16[3,80,128]{2,1,0:T(8,128)(2,1)S(1)}, u32[]{:S(2)}, u32[]{:S(2)}) collective-permute-start(bf16[3,80,128]{2,1,0:T(8,128)(2,1)S(1)} %get-tuple-element.65), channel_id=1, source_target_pairs={{0,1},{1,0},{2,3},{3,2},{4,5},{5,4},{6,7},{7,6},{8,9},{9,8},{10,11... | collective-permute-start | bytes 184328 | tf_op jit(solution)/shard_map/ppermute | solution.py:488
  15.3 6.6 %collective-permute-start.11 = (bf16[3,80,128]{2,1,0:T(8,128)(2,1)S(1)}, bf16[3,80,128]{2,1,0:T(8,128)(2,1)S(1)}, u32[]{:S(2)}, u32[]{:S(2)}) collective-permute-start(bf16[3,80,128]{2,1,0:T(8,128)(2,1)S(1)} %get-tuple-element.66), channel_id=1, source_target_pairs={{0,2},{1,3},{2,0},{3,1},{4,6},{5,7},{6,4},{7,5},{8,10},{9,11},{10,... | collective-permute-start | bytes 184328 | tf_op jit(solution)/shard_map/ppermute | solution.py:488
  17.9 6.1 %collective-permute-start.12 = (bf16[3,80,128]{2,1,0:T(8,128)(2,1)S(1)}, bf16[3,80,128]{2,1,0:T(8,128)(2,1)S(1)}, u32[]{:S(2)}, u32[]{:S(2)}) collective-permute-start(bf16[3,80,128]{2,1,0:T(8,128)(2,1)S(1)} %get-tuple-element.67), channel_id=1, source_target_pairs={{0,3},{1,2},{2,1},{3,0},{4,7},{5,6},{6,5},{7,4},{8,11},{9,10},{10,... | collective-permute-start | bytes 184328 | tf_op jit(solution)/shard_map/ppermute | solution.py:488
  18.1 5.9 %collective-permute-start.7 = (bf16[3,80,128]{2,1,0:T(8,128)(2,1)S(1)}, bf16[3,80,128]{2,1,0:T(8,128)(2,1)S(1)}, u32[]{:S(2)}, u32[]{:S(2)}) collective-permute-start(bf16[3,80,128]{2,1,0:T(8,128)(2,1)S(1)} %bitcast.36), channel_id=1, source_target_pairs={{0,8},{8,0},{16,24},{24,16},{1,9},{9,1},{17,25},{25,17},{2,10},{10... | collective-permute-start | bytes 184328 | tf_op jit(solution)/shard_map/ppermute | solution.py:488
  18.9 5.2 %collective-permute-start.8 = (bf16[3,80,128]{2,1,0:T(8,128)(2,1)S(1)}, bf16[3,80,128]{2,1,0:T(8,128)(2,1)S(1)}, u32[]{:S(2)}, u32[]{:S(2)}) collective-permute-start(bf16[3,80,128]{2,1,0:T(8,128)(2,1)S(1)} %bitcast.37), channel_id=1, source_target_pairs={{0,16},{8,24},{16,0},{24,8},{1,17},{9,25},{17,1},{25,9},{2,18},{10... | collective-permute-start | bytes 184328 | tf_op jit(solution)/shard_map/ppermute | solution.py:488
  20.4 5.1 %collective-permute-start.9 = (bf16[3,80,128]{2,1,0:T(8,128)(2,1)S(1)}, bf16[3,80,128]{2,1,0:T(8,128)(2,1)S(1)}, u32[]{:S(2)}, u32[]{:S(2)}) collective-permute-start(bf16[3,80,128]{2,1,0:T(8,128)(2,1)S(1)} %bitcast.38), channel_id=1, source_target_pairs={{0,24},{8,16},{16,8},{24,0},{1,25},{9,17},{17,9},{25,1},{2,26},{10... | collective-permute-start | bytes 184328 | tf_op jit(solution)/shard_map/ppermute | solution.py:488
  25.5 5.9 %collective-permute-start.17 = (f32[3,80,128]{2,1,0:T(8,128)S(1)}, f32[3,80,128]{2,1,0:T(8,128)S(1)}, u32[]{:S(2)}, u32[]{:S(2)}) collective-permute-start(f32[3,80,128]{2,1,0:T(8,128)S(1)} %add_add_fusion.1.refs_7_.refs_15_), channel_id=1, source_target_pairs={{0,24},{8,16},{16,8},{24,0},{1,25},{9,17},{17,9},{25,1},{2,26},{10... | collective-permute-start | bytes 368648 | tf_op jit(solution)/shard_map/ppermute | solution.py:488
  26.7 5.9 %collective-permute-start.19 = (f32[3,80,128]{2,1,0:T(8,128)S(1)}, f32[3,80,128]{2,1,0:T(8,128)S(1)}, u32[]{:S(2)}, u32[]{:S(2)}) collective-permute-start(f32[3,80,128]{2,1,0:T(8,128)S(1)} %add_add_fusion.1.refs_7_.refs_15_), channel_id=1, source_target_pairs={{0,16},{8,24},{16,0},{24,8},{1,17},{9,25},{17,1},{25,9},{2,18},{10... | collective-permute-start | bytes 368648 | tf_op jit(solution)/shard_map/ppermute | solution.py:488
  27.5 5.1 %collective-permute-start.21 = (f32[3,80,128]{2,1,0:T(8,128)S(1)}, f32[3,80,128]{2,1,0:T(8,128)S(1)}, u32[]{:S(2)}, u32[]{:S(2)}) collective-permute-start(f32[3,80,128]{2,1,0:T(8,128)S(1)} %add_add_fusion.1.refs_7_.refs_15_), channel_id=1, source_target_pairs={{0,8},{8,0},{16,24},{24,16},{1,9},{9,1},{17,25},{25,17},{2,10},{10... | collective-permute-start | bytes 368648 | tf_op jit(solution)/shard_map/ppermute | solution.py:488
  29.0 4.1 %collective-permute-start.23 = (f32[3,80,128]{2,1,0:T(8,128)S(1)}, f32[3,80,128]{2,1,0:T(8,128)S(1)}, u32[]{:S(2)}, u32[]{:S(2)}) collective-permute-start(f32[3,80,128]{2,1,0:T(8,128)S(1)} %add_add_fusion.1.refs_7_.refs_15_), channel_id=1, source_target_pairs={{0,4},{4,0},{1,5},{5,1},{2,6},{6,2},{3,7},{7,3},{8,12},{12,8},{9,1... | collective-permute-start | bytes 368648 | tf_op jit(solution)/shard_map/ppermute | solution.py:484
  31.4 1.7 %collective-permute-start.18 = (f32[3,80,128]{2,1,0:T(8,128)S(1)}, f32[3,80,128]{2,1,0:T(8,128)S(1)}, u32[]{:S(2)}, u32[]{:S(2)}) collective-permute-start(f32[3,80,128]{2,1,0:T(8,128)S(1)} %collective-permute-done.17.refs_1_.refs_9_), channel_id=1, source_target_pairs={{0,4},{4,0},{1,5},{5,1},{2,6},{6,2},{3,7},{7,3},{8,12},{12,8},{9,1... | collective-permute-start | bytes 368648 | tf_op jit(solution)/shard_map/ppermute | solution.py:484
  36.5 5.9 %collective-permute-start.24 = (bf16[3,80,128]{2,1,0:T(8,128)(2,1)S(1)}, bf16[3,80,128]{2,1,0:T(8,128)(2,1)S(1)}, u32[]{:S(2)}, u32[]{:S(2)}) collective-permute-start(bf16[3,80,128]{2,1,0:T(8,128)(2,1)S(1)} %get-tuple-element.73), channel_id=1, source_target_pairs={{0,1},{1,0},{2,3},{3,2},{4,5},{5,4},{6,7},{7,6},{8,9},{9,8},{10,11... | collective-permute-start | bytes 184328 | tf_op jit(solution)/shard_map/ppermute | solution.py:488
  37.3 7.4 %collective-permute-start.25 = (bf16[3,80,128]{2,1,0:T(8,128)(2,1)S(1)}, bf16[3,80,128]{2,1,0:T(8,128)(2,1)S(1)}, u32[]{:S(2)}, u32[]{:S(2)}) collective-permute-start(bf16[3,80,128]{2,1,0:T(8,128)(2,1)S(1)} %get-tuple-element.74), channel_id=1, source_target_pairs={{0,2},{1,3},{2,0},{3,1},{4,6},{5,7},{6,4},{7,5},{8,10},{9,11},{10,... | collective-permute-start | bytes 184328 | tf_op jit(solution)/shard_map/ppermute | solution.py:488
  40.7 6.1 %collective-permute-start.26 = (bf16[3,80,128]{2,1,0:T(8,128)(2,1)S(1)}, bf16[3,80,128]{2,1,0:T(8,128)(2,1)S(1)}, u32[]{:S(2)}, u32[]{:S(2)}) collective-permute-start(bf16[3,80,128]{2,1,0:T(8,128)(2,1)S(1)} %get-tuple-element.75), channel_id=1, source_target_pairs={{0,3},{1,2},{2,1},{3,0},{4,7},{5,6},{6,5},{7,4},{8,11},{9,10},{10,... | collective-permute-start | bytes 184328 | tf_op jit(solution)/shard_map/ppermute | solution.py:488
  41.0 8.5 %collective-permute-start.16 = (bf16[3,80,128]{2,1,0:T(8,128)(2,1)S(1)}, bf16[3,80,128]{2,1,0:T(8,128)(2,1)S(1)}, u32[]{:S(2)}, u32[]{:S(2)}) collective-permute-start(bf16[3,80,128]{2,1,0:T(8,128)(2,1)S(1)} %bitcast.39), channel_id=1, source_target_pairs={{0,4},{4,0},{1,5},{5,1},{2,6},{6,2},{3,7},{7,3},{8,12},{12,8},{9,1... | collective-permute-start | bytes 184328 | tf_op jit(solution)/shard_map/ppermute | solution.py:484
  41.8 8.6 %collective-permute-start.13 = (bf16[3,80,128]{2,1,0:T(8,128)(2,1)S(1)}, bf16[3,80,128]{2,1,0:T(8,128)(2,1)S(1)}, u32[]{:S(2)}, u32[]{:S(2)}) collective-permute-start(bf16[3,80,128]{2,1,0:T(8,128)(2,1)S(1)} %collective-permute-done.9.refs_2_), channel_id=1, source_target_pairs={{0,4},{4,0},{1,5},{5,1},{2,6},{6,2},{3,7},{7,3},{8,12},{12,8},{9,1... | collective-permute-start | bytes 184328 | tf_op jit(solution)/shard_map/ppermute | solution.py:484
  42.4 8.0 %collective-permute-start.14 = (bf16[3,80,128]{2,1,0:T(8,128)(2,1)S(1)}, bf16[3,80,128]{2,1,0:T(8,128)(2,1)S(1)}, u32[]{:S(2)}, u32[]{:S(2)}) collective-permute-start(bf16[3,80,128]{2,1,0:T(8,128)(2,1)S(1)} %collective-permute-done.8.refs_4_), channel_id=1, source_target_pairs={{0,4},{4,0},{1,5},{5,1},{2,6},{6,2},{3,7},{7,3},{8,12},{12,8},{9,1... | collective-permute-start | bytes 184328 | tf_op jit(solution)/shard_map/ppermute | solution.py:484
  46.9 5.2 %collective-permute-start.27 = (bf16[3,80,128]{2,1,0:T(8,128)(2,1)S(1)}, bf16[3,80,128]{2,1,0:T(8,128)(2,1)S(1)}, u32[]{:S(2)}, u32[]{:S(2)}) collective-permute-start(bf16[3,80,128]{2,1,0:T(8,128)(2,1)S(1)} %get-tuple-element.108), channel_id=1, source_target_pairs={{0,24},{8,16},{16,8},{24,0},{1,25},{9,17},{17,9},{25,1},{2,26},{10... | collective-permute-start | bytes 184328 | tf_op jit(solution)/shard_map/ppermute | solution.py:488
  48.1 4.6 %collective-permute-start.29 = (bf16[3,80,128]{2,1,0:T(8,128)(2,1)S(1)}, bf16[3,80,128]{2,1,0:T(8,128)(2,1)S(1)}, u32[]{:S(2)}, u32[]{:S(2)}) collective-permute-start(bf16[3,80,128]{2,1,0:T(8,128)(2,1)S(1)} %get-tuple-element.108), channel_id=1, source_target_pairs={{0,16},{8,24},{16,0},{24,8},{1,17},{9,25},{17,1},{25,9},{2,18},{10... | collective-permute-start | bytes 184328 | tf_op jit(solution)/shard_map/ppermute | solution.py:488
  49.4 4.2 %collective-permute-start.31 = (bf16[3,80,128]{2,1,0:T(8,128)(2,1)S(1)}, bf16[3,80,128]{2,1,0:T(8,128)(2,1)S(1)}, u32[]{:S(2)}, u32[]{:S(2)}) collective-permute-start(bf16[3,80,128]{2,1,0:T(8,128)(2,1)S(1)} %get-tuple-element.108), channel_id=1, source_target_pairs={{0,8},{8,0},{16,24},{24,16},{1,9},{9,1},{17,25},{25,17},{2,10},{10... | collective-permute-start | bytes 184328 | tf_op jit(solution)/shard_map/ppermute | solution.py:488
  50.4 3.2 %collective-permute-start.15 = (bf16[3,80,128]{2,1,0:T(8,128)(2,1)S(1)}, bf16[3,80,128]{2,1,0:T(8,128)(2,1)S(1)}, u32[]{:S(2)}, u32[]{:S(2)}) collective-permute-start(bf16[3,80,128]{2,1,0:T(8,128)(2,1)S(1)} %collective-permute-done.7.refs_6_), channel_id=1, source_target_pairs={{0,4},{4,0},{1,5},{5,1},{2,6},{6,2},{3,7},{7,3},{8,12},{12,8},{9,1... | collective-permute-start | bytes 184328 | tf_op jit(solution)/shard_map/ppermute | solution.py:484
  50.4 3.2 %collective-permute-start.33 = (bf16[3,80,128]{2,1,0:T(8,128)(2,1)S(1)}, bf16[3,80,128]{2,1,0:T(8,128)(2,1)S(1)}, u32[]{:S(2)}, u32[]{:S(2)}) collective-permute-start(bf16[3,80,128]{2,1,0:T(8,128)(2,1)S(1)} %get-tuple-element.108), channel_id=1, source_target_pairs={{0,4},{4,0},{1,5},{5,1},{2,6},{6,2},{3,7},{7,3},{8,12},{12,8},{9,1... | collective-permute-start | bytes 184328 | tf_op jit(solution)/shard_map/ppermute | solution.py:484
  57.7 6.8 %collective-permute-start.34 = (bf16[5,80,128]{2,1,0:T(8,128)(2,1)S(1)}, bf16[5,80,128]{2,1,0:T(8,128)(2,1)S(1)}, u32[]{:S(2)}, u32[]{:S(2)}) collective-permute-start(bf16[5,80,128]{2,1,0:T(8,128)(2,1)S(1)} %get-tuple-element.80.refs_7_), channel_id=1, source_target_pairs={{0,1},{1,0},{2,3},{3,2},{4,5},{5,4},{6,7},{7,6},{8,9},{9,8},{10,11... | collective-permute-start | bytes 307208 | tf_op jit(solution)/shard_map/ppermute | solution.py:488
  57.7 11.0 %collective-permute-start.35 = (bf16[5,80,128]{2,1,0:T(8,128)(2,1)S(1)}, bf16[5,80,128]{2,1,0:T(8,128)(2,1)S(1)}, u32[]{:S(2)}, u32[]{:S(2)}) collective-permute-start(bf16[5,80,128]{2,1,0:T(8,128)(2,1)S(1)} %get-tuple-element.80.refs_7_), channel_id=1, source_target_pairs={{0,2},{1,3},{2,0},{3,1},{4,6},{5,7},{6,4},{7,5},{8,10},{9,11},{10,... | collective-permute-start | bytes 307208 | tf_op jit(solution)/shard_map/ppermute | solution.py:488
  60.0 8.7 %collective-permute-start.36 = (bf16[5,80,128]{2,1,0:T(8,128)(2,1)S(1)}, bf16[5,80,128]{2,1,0:T(8,128)(2,1)S(1)}, u32[]{:S(2)}, u32[]{:S(2)}) collective-permute-start(bf16[5,80,128]{2,1,0:T(8,128)(2,1)S(1)} %get-tuple-element.80.refs_7_), channel_id=1, source_target_pairs={{0,3},{1,2},{2,1},{3,0},{4,7},{5,6},{6,5},{7,4},{8,11},{9,10},{10,... | collective-permute-start | bytes 307208 | tf_op jit(solution)/shard_map/ppermute | solution.py:488
  63.0 6.3 %collective-permute-start.40 = (bf16[5,80,128]{2,1,0:T(8,128)(2,1)S(1)}, bf16[5,80,128]{2,1,0:T(8,128)(2,1)S(1)}, u32[]{:S(2)}, u32[]{:S(2)}) collective-permute-start(bf16[5,80,128]{2,1,0:T(8,128)(2,1)S(1)} %get-tuple-element.80.refs_7_), channel_id=1, source_target_pairs={{0,4},{4,0},{1,5},{5,1},{2,6},{6,2},{3,7},{7,3},{8,12},{12,8},{9,1... | collective-permute-start | bytes 307208 | tf_op jit(solution)/shard_map/ppermute | solution.py:484
  72.6 5.3 %collective-permute-start.41 = (bf16[3,80,128]{2,1,0:T(8,128)(2,1)S(1)}, bf16[3,80,128]{2,1,0:T(8,128)(2,1)S(1)}, u32[]{:S(2)}, u32[]{:S(2)}) collective-permute-start(bf16[3,80,128]{2,1,0:T(8,128)(2,1)S(1)} %shard_map.90.refs_7_), channel_id=1, source_target_pairs={{0,24},{8,16},{16,8},{24,0},{1,25},{9,17},{17,9},{25,1},{2,26},{10... | collective-permute-start | bytes 184328 | tf_op jit(solution)/shard_map/ppermute | solution.py:488
  74.5 4.4 %collective-permute-start.43 = (bf16[3,80,128]{2,1,0:T(8,128)(2,1)S(1)}, bf16[3,80,128]{2,1,0:T(8,128)(2,1)S(1)}, u32[]{:S(2)}, u32[]{:S(2)}) collective-permute-start(bf16[3,80,128]{2,1,0:T(8,128)(2,1)S(1)} %shard_map.90.refs_7_), channel_id=1, source_target_pairs={{0,16},{8,24},{16,0},{24,8},{1,17},{9,25},{17,1},{25,9},{2,18},{10... | collective-permute-start | bytes 184328 | tf_op jit(solution)/shard_map/ppermute | solution.py:488
  75.7 4.2 %collective-permute-start.45 = (bf16[3,80,128]{2,1,0:T(8,128)(2,1)S(1)}, bf16[3,80,128]{2,1,0:T(8,128)(2,1)S(1)}, u32[]{:S(2)}, u32[]{:S(2)}) collective-permute-start(bf16[3,80,128]{2,1,0:T(8,128)(2,1)S(1)} %shard_map.90.refs_7_), channel_id=1, source_target_pairs={{0,8},{8,0},{16,24},{24,16},{1,9},{9,1},{17,25},{25,17},{2,10},{10... | collective-permute-start | bytes 184328 | tf_op jit(solution)/shard_map/ppermute | solution.py:488
  76.1 3.8 %collective-permute-start.47 = (bf16[3,80,128]{2,1,0:T(8,128)(2,1)S(1)}, bf16[3,80,128]{2,1,0:T(8,128)(2,1)S(1)}, u32[]{:S(2)}, u32[]{:S(2)}) collective-permute-start(bf16[3,80,128]{2,1,0:T(8,128)(2,1)S(1)} %shard_map.90.refs_7_), channel_id=1, source_target_pairs={{0,4},{4,0},{1,5},{5,1},{2,6},{6,2},{3,7},{7,3},{8,12},{12,8},{9,1... | collective-permute-start | bytes 184328 | tf_op jit(solution)/shard_map/ppermute | solution.py:484
  77.8 2.1 %collective-permute-start.42 = (bf16[3,80,128]{2,1,0:T(8,128)(2,1)S(1)}, bf16[3,80,128]{2,1,0:T(8,128)(2,1)S(1)}, u32[]{:S(2)}, u32[]{:S(2)}) collective-permute-start(bf16[3,80,128]{2,1,0:T(8,128)(2,1)S(1)} %collective-permute-done.41.refs_1_), channel_id=1, source_target_pairs={{0,4},{4,0},{1,5},{5,1},{2,6},{6,2},{3,7},{7,3},{8,12},{12,8},{9,1... | collective-permute-start | bytes 184328 | tf_op jit(solution)/shard_map/ppermute | solution.py:484
  82.4 7.1 %collective-permute-start.48 = (bf16[2,3,80,128]{3,2,1,0:T(8,128)(2,1)S(1)}, bf16[2,3,80,128]{3,2,1,0:T(8,128)(2,1)S(1)}, u32[]{:S(2)}, u32[]{:S(2)}) collective-permute-start(bf16[2,3,80,128]{3,2,1,0:T(8,128)(2,1)S(1)} %get-tuple-element.89), channel_id=1, source_target_pairs={{0,1},{1,0},{2,3},{3,2},{4,5},{5,4},{6,7},{7,6},{8,9},{9,8},{10,11... | collective-permute-start | bytes 368648 | tf_op jit(solution)/shard_map/ppermute | solution.py:488
  84.2 12.4 %collective-permute-start.49 = (bf16[2,3,80,128]{3,2,1,0:T(8,128)(2,1)S(1)}, bf16[2,3,80,128]{3,2,1,0:T(8,128)(2,1)S(1)}, u32[]{:S(2)}, u32[]{:S(2)}) collective-permute-start(bf16[2,3,80,128]{3,2,1,0:T(8,128)(2,1)S(1)} %get-tuple-element.89), channel_id=1, source_target_pairs={{0,2},{1,3},{2,0},{3,1},{4,6},{5,7},{6,4},{7,5},{8,10},{9,11},{10,... | collective-permute-start | bytes 368648 | tf_op jit(solution)/shard_map/ppermute | solution.py:488
  85.3 11.4 %collective-permute-start.50 = (bf16[2,3,80,128]{3,2,1,0:T(8,128)(2,1)S(1)}, bf16[2,3,80,128]{3,2,1,0:T(8,128)(2,1)S(1)}, u32[]{:S(2)}, u32[]{:S(2)}) collective-permute-start(bf16[2,3,80,128]{3,2,1,0:T(8,128)(2,1)S(1)} %get-tuple-element.89), channel_id=1, source_target_pairs={{0,3},{1,2},{2,1},{3,0},{4,7},{5,6},{6,5},{7,4},{8,11},{9,10},{10,... | collective-permute-start | bytes 368648 | tf_op jit(solution)/shard_map/ppermute | solution.py:488
  86.9 9.8 %collective-permute-start.54 = (bf16[3,3,80,128]{3,2,1,0:T(8,128)(2,1)S(1)}, bf16[3,3,80,128]{3,2,1,0:T(8,128)(2,1)S(1)}, u32[]{:S(2)}, u32[]{:S(2)}) collective-permute-start(bf16[3,3,80,128]{3,2,1,0:T(8,128)(2,1)S(1)} %pad_maximum_fusion), channel_id=1, source_target_pairs={{0,8},{8,0},{16,24},{24,16},{1,9},{9,1},{17,25},{25,17},{2,10},{10... | collective-permute-start | bytes 552968 | tf_op jit(solution)/shard_map/ppermute | solution.py:488
  87.6 9.8 %collective-permute-start.55 = (bf16[3,3,80,128]{3,2,1,0:T(8,128)(2,1)S(1)}, bf16[3,3,80,128]{3,2,1,0:T(8,128)(2,1)S(1)}, u32[]{:S(2)}, u32[]{:S(2)}) collective-permute-start(bf16[3,3,80,128]{3,2,1,0:T(8,128)(2,1)S(1)} %pad_maximum_fusion), channel_id=1, source_target_pairs={{0,16},{8,24},{16,0},{24,8},{1,17},{9,25},{17,1},{25,9},{2,18},{10... | collective-permute-start | bytes 552968 | tf_op jit(solution)/shard_map/ppermute | solution.py:488
  89.5 7.9 %collective-permute-start.56 = (bf16[3,3,80,128]{3,2,1,0:T(8,128)(2,1)S(1)}, bf16[3,3,80,128]{3,2,1,0:T(8,128)(2,1)S(1)}, u32[]{:S(2)}, u32[]{:S(2)}) collective-permute-start(bf16[3,3,80,128]{3,2,1,0:T(8,128)(2,1)S(1)} %pad_maximum_fusion), channel_id=1, source_target_pairs={{0,24},{8,16},{16,8},{24,0},{1,25},{9,17},{17,9},{25,1},{2,26},{10... | collective-permute-start | bytes 552968 | tf_op jit(solution)/shard_map/ppermute | solution.py:488
  97.5 2.4 %collective-permute-start.57 = (bf16[3,3,80,128]{3,2,1,0:T(8,128)(2,1)S(1)}, bf16[3,3,80,128]{3,2,1,0:T(8,128)(2,1)S(1)}, u32[]{:S(2)}, u32[]{:S(2)}) collective-permute-start(bf16[3,3,80,128]{3,2,1,0:T(8,128)(2,1)S(1)} %collective-permute-done.56.refs_1_), channel_id=1, source_target_pairs={{0,4},{4,0},{1,5},{5,1},{2,6},{6,2},{3,7},{7,3},{8,12},{12,8},{9,1... | collective-permute-start | bytes 552968 | tf_op jit(solution)/shard_map/ppermute | solution.py:484
  97.5 2.4 %collective-permute-start.58 = (bf16[3,3,80,128]{3,2,1,0:T(8,128)(2,1)S(1)}, bf16[3,3,80,128]{3,2,1,0:T(8,128)(2,1)S(1)}, u32[]{:S(2)}, u32[]{:S(2)}) collective-permute-start(bf16[3,3,80,128]{3,2,1,0:T(8,128)(2,1)S(1)} %collective-permute-done.55.refs_3_), channel_id=1, source_target_pairs={{0,4},{4,0},{1,5},{5,1},{2,6},{6,2},{3,7},{7,3},{8,12},{12,8},{9,1... | collective-permute-start | bytes 552968 | tf_op jit(solution)/shard_map/ppermute | solution.py:484
  98.0 2.4 %collective-permute-start.59 = (bf16[3,3,80,128]{3,2,1,0:T(8,128)(2,1)S(1)}, bf16[3,3,80,128]{3,2,1,0:T(8,128)(2,1)S(1)}, u32[]{:S(2)}, u32[]{:S(2)}) collective-permute-start(bf16[3,3,80,128]{3,2,1,0:T(8,128)(2,1)S(1)} %collective-permute-done.54.refs_5_), channel_id=1, source_target_pairs={{0,4},{4,0},{1,5},{5,1},{2,6},{6,2},{3,7},{7,3},{8,12},{12,8},{9,1... | collective-permute-start | bytes 552968 | tf_op jit(solution)/shard_map/ppermute | solution.py:484
  98.0 8.3 %collective-permute-start.52 = (bf16[3,3,80,128]{3,2,1,0:T(8,128)(2,1)S(1)}, bf16[3,3,80,128]{3,2,1,0:T(8,128)(2,1)S(1)}, u32[]{:S(2)}, u32[]{:S(2)}) collective-permute-start(bf16[3,3,80,128]{3,2,1,0:T(8,128)(2,1)S(1)} %pad_maximum_fusion.2.refs_7_), channel_id=1, source_target_pairs={{0,8},{8,0},{16,24},{24,16},{1,9},{9,1},{17,25},{25,17},{2,10},{10... | collective-permute-start | bytes 552968 | tf_op jit(solution)/shard_map/ppermute | solution.py:488
  99.0 7.2 %collective-permute-start.53 = (bf16[3,3,80,128]{3,2,1,0:T(8,128)(2,1)S(1)}, bf16[3,3,80,128]{3,2,1,0:T(8,128)(2,1)S(1)}, u32[]{:S(2)}, u32[]{:S(2)}) collective-permute-start(bf16[3,3,80,128]{3,2,1,0:T(8,128)(2,1)S(1)} %pad_maximum_fusion.2.refs_7_), channel_id=1, source_target_pairs={{0,16},{8,24},{16,0},{24,8},{1,17},{9,25},{17,1},{25,9},{2,18},{10... | collective-permute-start | bytes 552968 | tf_op jit(solution)/shard_map/ppermute | solution.py:488
  99.9 6.9 %collective-permute-start.62 = (bf16[3,3,80,128]{3,2,1,0:T(8,128)(2,1)S(1)}, bf16[3,3,80,128]{3,2,1,0:T(8,128)(2,1)S(1)}, u32[]{:S(2)}, u32[]{:S(2)}) collective-permute-start(bf16[3,3,80,128]{3,2,1,0:T(8,128)(2,1)S(1)} %pad_maximum_fusion.2.refs_7_), channel_id=1, source_target_pairs={{0,4},{4,0},{1,5},{5,1},{2,6},{6,2},{3,7},{7,3},{8,12},{12,8},{9,1... | collective-permute-start | bytes 552968 | tf_op jit(solution)/shard_map/ppermute | solution.py:484
  99.9 6.9 %collective-permute-start.51 = (bf16[3,3,80,128]{3,2,1,0:T(8,128)(2,1)S(1)}, bf16[3,3,80,128]{3,2,1,0:T(8,128)(2,1)S(1)}, u32[]{:S(2)}, u32[]{:S(2)}) collective-permute-start(bf16[3,3,80,128]{3,2,1,0:T(8,128)(2,1)S(1)} %pad_maximum_fusion.1.refs_1_), channel_id=1, source_target_pairs={{0,4},{4,0},{1,5},{5,1},{2,6},{6,2},{3,7},{7,3},{8,12},{12,8},{9,1... | collective-permute-start | bytes 552968 | tf_op jit(solution)/shard_map/ppermute | solution.py:484
  (22 other events, 91.0 us)

commit v5 on v4

--- a/solution.py
+++ b/solution.py
@@ -164,6 +164,10 @@
 LANES = 128
 HIGH = lax.Precision.HIGHEST
 SIDES = [(slot, side) for slot in range(4) for side in range(2)]
+
+
+def gate_of(values):
+    return 0.5 + 0.5 * jnp.tanh(0.5 * values)
 
 
 def call(kernel, outs, args, scratch=(), grid=None, specs=None, flops=0, reads=0, grant=16):
@@ -297,7 +301,7 @@
     for slot, side in SIDES:
         for frame in range(frames):
             normed = (sums[2 * slot + side][frame] - mean) * inv
-            hidden[slot, side, frame] = (normed * jax.nn.sigmoid(normed)).astype(BF16)
+            hidden[slot, side, frame] = (normed * gate_of(normed)).astype(BF16)
             if slot == 0 and side == 0:
                 norm[frame] = normed
     lane = lax.broadcasted_iota(jnp.int32, scale.shape, 1)
@@ -308,14 +312,15 @@
     forward_product(where, weight, shifted, parts, total, frames)
 
 
-def third_kernel(frames, members, where, mixer, *rest):
-    sums, given, own, (result, halo, every, grads, norms) = rest[:8], rest[8:16], rest[16], rest[17:]
+def third_kernel(frames, members, where, mixer, total, own, *rest):
+    pairs, (result, halo, every, grads, norms) = rest[:8], rest[8:]
+    sums, given = [total] + [pair.at[0] for pair in pairs[1:]], [pair.at[1] for pair in pairs]
     mean, inv = statistics(sums, mixer[...], members)
     first = second = None
     for slot, side in SIDES:
         for frame in range(frames):
             normed = (sums[2 * slot + side][frame].astype(F32) - mean) * inv
-            gate = jax.nn.sigmoid(normed)
+            gate = gate_of(normed)
             grad = given[2 * slot + side][frame].astype(F32) * gate * (1.0 + normed * (1.0 - gate))
             first = grad if first is None else first + grad
             second = grad * normed if second is None else second + grad * normed
@@ -344,7 +349,7 @@
     out = back_product(weight, shifted, frames)
     for frame in range(frames):
         normed = norm[frame]
-        gate = jax.nn.sigmoid(normed)
+        gate = gate_of(normed)
         cells = out[:, frame * LANES : (frame + 1) * LANES]
         grad[frame] = (cells * gate * (1.0 + normed * (1.0 - gate))).astype(BF16)
 
@@ -538,9 +543,7 @@
         functools.partial(first_kernel, frames), parts_shape,
         (where, conv_first, *every_input), (shifted, total), **conv_cost,
     )
-    given, parts = lax.optimization_barrier((given, parts))
-    near, sums = lax.optimization_barrier((hops(given), over_channels(parts)))
-    every_given = with_sides([given] + near)
+    sums = over_channels(parts)
     first_sums = around(sums)
     hidden, norm, scale, *parts = call(
         functools.partial(second_kernel, frames, members),
@@ -559,12 +562,12 @@
     far = [hop(parts[k], "chan", k) for k in range(1, 4)]
     far, padded_inputs = lax.optimization_barrier((far, padded_inputs))
     sums = parts[0] + sum(values.astype(F32) for values in far)
-    second_sums = [sums, *around(sums.astype(BF16))[1:]]
+    every_pair = around(jnp.stack([sums.astype(BF16), given]))
     every_shape = jax.ShapeDtypeStruct((count, 2, *block), BF16)
     result, halo, every_second = call(
         functools.partial(third_kernel, frames, members),
         [cells_shape, jax.ShapeDtypeStruct((frames + 2, channels, LANES), BF16), every_shape],
-        (where, mixer, *second_sums, *every_given, inputs),
+        (where, mixer, sums, inputs, *every_pair),
         (pltpu.VMEM((4, 2, *block), F32), pltpu.VMEM((4, 2, *block), F32)), grant=24,
     )
     (padded_hidden,) = call(

time: 116 us -> 117 us (level)
  waiting for transfers between devices: 40 us -> 43.2 us
  starting transfers between devices: 45.7 us -> 43.2 us
    ppermute x32 -> x29, waiting for transfers between devices: 32.8 us -> 36.5 us  [hop(): return lax.ppermute(values, axis, [(i, i ^ step) for i in range(4)])]
    ppermute x32 -> x29, starting transfers between devices: 41.3 us -> 39.3 us  [hop(): return lax.ppermute(values, axis, [(i, i ^ step) for i in range(4)])]
    ppermute x31 -> x27, starting transfers between devices: 4.4 us -> 3.95 us  [swap(): return lax.ppermute(values, 'row', [(0, 1), (1, 0)])]
    ppermute x31 -> x27, waiting for transfers between devices: 7.15 us -> 6.7 us  [swap(): return lax.ppermute(values, 'row', [(0, 1), (1, 0)])]
  transfers between devices with their start and end apart: 63 -> 56, of which waited for: 33 -> 29; matrix products, arithmetic and copies ran while one was open for 0% -> 0% of each run, Pallas kernels for 7% -> 7%
where the time goes in v5:
time: 117 us; the launch traced here: 116 us
  starting transfers between devices  43.2 us (37%)
  waiting for transfers between devices  43.2 us (37%)
  Pallas kernels  25.6 us (22%)
  local copies, waits for them, and re-layouts  2.95 us (3%)
    ppermute x29, starting transfers between devices, hop(): return lax.ppermute(values, axis, [(i, i ^ step) for i in range(4)])  39.3 us
    ppermute x29, waiting for transfers between devices, hop(): return lax.ppermute(values, axis, [(i, i ^ step) for i in range(4)])  36.5 us
    pallas_call x10, Pallas kernels, call(): pl.pallas_call(kernel, out_shape=outs, in_specs=in_specs, out_specs=[vmem...  25.6 us
    ppermute x27, waiting for transfers between devices, swap(): return lax.ppermute(values, 'row', [(0, 1), (1, 0)])  6.7 us
    ppermute x27, starting transfers between devices, swap(): return lax.ppermute(values, 'row', [(0, 1), (1, 0)])  3.95 us
    unnamed x14, local copies, waits for them, and re-layouts  2.9 us
  transfers between devices with their start and end apart: 56, of which 29 were waited for; matrix products, arithmetic and copies ran while one was open for 0% of the time, Pallas kernels for 7%

profile of v5, /device:TPU:0, one launch (start us, length us, event | category | flops | bytes accessed | tf_op | source)
XLA Modules:
  0.0 116.4 jit_solution(17187980952280219154)
XLA Ops:
  0.6 3.0 %collective-permute-start = (bf16[3,80,128]{2,1,0:T(8,128)(2,1)}, bf16[3,80,128]{2,1,0:T(8,128)(2,1)S(1)}, u32[]{:S(2)}, u32[]{:S(2)}) collective-permute-start(bf16[3,80,128]{2,1,0:T(8,128)(2,1)} %bitcast.33), channel_id=1, source_target_pairs={{0,8},{8,0},{16,24},{24,16},{1,9},{9,1},{17,25},{25,17},{2,10},{10... | collective-permute-start | bytes 184328 | tf_op jit(solution)/shard_map/ppermute | solution.py:493
  3.6 1.5 %collective-permute-start.1 = (bf16[3,80,128]{2,1,0:T(8,128)(2,1)}, bf16[3,80,128]{2,1,0:T(8,128)(2,1)S(1)}, u32[]{:S(2)}, u32[]{:S(2)}) collective-permute-start(bf16[3,80,128]{2,1,0:T(8,128)(2,1)} %bitcast.34), channel_id=1, source_target_pairs={{0,16},{8,24},{16,0},{24,8},{1,17},{9,25},{17,1},{25,9},{2,18},{10... | collective-permute-start | bytes 184328 | tf_op jit(solution)/shard_map/ppermute | solution.py:493
  5.3 1.4 %copy-done = bf16[27,80,320]{2,1,0:T(8,128)(2,1)S(1)} copy-done((bf16[27,80,320]{2,1,0:T(8,128)(2,1)S(1)}, bf16[27,80,320]{2,1,0:T(8,128)(2,1)}, u32[]{:S(2)}) %copy-start) | copy-done | bytes 1382424
  6.7 1.4 %copy-done.2 = bf16[27,80,320]{2,1,0:T(8,128)(2,1)S(1)} copy-done((bf16[27,80,320]{2,1,0:T(8,128)(2,1)S(1)}, bf16[27,80,320]{2,1,0:T(8,128)(2,1)}, u32[]{:S(2)}) %copy-start.2) | copy-done | bytes 1382424
  9.0 1.4 %collective-permute-done.2.refs_1_ = bf16[3,80,128]{2,1,0:T(8,128)(2,1)S(1)} collective-permute-done((bf16[3,80,128]{2,1,0:T(8,128)(2,1)}, bf16[3,80,128]{2,1,0:T(8,128)(2,1)S(1)}, u32[]{:S(2)}, u32[]{:S(2)}) %collective-permute-start.2) | collective-permute-done | bytes 61472 | tf_op jit(solution)/shard_map/ppermute | solution.py:493
  12.3 1.4 %shard_map.85 = (f32[3,80,128]{2,1,0:T(8,128)S(1)}, bf16[3,80,128]{2,1,0:T(8,128)(2,1)S(1)}, bf16[3,80,128]{2,1,0:T(8,128)(2,1)S(1)}, bf16[3,80,128]{2,1,0:T(8,128)(2,1)S(1)}) custom-call(s32[3]{0:T(128)S(1)} %pad_add_fusion.where, bf16[3,80,128]{2,1,0:T(8,128)(2,1)S(1)} %collective-permute-done.3.refs_0_, ...), custom_call_target="tpu_custom_call" | custom-call | flops 353894400 | bytes 921600 | tf_op jit(solution)/shard_map/pallas_call | solution.py:183
  13.7 1.6 %collective-permute-start.7 = (bf16[3,80,128]{2,1,0:T(8,128)(2,1)S(1)}, bf16[3,80,128]{2,1,0:T(8,128)(2,1)S(1)}, u32[]{:S(2)}, u32[]{:S(2)}) collective-permute-start(bf16[3,80,128]{2,1,0:T(8,128)(2,1)S(1)} %get-tuple-element.51), channel_id=1, source_target_pairs={{0,1},{1,0},{2,3},{3,2},{4,5},{5,4},{6,7},{7,6},{8,9},{9,8},{10,11... | collective-permute-start | bytes 184328 | tf_op jit(solution)/shard_map/ppermute | solution.py:493
  15.3 2.6 %collective-permute-start.8 = (bf16[3,80,128]{2,1,0:T(8,128)(2,1)S(1)}, bf16[3,80,128]{2,1,0:T(8,128)(2,1)S(1)}, u32[]{:S(2)}, u32[]{:S(2)}) collective-permute-start(bf16[3,80,128]{2,1,0:T(8,128)(2,1)S(1)} %get-tuple-element.52), channel_id=1, source_target_pairs={{0,2},{1,3},{2,0},{3,1},{4,6},{5,7},{6,4},{7,5},{8,10},{9,11},{10,... | collective-permute-start | bytes 184328 | tf_op jit(solution)/shard_map/ppermute | solution.py:493
  18.1 3.8 %collective-permute-done.8 = bf16[3,80,128]{2,1,0:T(8,128)(2,1)S(1)} collective-permute-done((bf16[3,80,128]{2,1,0:T(8,128)(2,1)S(1)}, bf16[3,80,128]{2,1,0:T(8,128)(2,1)S(1)}, u32[]{:S(2)}, u32[]{:S(2)}) %collective-permute-start.8) | collective-permute-done | bytes 61472 | tf_op jit(solution)/shard_map/ppermute | solution.py:493
  21.9 2.1 %collective-permute-done.9 = bf16[3,80,128]{2,1,0:T(8,128)(2,1)S(1)} collective-permute-done((bf16[3,80,128]{2,1,0:T(8,128)(2,1)S(1)}, bf16[3,80,128]{2,1,0:T(8,128)(2,1)S(1)}, u32[]{:S(2)}, u32[]{:S(2)}) %collective-permute-start.9) | collective-permute-done | bytes 61472 | tf_op jit(solution)/shard_map/ppermute | solution.py:493
  24.1 1.7 %collective-permute-start.10 = (f32[3,80,128]{2,1,0:T(8,128)S(1)}, f32[3,80,128]{2,1,0:T(8,128)S(1)}, u32[]{:S(2)}, u32[]{:S(2)}) collective-permute-start(f32[3,80,128]{2,1,0:T(8,128)S(1)} %add_add_fusion.1.refs_7_.refs_15_), channel_id=1, source_target_pairs={{0,24},{8,16},{16,8},{24,0},{1,25},{9,17},{17,9},{25,1},{2,26},{10... | collective-permute-start | bytes 368648 | tf_op jit(solution)/shard_map/ppermute | solution.py:493
  26.3 1.3 %collective-permute-start.14 = (f32[3,80,128]{2,1,0:T(8,128)S(1)}, f32[3,80,128]{2,1,0:T(8,128)S(1)}, u32[]{:S(2)}, u32[]{:S(2)}) collective-permute-start(f32[3,80,128]{2,1,0:T(8,128)S(1)} %add_add_fusion.1.refs_7_.refs_15_), channel_id=1, source_target_pairs={{0,8},{8,0},{16,24},{24,16},{1,9},{9,1},{17,25},{25,17},{2,10},{10... | collective-permute-start | bytes 368648 | tf_op jit(solution)/shard_map/ppermute | solution.py:493
  27.6 3.1 %collective-permute-done.10.refs_1_.refs_9_ = f32[3,80,128]{2,1,0:T(8,128)S(1)} collective-permute-done((f32[3,80,128]{2,1,0:T(8,128)S(1)}, f32[3,80,128]{2,1,0:T(8,128)S(1)}, u32[]{:S(2)}, u32[]{:S(2)}) %collective-permute-start.10) | collective-permute-done | bytes 122912 | tf_op jit(solution)/shard_map/ppermute | solution.py:493
  30.7 0.9 collective-permute-done.12.refs_3_.refs_11_
  33.1 2.4 %shard_map.86 = (bf16[4,2,3,80,128]{4,3,2,1,0:T(8,128)(2,1)S(1)}, f32[3,80,128]{2,1,0:T(8,128)S(1)}, f32[80,128]{1,0:T(8,128)S(1)}, f32[3,80,128]{2,1,0:T(8,128)...) custom-call(s32[3]{0:T(128)S(1)} %pad_add_fusion.where, ...), custom_call_target="tpu_custom_call" | custom-call | flops 353894400 | bytes 921600 | tf_op jit(solution)/shard_map/pallas_call | solution.py:183
  36.3 1.5 %collective-permute-start.18 = (bf16[3,80,128]{2,1,0:T(8,128)(2,1)S(1)}, bf16[3,80,128]{2,1,0:T(8,128)(2,1)S(1)}, u32[]{:S(2)}, u32[]{:S(2)}) collective-permute-start(bf16[3,80,128]{2,1,0:T(8,128)(2,1)S(1)} %get-tuple-element.56), channel_id=1, source_target_pairs={{0,2},{1,3},{2,0},{3,1},{4,6},{5,7},{6,4},{7,5},{8,10},{9,11},{10,... | collective-permute-start | bytes 184328 | tf_op jit(solution)/shard_map/ppermute | solution.py:493
  37.9 2.1 %collective-permute-start.19 = (bf16[3,80,128]{2,1,0:T(8,128)(2,1)S(1)}, bf16[3,80,128]{2,1,0:T(8,128)(2,1)S(1)}, u32[]{:S(2)}, u32[]{:S(2)}) collective-permute-start(bf16[3,80,128]{2,1,0:T(8,128)(2,1)S(1)} %get-tuple-element.57), channel_id=1, source_target_pairs={{0,3},{1,2},{2,1},{3,0},{4,7},{5,6},{6,5},{7,4},{8,11},{9,10},{10,... | collective-permute-start | bytes 184328 | tf_op jit(solution)/shard_map/ppermute | solution.py:493
  40.0 0.9 shard_map.87.refs_9_
  40.9 3.7 %collective-permute-done.18 = bf16[3,80,128]{2,1,0:T(8,128)(2,1)S(1)} collective-permute-done((bf16[3,80,128]{2,1,0:T(8,128)(2,1)S(1)}, bf16[3,80,128]{2,1,0:T(8,128)(2,1)S(1)}, u32[]{:S(2)}, u32[]{:S(2)}) %collective-permute-start.18) | collective-permute-done | bytes 61472 | tf_op jit(solution)/shard_map/ppermute | solution.py:493
  44.6 1.8 %collective-permute-start.20 = (bf16[2,3,80,128]{3,2,1,0:T(8,128)(2,1)S(1)}, bf16[2,3,80,128]{3,2,1,0:T(8,128)(2,1)S(1)}, u32[]{:S(2)}, u32[]{:S(2)}) collective-permute-start(bf16[2,3,80,128]{3,2,1,0:T(8,128)(2,1)S(1)} %pad_maximum_fusion.3.refs_7_), channel_id=1, source_target_pairs={{0,24},{8,16},{16,8},{24,0},{1,25},{9,17},{17,9},{25,1},{2,26},{10... | collective-permute-start | bytes 368648 | tf_op jit(solution)/shard_map/ppermute | solution.py:493
  47.0 1.1 collective-permute-start.24
  48.2 2.6 %collective-permute-done.20.refs_1_ = bf16[2,3,80,128]{3,2,1,0:T(8,128)(2,1)S(1)} collective-permute-done((bf16[2,3,80,128]{3,2,1,0:T(8,128)(2,1)S(1)}, bf16[2,3,80,128]{3,2,1,0:T(8,128)(2,1)S(1)}, u32[]{:S(2)}, u32[]{:S(2)}) %collective-permute-start.20) | collective-permute-done | bytes 122912 | tf_op jit(solution)/shard_map/ppermute | solution.py:493
  50.8 1.2 %collective-permute-done.22.refs_3_ = bf16[2,3,80,128]{3,2,1,0:T(8,128)(2,1)S(1)} collective-permute-done((bf16[2,3,80,128]{3,2,1,0:T(8,128)(2,1)S(1)}, bf16[2,3,80,128]{3,2,1,0:T(8,128)(2,1)S(1)}, u32[]{:S(2)}, u32[]{:S(2)}) %collective-permute-start.22) | collective-permute-done | bytes 122912 | tf_op jit(solution)/shard_map/ppermute | solution.py:493
  53.5 2.9 %shard_map.88 = (bf16[3,80,128]{2,1,0:T(8,128)(2,1)}, bf16[5,80,128]{2,1,0:T(8,128)(2,1)S(1)}, bf16[4,2,3,80,128]{4,3,2,1,0:T(8,128)(2,1)S(1)}) custom-call(s32[3]{0:T(128)S(1)} %pad_add_fusion.where, bf16[2,3,80,128]{3,2,1,0:T(8,128)(2,1)S(1)} %collective-permute-done.21.refs_0_, bf16[2,3,80,128]{3,2,1,0:T(8,128)(2,1)S(1)} %collective-permute-done.20.refs_1_, ...), custom_call_target="tpu_custom_call" | custom-call | tf_op jit(solution)/shard_map/pallas_call | solution.py:183
  56.4 2.3 %collective-permute-start.27 = (bf16[5,80,128]{2,1,0:T(8,128)(2,1)S(1)}, bf16[5,80,128]{2,1,0:T(8,128)(2,1)S(1)}, u32[]{:S(2)}, u32[]{:S(2)}) collective-permute-start(bf16[5,80,128]{2,1,0:T(8,128)(2,1)S(1)} %get-tuple-element.62.refs_7_), channel_id=1, source_target_pairs={{0,1},{1,0},{2,3},{3,2},{4,5},{5,4},{6,7},{7,6},{8,9},{9,8},{10,11... | collective-permute-start | bytes 307208 | tf_op jit(solution)/shard_map/ppermute | solution.py:493
  58.7 1.0 collective-permute-start.28
  59.7 1.5 %collective-permute-start.29 = (bf16[5,80,128]{2,1,0:T(8,128)(2,1)S(1)}, bf16[5,80,128]{2,1,0:T(8,128)(2,1)S(1)}, u32[]{:S(2)}, u32[]{:S(2)}) collective-permute-start(bf16[5,80,128]{2,1,0:T(8,128)(2,1)S(1)} %get-tuple-element.62.refs_7_), channel_id=1, source_target_pairs={{0,3},{1,2},{2,1},{3,0},{4,7},{5,6},{6,5},{7,4},{8,11},{9,10},{10,... | collective-permute-start | bytes 307208 | tf_op jit(solution)/shard_map/ppermute | solution.py:493
  61.2 0.9 shard_map.89.refs_13_
  62.1 7.6 %collective-permute-done.28.refs_3_.refs_9_ = bf16[5,80,128]{2,1,0:T(8,128)(2,1)S(1)} collective-permute-done((bf16[5,80,128]{2,1,0:T(8,128)(2,1)S(1)}, bf16[5,80,128]{2,1,0:T(8,128)(2,1)S(1)}, u32[]{:S(2)}, u32[]{:S(2)}) %collective-permute-start.28) | collective-permute-done | bytes 102432 | tf_op jit(solution)/shard_map/ppermute | solution.py:493
  71.6 2.0 %shard_map.90.refs_7_ = bf16[3,80,128]{2,1,0:T(8,128)(2,1)S(1)} custom-call(s32[3]{0:T(128)S(1)} %pad_add_fusion.where, bf16[5,80,128]{2,1,0:T(8,128)(2,1)S(1)} %collective-permute-done.30.refs_0_.refs_6_, bf16[5,80,128]{2,1,0:T(8,128)(2,1)S(1)} %collective-permute-done.29.refs_1_.refs_7_, bf16[5,80,128]{2,1,0:T(8,128)(2,1)S(1)} %collective-permute-done.31.refs_2_.refs_8_, ...), custom_call_target="tpu_custom_call" | custom-call | flops 353894400 | bytes 921600 | tf_op jit(solution)/shard_map/pallas_call | solution.py:183
  73.5 1.6 %collective-permute-start.34 = (bf16[3,80,128]{2,1,0:T(8,128)(2,1)S(1)}, bf16[3,80,128]{2,1,0:T(8,128)(2,1)S(1)}, u32[]{:S(2)}, u32[]{:S(2)}) collective-permute-start(bf16[3,80,128]{2,1,0:T(8,128)(2,1)S(1)} %shard_map.90.refs_7_), channel_id=1, source_target_pairs={{0,24},{8,16},{16,8},{24,0},{1,25},{9,17},{17,9},{25,1},{2,26},{10... | collective-permute-start | bytes 184328 | tf_op jit(solution)/shard_map/ppermute | solution.py:493
  76.0 1.1 collective-permute-start.38
  77.1 1.7 %collective-permute-done.34.refs_1_ = bf16[3,80,128]{2,1,0:T(8,128)(2,1)S(1)} collective-permute-done((bf16[3,80,128]{2,1,0:T(8,128)(2,1)S(1)}, bf16[3,80,128]{2,1,0:T(8,128)(2,1)S(1)}, u32[]{:S(2)}, u32[]{:S(2)}) %collective-permute-start.34) | collective-permute-done | bytes 61472 | tf_op jit(solution)/shard_map/ppermute | solution.py:493
  78.8 1.1 collective-permute-done.36.refs_3_
  81.4 1.3 %shard_map.91 = (bf16[2,3,80,128]{3,2,1,0:T(8,128)(2,1)S(1)}, bf16[4,2,3,80,128]{4,3,2,1,0:T(8,128)(2,1)S(1)}) custom-call(s32[3]{0:T(128)S(1)} %pad_add_fusion.where, bf16[3,80,128]{2,1,0:T(8,128)(2,1)S(1)} %collective-permute-done.35.refs_0_, bf16[3,80,128]{2,1,0:T(8,128)(2,1)S(1)} %collective-permute-done.34.refs_1_, ...), custom_call_target="tpu_custom_call" | custom-call | tf_op jit(solution)/shard_map/pallas_call | solution.py:183
  82.7 1.9 %collective-permute-start.41 = (bf16[2,3,80,128]{3,2,1,0:T(8,128)(2,1)S(1)}, bf16[2,3,80,128]{3,2,1,0:T(8,128)(2,1)S(1)}, u32[]{:S(2)}, u32[]{:S(2)}) collective-permute-start(bf16[2,3,80,128]{3,2,1,0:T(8,128)(2,1)S(1)} %get-tuple-element.71), channel_id=1, source_target_pairs={{0,1},{1,0},{2,3},{3,2},{4,5},{5,4},{6,7},{7,6},{8,9},{9,8},{10,11... | collective-permute-start | bytes 368648 | tf_op jit(solution)/shard_map/ppermute | solution.py:493
  84.6 1.0 collective-permute-start.42
  85.7 1.5 %collective-permute-start.43 = (bf16[2,3,80,128]{3,2,1,0:T(8,128)(2,1)S(1)}, bf16[2,3,80,128]{3,2,1,0:T(8,128)(2,1)S(1)}, u32[]{:S(2)}, u32[]{:S(2)}) collective-permute-start(bf16[2,3,80,128]{3,2,1,0:T(8,128)(2,1)S(1)} %get-tuple-element.71), channel_id=1, source_target_pairs={{0,3},{1,2},{2,1},{3,0},{4,7},{5,6},{6,5},{7,4},{8,11},{9,10},{10,... | collective-permute-start | bytes 368648 | tf_op jit(solution)/shard_map/ppermute | solution.py:493
  87.2 1.1 collective-permute-start.47
  88.3 1.0 collective-permute-start.48
  90.1 1.6 %collective-permute-start.49 = (bf16[3,3,80,128]{3,2,1,0:T(8,128)(2,1)S(1)}, bf16[3,3,80,128]{3,2,1,0:T(8,128)(2,1)S(1)}, u32[]{:S(2)}, u32[]{:S(2)}) collective-permute-start(bf16[3,3,80,128]{3,2,1,0:T(8,128)(2,1)S(1)} %pad_maximum_fusion), channel_id=1, source_target_pairs={{0,24},{8,16},{16,8},{24,0},{1,25},{9,17},{17,9},{25,1},{2,26},{10... | collective-permute-start | bytes 552968 | tf_op jit(solution)/shard_map/ppermute | solution.py:493
  91.7 5.3 %collective-permute-done.42 = bf16[2,3,80,128]{3,2,1,0:T(8,128)(2,1)S(1)} collective-permute-done((bf16[2,3,80,128]{3,2,1,0:T(8,128)(2,1)S(1)}, bf16[2,3,80,128]{3,2,1,0:T(8,128)(2,1)S(1)}, u32[]{:S(2)}, u32[]{:S(2)}) %collective-permute-start.42) | collective-permute-done | bytes 122912 | tf_op jit(solution)/shard_map/ppermute | solution.py:493
  97.1 0.9 collective-permute-done.48.refs_3_
  98.6 0.9 collective-permute-start.45
  99.5 1.2 %collective-permute-start.46 = (bf16[3,3,80,128]{3,2,1,0:T(8,128)(2,1)S(1)}, bf16[3,3,80,128]{3,2,1,0:T(8,128)(2,1)S(1)}, u32[]{:S(2)}, u32[]{:S(2)}) collective-permute-start(bf16[3,3,80,128]{3,2,1,0:T(8,128)(2,1)S(1)} %pad_maximum_fusion.2.refs_7_), channel_id=1, source_target_pairs={{0,16},{8,24},{16,0},{24,8},{1,17},{9,25},{17,1},{25,9},{2,18},{10... | collective-permute-start | bytes 552968 | tf_op jit(solution)/shard_map/ppermute | solution.py:493
  101.3 5.8 %shard_map.92 = f32[27,80,320]{2,1,0:T(8,128)} custom-call(s32[3]{0:T(128)S(1)} %pad_add_fusion.where, bf16[3,3,80,128]{3,2,1,0:T(8,128)(2,1)S(1)} %collective-permute-done.50.refs_0_, bf16[3,3,80,128]{3,2,1,0:T(8,128)(2,1)S(1)} %collective-permute-done.49.refs_1_, bf16[3,3,80,128]{3,2,1,0:T(8,128)(2,1)S(1)} %collective-permute-done.51.refs_2_, ...), custom_call_target="tpu_custom_call" | custom-call | flops 2831155200 | bytes 8000000 | tf_op jit(solution)/shard_map/pallas_call | solution.py:183
  107.7 0.9 collective-permute-done.53.refs_2_
  108.9 7.3 %shard_map.93 = (f32[27,80,320]{2,1,0:T(8,128)}, bf16[3,80,128]{2,1,0:T(8,128)(2,1)}) custom-call(s32[3]{0:T(128)S(1)} %pad_add_fusion.where, bf16[3,3,80,128]{3,2,1,0:T(8,128)(2,1)S(1)} %collective-permute-done.44.refs_0_, bf16[3,3,80,128]{3,2,1,0:T(8,128)(2,1)S(1)} %pad_maximum_fusion.1.refs_1_, ...), custom_call_target="tpu_custom_call" | custom-call | flops 2831155200 | bytes 8000000 | tf_op jit(solution)/shard_map/pallas_call | solution.py:183
  (100 shorter events, 15.1 us)
Async XLA Ops:
  0.6 8.4 %collective-permute-start = (bf16[3,80,128]{2,1,0:T(8,128)(2,1)}, bf16[3,80,128]{2,1,0:T(8,128)(2,1)S(1)}, u32[]{:S(2)}, u32[]{:S(2)}) collective-permute-start(bf16[3,80,128]{2,1,0:T(8,128)(2,1)} %bitcast.33), channel_id=1, source_target_pairs={{0,8},{8,0},{16,24},{24,16},{1,9},{9,1},{17,25},{25,17},{2,10},{10... | collective-permute-start | bytes 184328 | tf_op jit(solution)/shard_map/ppermute | solution.py:493
  3.6 5.4 %collective-permute-start.1 = (bf16[3,80,128]{2,1,0:T(8,128)(2,1)}, bf16[3,80,128]{2,1,0:T(8,128)(2,1)S(1)}, u32[]{:S(2)}, u32[]{:S(2)}) collective-permute-start(bf16[3,80,128]{2,1,0:T(8,128)(2,1)} %bitcast.34), channel_id=1, source_target_pairs={{0,16},{8,24},{16,0},{24,8},{1,17},{9,25},{17,1},{25,9},{2,18},{10... | collective-permute-start | bytes 184328 | tf_op jit(solution)/shard_map/ppermute | solution.py:493
  5.2 5.3 %collective-permute-start.2 = (bf16[3,80,128]{2,1,0:T(8,128)(2,1)}, bf16[3,80,128]{2,1,0:T(8,128)(2,1)S(1)}, u32[]{:S(2)}, u32[]{:S(2)}) collective-permute-start(bf16[3,80,128]{2,1,0:T(8,128)(2,1)} %bitcast.35), channel_id=1, source_target_pairs={{0,24},{8,16},{16,8},{24,0},{1,25},{9,17},{17,9},{25,1},{2,26},{10... | collective-permute-start | bytes 184328 | tf_op jit(solution)/shard_map/ppermute | solution.py:493
  5.2 5.8 %collective-permute-start.6 = (bf16[3,80,128]{2,1,0:T(8,128)(2,1)}, bf16[3,80,128]{2,1,0:T(8,128)(2,1)S(1)}, u32[]{:S(2)}, u32[]{:S(2)}) collective-permute-start(bf16[3,80,128]{2,1,0:T(8,128)(2,1)} %bitcast.36), channel_id=1, source_target_pairs={{0,4},{4,0},{1,5},{5,1},{2,6},{6,2},{3,7},{7,3},{8,12},{12,8},{9,1... | collective-permute-start | bytes 184328 | tf_op jit(solution)/shard_map/ppermute | solution.py:489
  10.5 1.4 %collective-permute-start.4 = (bf16[3,80,128]{2,1,0:T(8,128)(2,1)S(1)}, bf16[3,80,128]{2,1,0:T(8,128)(2,1)S(1)}, u32[]{:S(2)}, u32[]{:S(2)}) collective-permute-start(bf16[3,80,128]{2,1,0:T(8,128)(2,1)S(1)} %collective-permute-done.1.refs_3_), channel_id=1, source_target_pairs={{0,4},{4,0},{1,5},{5,1},{2,6},{6,2},{3,7},{7,3},{8,12},{12,8},{9,1... | collective-permute-start | bytes 184328 | tf_op jit(solution)/shard_map/ppermute | solution.py:489
  13.7 4.5 %collective-permute-start.7 = (bf16[3,80,128]{2,1,0:T(8,128)(2,1)S(1)}, bf16[3,80,128]{2,1,0:T(8,128)(2,1)S(1)}, u32[]{:S(2)}, u32[]{:S(2)}) collective-permute-start(bf16[3,80,128]{2,1,0:T(8,128)(2,1)S(1)} %get-tuple-element.51), channel_id=1, source_target_pairs={{0,1},{1,0},{2,3},{3,2},{4,5},{5,4},{6,7},{7,6},{8,9},{9,8},{10,11... | collective-permute-start | bytes 184328 | tf_op jit(solution)/shard_map/ppermute | solution.py:493
  15.3 6.6 %collective-permute-start.8 = (bf16[3,80,128]{2,1,0:T(8,128)(2,1)S(1)}, bf16[3,80,128]{2,1,0:T(8,128)(2,1)S(1)}, u32[]{:S(2)}, u32[]{:S(2)}) collective-permute-start(bf16[3,80,128]{2,1,0:T(8,128)(2,1)S(1)} %get-tuple-element.52), channel_id=1, source_target_pairs={{0,2},{1,3},{2,0},{3,1},{4,6},{5,7},{6,4},{7,5},{8,10},{9,11},{10,... | collective-permute-start | bytes 184328 | tf_op jit(solution)/shard_map/ppermute | solution.py:493
  17.9 6.1 %collective-permute-start.9 = (bf16[3,80,128]{2,1,0:T(8,128)(2,1)S(1)}, bf16[3,80,128]{2,1,0:T(8,128)(2,1)S(1)}, u32[]{:S(2)}, u32[]{:S(2)}) collective-permute-start(bf16[3,80,128]{2,1,0:T(8,128)(2,1)S(1)} %get-tuple-element.53), channel_id=1, source_target_pairs={{0,3},{1,2},{2,1},{3,0},{4,7},{5,6},{6,5},{7,4},{8,11},{9,10},{10,... | collective-permute-start | bytes 184328 | tf_op jit(solution)/shard_map/ppermute | solution.py:493
  24.1 6.6 %collective-permute-start.10 = (f32[3,80,128]{2,1,0:T(8,128)S(1)}, f32[3,80,128]{2,1,0:T(8,128)S(1)}, u32[]{:S(2)}, u32[]{:S(2)}) collective-permute-start(f32[3,80,128]{2,1,0:T(8,128)S(1)} %add_add_fusion.1.refs_7_.refs_15_), channel_id=1, source_target_pairs={{0,24},{8,16},{16,8},{24,0},{1,25},{9,17},{17,9},{25,1},{2,26},{10... | collective-permute-start | bytes 368648 | tf_op jit(solution)/shard_map/ppermute | solution.py:493
  25.8 5.8 %collective-permute-start.12 = (f32[3,80,128]{2,1,0:T(8,128)S(1)}, f32[3,80,128]{2,1,0:T(8,128)S(1)}, u32[]{:S(2)}, u32[]{:S(2)}) collective-permute-start(f32[3,80,128]{2,1,0:T(8,128)S(1)} %add_add_fusion.1.refs_7_.refs_15_), channel_id=1, source_target_pairs={{0,16},{8,24},{16,0},{24,8},{1,17},{9,25},{17,1},{25,9},{2,18},{10... | collective-permute-start | bytes 368648 | tf_op jit(solution)/shard_map/ppermute | solution.py:493
  26.3 5.3 %collective-permute-start.14 = (f32[3,80,128]{2,1,0:T(8,128)S(1)}, f32[3,80,128]{2,1,0:T(8,128)S(1)}, u32[]{:S(2)}, u32[]{:S(2)}) collective-permute-start(f32[3,80,128]{2,1,0:T(8,128)S(1)} %add_add_fusion.1.refs_7_.refs_15_), channel_id=1, source_target_pairs={{0,8},{8,0},{16,24},{24,16},{1,9},{9,1},{17,25},{25,17},{2,10},{10... | collective-permute-start | bytes 368648 | tf_op jit(solution)/shard_map/ppermute | solution.py:493
  27.6 4.5 %collective-permute-start.16 = (f32[3,80,128]{2,1,0:T(8,128)S(1)}, f32[3,80,128]{2,1,0:T(8,128)S(1)}, u32[]{:S(2)}, u32[]{:S(2)}) collective-permute-start(f32[3,80,128]{2,1,0:T(8,128)S(1)} %add_add_fusion.1.refs_7_.refs_15_), channel_id=1, source_target_pairs={{0,4},{4,0},{1,5},{5,1},{2,6},{6,2},{3,7},{7,3},{8,12},{12,8},{9,1... | collective-permute-start | bytes 368648 | tf_op jit(solution)/shard_map/ppermute | solution.py:489
  30.7 1.4 %collective-permute-start.11 = (f32[3,80,128]{2,1,0:T(8,128)S(1)}, f32[3,80,128]{2,1,0:T(8,128)S(1)}, u32[]{:S(2)}, u32[]{:S(2)}) collective-permute-start(f32[3,80,128]{2,1,0:T(8,128)S(1)} %collective-permute-done.10.refs_1_.refs_9_), channel_id=1, source_target_pairs={{0,4},{4,0},{1,5},{5,1},{2,6},{6,2},{3,7},{7,3},{8,12},{12,8},{9,1... | collective-permute-start | bytes 368648 | tf_op jit(solution)/shard_map/ppermute | solution.py:489
  31.6 1.5 %collective-permute-start.15 = (f32[3,80,128]{2,1,0:T(8,128)S(1)}, f32[3,80,128]{2,1,0:T(8,128)S(1)}, u32[]{:S(2)}, u32[]{:S(2)}) collective-permute-start(f32[3,80,128]{2,1,0:T(8,128)S(1)} %collective-permute-done.14.refs_5_.refs_13_), channel_id=1, source_target_pairs={{0,4},{4,0},{1,5},{5,1},{2,6},{6,2},{3,7},{7,3},{8,12},{12,8},{9,1... | collective-permute-start | bytes 368648 | tf_op jit(solution)/shard_map/ppermute | solution.py:489
  35.5 5.3 %collective-permute-start.17 = (bf16[3,80,128]{2,1,0:T(8,128)(2,1)S(1)}, bf16[3,80,128]{2,1,0:T(8,128)(2,1)S(1)}, u32[]{:S(2)}, u32[]{:S(2)}) collective-permute-start(bf16[3,80,128]{2,1,0:T(8,128)(2,1)S(1)} %get-tuple-element.55), channel_id=1, source_target_pairs={{0,1},{1,0},{2,3},{3,2},{4,5},{5,4},{6,7},{7,6},{8,9},{9,8},{10,11... | collective-permute-start | bytes 184328 | tf_op jit(solution)/shard_map/ppermute | solution.py:493
  36.3 8.2 %collective-permute-start.18 = (bf16[3,80,128]{2,1,0:T(8,128)(2,1)S(1)}, bf16[3,80,128]{2,1,0:T(8,128)(2,1)S(1)}, u32[]{:S(2)}, u32[]{:S(2)}) collective-permute-start(bf16[3,80,128]{2,1,0:T(8,128)(2,1)S(1)} %get-tuple-element.56), channel_id=1, source_target_pairs={{0,2},{1,3},{2,0},{3,1},{4,6},{5,7},{6,4},{7,5},{8,10},{9,11},{10,... | collective-permute-start | bytes 184328 | tf_op jit(solution)/shard_map/ppermute | solution.py:493
  37.9 6.7 %collective-permute-start.19 = (bf16[3,80,128]{2,1,0:T(8,128)(2,1)S(1)}, bf16[3,80,128]{2,1,0:T(8,128)(2,1)S(1)}, u32[]{:S(2)}, u32[]{:S(2)}) collective-permute-start(bf16[3,80,128]{2,1,0:T(8,128)(2,1)S(1)} %get-tuple-element.57), channel_id=1, source_target_pairs={{0,3},{1,2},{2,1},{3,0},{4,7},{5,6},{6,5},{7,4},{8,11},{9,10},{10,... | collective-permute-start | bytes 184328 | tf_op jit(solution)/shard_map/ppermute | solution.py:493
  44.6 6.2 %collective-permute-start.20 = (bf16[2,3,80,128]{3,2,1,0:T(8,128)(2,1)S(1)}, bf16[2,3,80,128]{3,2,1,0:T(8,128)(2,1)S(1)}, u32[]{:S(2)}, u32[]{:S(2)}) collective-permute-start(bf16[2,3,80,128]{3,2,1,0:T(8,128)(2,1)S(1)} %pad_maximum_fusion.3.refs_7_), channel_id=1, source_target_pairs={{0,24},{8,16},{16,8},{24,0},{1,25},{9,17},{17,9},{25,1},{2,26},{10... | collective-permute-start | bytes 368648 | tf_op jit(solution)/shard_map/ppermute | solution.py:493
  46.4 5.7 %collective-permute-start.22 = (bf16[2,3,80,128]{3,2,1,0:T(8,128)(2,1)S(1)}, bf16[2,3,80,128]{3,2,1,0:T(8,128)(2,1)S(1)}, u32[]{:S(2)}, u32[]{:S(2)}) collective-permute-start(bf16[2,3,80,128]{3,2,1,0:T(8,128)(2,1)S(1)} %pad_maximum_fusion.3.refs_7_), channel_id=1, source_target_pairs={{0,16},{8,24},{16,0},{24,8},{1,17},{9,25},{17,1},{25,9},{2,18},{10... | collective-permute-start | bytes 368648 | tf_op jit(solution)/shard_map/ppermute | solution.py:493
  47.0 5.0 %collective-permute-start.24 = (bf16[2,3,80,128]{3,2,1,0:T(8,128)(2,1)S(1)}, bf16[2,3,80,128]{3,2,1,0:T(8,128)(2,1)S(1)}, u32[]{:S(2)}, u32[]{:S(2)}) collective-permute-start(bf16[2,3,80,128]{3,2,1,0:T(8,128)(2,1)S(1)} %pad_maximum_fusion.3.refs_7_), channel_id=1, source_target_pairs={{0,8},{8,0},{16,24},{24,16},{1,9},{9,1},{17,25},{25,17},{2,10},{10... | collective-permute-start | bytes 368648 | tf_op jit(solution)/shard_map/ppermute | solution.py:493
  48.2 4.4 %collective-permute-start.26 = (bf16[2,3,80,128]{3,2,1,0:T(8,128)(2,1)S(1)}, bf16[2,3,80,128]{3,2,1,0:T(8,128)(2,1)S(1)}, u32[]{:S(2)}, u32[]{:S(2)}) collective-permute-start(bf16[2,3,80,128]{3,2,1,0:T(8,128)(2,1)S(1)} %pad_maximum_fusion.3.refs_7_), channel_id=1, source_target_pairs={{0,4},{4,0},{1,5},{5,1},{2,6},{6,2},{3,7},{7,3},{8,12},{12,8},{9,1... | collective-permute-start | bytes 368648 | tf_op jit(solution)/shard_map/ppermute | solution.py:489
  50.8 1.8 %collective-permute-start.21 = (bf16[2,3,80,128]{3,2,1,0:T(8,128)(2,1)S(1)}, bf16[2,3,80,128]{3,2,1,0:T(8,128)(2,1)S(1)}, u32[]{:S(2)}, u32[]{:S(2)}) collective-permute-start(bf16[2,3,80,128]{3,2,1,0:T(8,128)(2,1)S(1)} %collective-permute-done.20.refs_1_), channel_id=1, source_target_pairs={{0,4},{4,0},{1,5},{5,1},{2,6},{6,2},{3,7},{7,3},{8,12},{12,8},{9,1... | collective-permute-start | bytes 368648 | tf_op jit(solution)/shard_map/ppermute | solution.py:489
  52.0 1.5 %collective-permute-start.25 = (bf16[2,3,80,128]{3,2,1,0:T(8,128)(2,1)S(1)}, bf16[2,3,80,128]{3,2,1,0:T(8,128)(2,1)S(1)}, u32[]{:S(2)}, u32[]{:S(2)}) collective-permute-start(bf16[2,3,80,128]{3,2,1,0:T(8,128)(2,1)S(1)} %collective-permute-done.24.refs_5_), channel_id=1, source_target_pairs={{0,4},{4,0},{1,5},{5,1},{2,6},{6,2},{3,7},{7,3},{8,12},{12,8},{9,1... | collective-permute-start | bytes 368648 | tf_op jit(solution)/shard_map/ppermute | solution.py:489
  56.4 5.8 %collective-permute-start.27 = (bf16[5,80,128]{2,1,0:T(8,128)(2,1)S(1)}, bf16[5,80,128]{2,1,0:T(8,128)(2,1)S(1)}, u32[]{:S(2)}, u32[]{:S(2)}) collective-permute-start(bf16[5,80,128]{2,1,0:T(8,128)(2,1)S(1)} %get-tuple-element.62.refs_7_), channel_id=1, source_target_pairs={{0,1},{1,0},{2,3},{3,2},{4,5},{5,4},{6,7},{7,6},{8,9},{9,8},{10,11... | collective-permute-start | bytes 307208 | tf_op jit(solution)/shard_map/ppermute | solution.py:493
  58.7 11.0 %collective-permute-start.28 = (bf16[5,80,128]{2,1,0:T(8,128)(2,1)S(1)}, bf16[5,80,128]{2,1,0:T(8,128)(2,1)S(1)}, u32[]{:S(2)}, u32[]{:S(2)}) collective-permute-start(bf16[5,80,128]{2,1,0:T(8,128)(2,1)S(1)} %get-tuple-element.62.refs_7_), channel_id=1, source_target_pairs={{0,2},{1,3},{2,0},{3,1},{4,6},{5,7},{6,4},{7,5},{8,10},{9,11},{10,... | collective-permute-start | bytes 307208 | tf_op jit(solution)/shard_map/ppermute | solution.py:493
  59.7 10.0 %collective-permute-start.29 = (bf16[5,80,128]{2,1,0:T(8,128)(2,1)S(1)}, bf16[5,80,128]{2,1,0:T(8,128)(2,1)S(1)}, u32[]{:S(2)}, u32[]{:S(2)}) collective-permute-start(bf16[5,80,128]{2,1,0:T(8,128)(2,1)S(1)} %get-tuple-element.62.refs_7_), channel_id=1, source_target_pairs={{0,3},{1,2},{2,1},{3,0},{4,7},{5,6},{6,5},{7,4},{8,11},{9,10},{10,... | collective-permute-start | bytes 307208 | tf_op jit(solution)/shard_map/ppermute | solution.py:493
  62.1 8.2 %collective-permute-start.33 = (bf16[5,80,128]{2,1,0:T(8,128)(2,1)S(1)}, bf16[5,80,128]{2,1,0:T(8,128)(2,1)S(1)}, u32[]{:S(2)}, u32[]{:S(2)}) collective-permute-start(bf16[5,80,128]{2,1,0:T(8,128)(2,1)S(1)} %get-tuple-element.62.refs_7_), channel_id=1, source_target_pairs={{0,4},{4,0},{1,5},{5,1},{2,6},{6,2},{3,7},{7,3},{8,12},{12,8},{9,1... | collective-permute-start | bytes 307208 | tf_op jit(solution)/shard_map/ppermute | solution.py:489
  69.7 1.5 %collective-permute-start.31 = (bf16[5,80,128]{2,1,0:T(8,128)(2,1)S(1)}, bf16[5,80,128]{2,1,0:T(8,128)(2,1)S(1)}, u32[]{:S(2)}, u32[]{:S(2)}) collective-permute-start(bf16[5,80,128]{2,1,0:T(8,128)(2,1)S(1)} %collective-permute-done.28.refs_3_.refs_9_), channel_id=1, source_target_pairs={{0,4},{4,0},{1,5},{5,1},{2,6},{6,2},{3,7},{7,3},{8,12},{12,8},{9,1... | collective-permute-start | bytes 307208 | tf_op jit(solution)/shard_map/ppermute | solution.py:489
  73.5 5.2 %collective-permute-start.34 = (bf16[3,80,128]{2,1,0:T(8,128)(2,1)S(1)}, bf16[3,80,128]{2,1,0:T(8,128)(2,1)S(1)}, u32[]{:S(2)}, u32[]{:S(2)}) collective-permute-start(bf16[3,80,128]{2,1,0:T(8,128)(2,1)S(1)} %shard_map.90.refs_7_), channel_id=1, source_target_pairs={{0,24},{8,16},{16,8},{24,0},{1,25},{9,17},{17,9},{25,1},{2,26},{10... | collective-permute-start | bytes 184328 | tf_op jit(solution)/shard_map/ppermute | solution.py:493
  75.1 4.7 %collective-permute-start.36 = (bf16[3,80,128]{2,1,0:T(8,128)(2,1)S(1)}, bf16[3,80,128]{2,1,0:T(8,128)(2,1)S(1)}, u32[]{:S(2)}, u32[]{:S(2)}) collective-permute-start(bf16[3,80,128]{2,1,0:T(8,128)(2,1)S(1)} %shard_map.90.refs_7_), channel_id=1, source_target_pairs={{0,16},{8,24},{16,0},{24,8},{1,17},{9,25},{17,1},{25,9},{2,18},{10... | collective-permute-start | bytes 184328 | tf_op jit(solution)/shard_map/ppermute | solution.py:493
  76.0 4.2 %collective-permute-start.38 = (bf16[3,80,128]{2,1,0:T(8,128)(2,1)S(1)}, bf16[3,80,128]{2,1,0:T(8,128)(2,1)S(1)}, u32[]{:S(2)}, u32[]{:S(2)}) collective-permute-start(bf16[3,80,128]{2,1,0:T(8,128)(2,1)S(1)} %shard_map.90.refs_7_), channel_id=1, source_target_pairs={{0,8},{8,0},{16,24},{24,16},{1,9},{9,1},{17,25},{25,17},{2,10},{10... | collective-permute-start | bytes 184328 | tf_op jit(solution)/shard_map/ppermute | solution.py:493
  77.1 3.3 %collective-permute-start.40 = (bf16[3,80,128]{2,1,0:T(8,128)(2,1)S(1)}, bf16[3,80,128]{2,1,0:T(8,128)(2,1)S(1)}, u32[]{:S(2)}, u32[]{:S(2)}) collective-permute-start(bf16[3,80,128]{2,1,0:T(8,128)(2,1)S(1)} %shard_map.90.refs_7_), channel_id=1, source_target_pairs={{0,4},{4,0},{1,5},{5,1},{2,6},{6,2},{3,7},{7,3},{8,12},{12,8},{9,1... | collective-permute-start | bytes 184328 | tf_op jit(solution)/shard_map/ppermute | solution.py:489
  78.8 1.7 %collective-permute-start.35 = (bf16[3,80,128]{2,1,0:T(8,128)(2,1)S(1)}, bf16[3,80,128]{2,1,0:T(8,128)(2,1)S(1)}, u32[]{:S(2)}, u32[]{:S(2)}) collective-permute-start(bf16[3,80,128]{2,1,0:T(8,128)(2,1)S(1)} %collective-permute-done.34.refs_1_), channel_id=1, source_target_pairs={{0,4},{4,0},{1,5},{5,1},{2,6},{6,2},{3,7},{7,3},{8,12},{12,8},{9,1... | collective-permute-start | bytes 184328 | tf_op jit(solution)/shard_map/ppermute | solution.py:489
  82.7 7.4 %collective-permute-start.41 = (bf16[2,3,80,128]{3,2,1,0:T(8,128)(2,1)S(1)}, bf16[2,3,80,128]{3,2,1,0:T(8,128)(2,1)S(1)}, u32[]{:S(2)}, u32[]{:S(2)}) collective-permute-start(bf16[2,3,80,128]{3,2,1,0:T(8,128)(2,1)S(1)} %get-tuple-element.71), channel_id=1, source_target_pairs={{0,1},{1,0},{2,3},{3,2},{4,5},{5,4},{6,7},{7,6},{8,9},{9,8},{10,11... | collective-permute-start | bytes 368648 | tf_op jit(solution)/shard_map/ppermute | solution.py:493
  84.6 12.4 %collective-permute-start.42 = (bf16[2,3,80,128]{3,2,1,0:T(8,128)(2,1)S(1)}, bf16[2,3,80,128]{3,2,1,0:T(8,128)(2,1)S(1)}, u32[]{:S(2)}, u32[]{:S(2)}) collective-permute-start(bf16[2,3,80,128]{3,2,1,0:T(8,128)(2,1)S(1)} %get-tuple-element.71), channel_id=1, source_target_pairs={{0,2},{1,3},{2,0},{3,1},{4,6},{5,7},{6,4},{7,5},{8,10},{9,11},{10,... | collective-permute-start | bytes 368648 | tf_op jit(solution)/shard_map/ppermute | solution.py:493
  85.7 11.4 %collective-permute-start.43 = (bf16[2,3,80,128]{3,2,1,0:T(8,128)(2,1)S(1)}, bf16[2,3,80,128]{3,2,1,0:T(8,128)(2,1)S(1)}, u32[]{:S(2)}, u32[]{:S(2)}) collective-permute-start(bf16[2,3,80,128]{3,2,1,0:T(8,128)(2,1)S(1)} %get-tuple-element.71), channel_id=1, source_target_pairs={{0,3},{1,2},{2,1},{3,0},{4,7},{5,6},{6,5},{7,4},{8,11},{9,10},{10,... | collective-permute-start | bytes 368648 | tf_op jit(solution)/shard_map/ppermute | solution.py:493
  87.2 9.9 %collective-permute-start.47 = (bf16[3,3,80,128]{3,2,1,0:T(8,128)(2,1)S(1)}, bf16[3,3,80,128]{3,2,1,0:T(8,128)(2,1)S(1)}, u32[]{:S(2)}, u32[]{:S(2)}) collective-permute-start(bf16[3,3,80,128]{3,2,1,0:T(8,128)(2,1)S(1)} %pad_maximum_fusion), channel_id=1, source_target_pairs={{0,8},{8,0},{16,24},{24,16},{1,9},{9,1},{17,25},{25,17},{2,10},{10... | collective-permute-start | bytes 552968 | tf_op jit(solution)/shard_map/ppermute | solution.py:493
  88.3 9.8 %collective-permute-start.48 = (bf16[3,3,80,128]{3,2,1,0:T(8,128)(2,1)S(1)}, bf16[3,3,80,128]{3,2,1,0:T(8,128)(2,1)S(1)}, u32[]{:S(2)}, u32[]{:S(2)}) collective-permute-start(bf16[3,3,80,128]{3,2,1,0:T(8,128)(2,1)S(1)} %pad_maximum_fusion), channel_id=1, source_target_pairs={{0,16},{8,24},{16,0},{24,8},{1,17},{9,25},{17,1},{25,9},{2,18},{10... | collective-permute-start | bytes 552968 | tf_op jit(solution)/shard_map/ppermute | solution.py:493
  90.1 8.0 %collective-permute-start.49 = (bf16[3,3,80,128]{3,2,1,0:T(8,128)(2,1)S(1)}, bf16[3,3,80,128]{3,2,1,0:T(8,128)(2,1)S(1)}, u32[]{:S(2)}, u32[]{:S(2)}) collective-permute-start(bf16[3,3,80,128]{3,2,1,0:T(8,128)(2,1)S(1)} %pad_maximum_fusion), channel_id=1, source_target_pairs={{0,24},{8,16},{16,8},{24,0},{1,25},{9,17},{17,9},{25,1},{2,26},{10... | collective-permute-start | bytes 552968 | tf_op jit(solution)/shard_map/ppermute | solution.py:493
  98.1 2.7 %collective-permute-start.50 = (bf16[3,3,80,128]{3,2,1,0:T(8,128)(2,1)S(1)}, bf16[3,3,80,128]{3,2,1,0:T(8,128)(2,1)S(1)}, u32[]{:S(2)}, u32[]{:S(2)}) collective-permute-start(bf16[3,3,80,128]{3,2,1,0:T(8,128)(2,1)S(1)} %collective-permute-done.49.refs_1_), channel_id=1, source_target_pairs={{0,4},{4,0},{1,5},{5,1},{2,6},{6,2},{3,7},{7,3},{8,12},{12,8},{9,1... | collective-permute-start | bytes 552968 | tf_op jit(solution)/shard_map/ppermute | solution.py:489
  98.1 2.7 %collective-permute-start.51 = (bf16[3,3,80,128]{3,2,1,0:T(8,128)(2,1)S(1)}, bf16[3,3,80,128]{3,2,1,0:T(8,128)(2,1)S(1)}, u32[]{:S(2)}, u32[]{:S(2)}) collective-permute-start(bf16[3,3,80,128]{3,2,1,0:T(8,128)(2,1)S(1)} %collective-permute-done.48.refs_3_), channel_id=1, source_target_pairs={{0,4},{4,0},{1,5},{5,1},{2,6},{6,2},{3,7},{7,3},{8,12},{12,8},{9,1... | collective-permute-start | bytes 552968 | tf_op jit(solution)/shard_map/ppermute | solution.py:489
  98.6 2.7 %collective-permute-start.52 = (bf16[3,3,80,128]{3,2,1,0:T(8,128)(2,1)S(1)}, bf16[3,3,80,128]{3,2,1,0:T(8,128)(2,1)S(1)}, u32[]{:S(2)}, u32[]{:S(2)}) collective-permute-start(bf16[3,3,80,128]{3,2,1,0:T(8,128)(2,1)S(1)} %collective-permute-done.47.refs_5_), channel_id=1, source_target_pairs={{0,4},{4,0},{1,5},{5,1},{2,6},{6,2},{3,7},{7,3},{8,12},{12,8},{9,1... | collective-permute-start | bytes 552968 | tf_op jit(solution)/shard_map/ppermute | solution.py:489
  98.6 8.5 %collective-permute-start.45 = (bf16[3,3,80,128]{3,2,1,0:T(8,128)(2,1)S(1)}, bf16[3,3,80,128]{3,2,1,0:T(8,128)(2,1)S(1)}, u32[]{:S(2)}, u32[]{:S(2)}) collective-permute-start(bf16[3,3,80,128]{3,2,1,0:T(8,128)(2,1)S(1)} %pad_maximum_fusion.2.refs_7_), channel_id=1, source_target_pairs={{0,8},{8,0},{16,24},{24,16},{1,9},{9,1},{17,25},{25,17},{2,10},{10... | collective-permute-start | bytes 552968 | tf_op jit(solution)/shard_map/ppermute | solution.py:493
  99.5 7.6 %collective-permute-start.46 = (bf16[3,3,80,128]{3,2,1,0:T(8,128)(2,1)S(1)}, bf16[3,3,80,128]{3,2,1,0:T(8,128)(2,1)S(1)}, u32[]{:S(2)}, u32[]{:S(2)}) collective-permute-start(bf16[3,3,80,128]{3,2,1,0:T(8,128)(2,1)S(1)} %pad_maximum_fusion.2.refs_7_), channel_id=1, source_target_pairs={{0,16},{8,24},{16,0},{24,8},{1,17},{9,25},{17,1},{25,9},{2,18},{10... | collective-permute-start | bytes 552968 | tf_op jit(solution)/shard_map/ppermute | solution.py:493
  100.8 6.9 %collective-permute-start.55 = (bf16[3,3,80,128]{3,2,1,0:T(8,128)(2,1)S(1)}, bf16[3,3,80,128]{3,2,1,0:T(8,128)(2,1)S(1)}, u32[]{:S(2)}, u32[]{:S(2)}) collective-permute-start(bf16[3,3,80,128]{3,2,1,0:T(8,128)(2,1)S(1)} %pad_maximum_fusion.2.refs_7_), channel_id=1, source_target_pairs={{0,4},{4,0},{1,5},{5,1},{2,6},{6,2},{3,7},{7,3},{8,12},{12,8},{9,1... | collective-permute-start | bytes 552968 | tf_op jit(solution)/shard_map/ppermute | solution.py:489
  100.8 6.9 %collective-permute-start.44 = (bf16[3,3,80,128]{3,2,1,0:T(8,128)(2,1)S(1)}, bf16[3,3,80,128]{3,2,1,0:T(8,128)(2,1)S(1)}, u32[]{:S(2)}, u32[]{:S(2)}) collective-permute-start(bf16[3,3,80,128]{3,2,1,0:T(8,128)(2,1)S(1)} %pad_maximum_fusion.1.refs_1_), channel_id=1, source_target_pairs={{0,4},{4,0},{1,5},{5,1},{2,6},{6,2},{3,7},{7,3},{8,12},{12,8},{9,1... | collective-permute-start | bytes 552968 | tf_op jit(solution)/shard_map/ppermute | solution.py:489
  107.1 1.5 %collective-permute-start.53 = (bf16[3,3,80,128]{3,2,1,0:T(8,128)(2,1)S(1)}, bf16[3,3,80,128]{3,2,1,0:T(8,128)(2,1)S(1)}, u32[]{:S(2)}, u32[]{:S(2)}) collective-permute-start(bf16[3,3,80,128]{3,2,1,0:T(8,128)(2,1)S(1)} %collective-permute-done.46.refs_3_), channel_id=1, source_target_pairs={{0,4},{4,0},{1,5},{5,1},{2,6},{6,2},{3,7},{7,3},{8,12},{12,8},{9,1... | collective-permute-start | bytes 552968 | tf_op jit(solution)/shard_map/ppermute | solution.py:489
  107.2 1.6 %collective-permute-start.54 = (bf16[3,3,80,128]{3,2,1,0:T(8,128)(2,1)S(1)}, bf16[3,3,80,128]{3,2,1,0:T(8,128)(2,1)S(1)}, u32[]{:S(2)}, u32[]{:S(2)}) collective-permute-start(bf16[3,3,80,128]{3,2,1,0:T(8,128)(2,1)S(1)} %collective-permute-done.45.refs_5_), channel_id=1, source_target_pairs={{0,4},{4,0},{1,5},{5,1},{2,6},{6,2},{3,7},{7,3},{8,12},{12,8},{9,1... | collective-permute-start | bytes 552968 | tf_op jit(solution)/shard_map/ppermute | solution.py:489
  (15 other events, 78.6 us)
